TPU v7x, 32 devices: a whole 2x2x4 slice. The times are simulated.
32 devices in a mesh: prompt: 8 (over y, x, core), ctx: 4 (over z).
Axes of the slice: x: 2, y: 2, z: 4, core: 2. Of those that a mesh axis runs over, the one named last changes fastest.
Arguments:
- prefix_qkv: bfloat16 [8, 512, 768], P('prompt', 'ctx'), may hold values from -8 to 8
- rollout: bfloat16 [8, 4, 8, 128, 768], P('prompt', 'ctx'), may hold values from -8 to 8
- arrival_order: int32 [8, 4, 1024], P('prompt', 'ctx'), may hold values from 0 to 1023, each once within a row
- resp_len: int32 [8, 8], P('prompt', 'ctx'), may hold values from 1 to 512, 2560 in all within a row
Outputs:
- prefix_out: bfloat16 [8, 512, 512], P('prompt', 'ctx')
- resp_out: bfloat16 [8, 8, 512, 512], P('prompt', 'ctx')
All inputs are finite; a program needn't handle non-finite values. No bound on the sum of `resp_len` on one device may be relied on, other than what follows from the above.
Results may differ from a plain program's by a relative error of at most 0.0075.
Values may be sent and summed in bfloat16 or wider, within the bound.
No kernel may reach another device: no remote copies, remote signals or barrier semaphores. Data moves between devices by JAX's collectives and lax.ppermute only.
A program may use at most 64 MiB of HBM per device.

v0:
```python
import math

import jax
import jax.numpy as jnp
from jax import lax
from jax.sharding import PartitionSpec as P

HEAD = 128
RESP_DEV = 2


MASKED_SCORE = -1e30


def shifted(x, axis, by):
    peers = lax.axis_size(axis)
    return lax.ppermute(x, axis, [(i, (i + by) % peers) for i in range(peers)])


def absorb(state, queries, key_rows, values, allowed):
    row_max, row_sum, weighted = state
    scores = jnp.einsum(
        "rhd,kd->hrk", queries, key_rows, preferred_element_type=jnp.float32
    ) * HEAD ** (-0.5)
    scores = jnp.where(allowed[None], scores, MASKED_SCORE)
    new_max = jnp.maximum(row_max, jnp.max(scores, axis=-1))
    weights = jnp.exp(scores - new_max[..., None])
    rescale = jnp.exp(row_max - new_max)
    row_sum = row_sum * rescale + jnp.sum(weights, axis=-1)
    weighted = weighted * rescale[..., None] + jnp.einsum(
        "hrk,kd->hrd", weights.astype(jnp.bfloat16), values, preferred_element_type=jnp.float32
    )
    return (new_max, row_sum, weighted)


def empty_state(head_count, row_count):
    return (
        jnp.full((head_count, row_count), MASKED_SCORE, jnp.float32),
        jnp.zeros((head_count, row_count), jnp.float32),
        jnp.zeros((head_count, row_count, HEAD), jnp.float32),
    )


def finish(state):
    row_max, row_sum, weighted = state
    result = weighted / row_sum[..., None]
    head_count, row_count, head_size = result.shape
    return jnp.transpose(result, (1, 0, 2)).reshape(row_count, head_count * head_size)


def body(prefix_qkv, rollout, arrival_order, resp_len):
    ctx_count = lax.axis_size("ctx")
    ctx_index = lax.axis_index("ctx")
    prefix_rows = prefix_qkv[0]
    prefix_len = prefix_rows.shape[0]
    query_span = prefix_rows.shape[1] - 2 * HEAD
    head_count = query_span // HEAD
    prefix_kv = prefix_rows[:, query_span:]
    own_low = ctx_index * prefix_len
    row_order = arrival_order[0, 0]
    arrived = lax.all_to_all(rollout, "prompt", split_axis=2, concat_axis=0, tiled=True)
    arrived_rows = arrived.reshape(-1, arrived.shape[-1])
    placed = jnp.take(arrived_rows, row_order, axis=0)
    resp_rows = placed.shape[0]
    resp_start = empty_state(head_count, resp_rows)
    slot_len = resp_rows // RESP_DEV
    prefix_queries = prefix_rows[:, :query_span].reshape(prefix_len, head_count, HEAD)
    resp_queries = placed[:, :query_span].reshape(resp_rows, head_count, HEAD)
    prefix_pos = own_low + jnp.arange(prefix_len)

    def fold_piece(states, piece, start):
        piece_rows = piece.shape[0]
        block_size = math.gcd(piece_rows, 128)
        open_mask = jnp.ones((resp_rows, block_size), dtype=bool)

        def absorb_block(i, carried):
            prefix_state, resp_state = carried
            key_rows = piece[:, :HEAD]
            values = piece[:, HEAD:]
            block_start = start + i * block_size
            key_pos = block_start + jnp.arange(block_size)
            prefix_state = absorb(
                prefix_state,
                prefix_queries,
                key_rows,
                values,
                key_pos[None, :] <= prefix_pos[:, None],
            )
            resp_state = absorb(resp_state, resp_queries, key_rows, values, open_mask)
            return (prefix_state, resp_state)

        return lax.fori_loop(0, piece_rows // block_size, absorb_block, states)

    states = (empty_state(head_count, prefix_len), resp_start)
    states = fold_piece(states, prefix_kv, own_low)
    forward_turns = ctx_count // 2
    backward_turns = (ctx_count - 1) // 2

    def pair_turn(t, carried):
        fold_states, from_below, from_above = carried
        from_below = shifted(from_below, "ctx", 1)
        from_above = shifted(from_above, "ctx", -1)
        fold_states = fold_piece(fold_states, from_below, (ctx_index - t) % ctx_count * prefix_len)
        fold_states = fold_piece(fold_states, from_above, (ctx_index + t) % ctx_count * prefix_len)
        return (fold_states, from_below, from_above)

    states, from_below, from_above = lax.fori_loop(
        1, backward_turns + 1, pair_turn, (states, prefix_kv, prefix_kv)
    )
    from_below = shifted(from_below, "ctx", 1)
    states = fold_piece(states, from_below, (ctx_index - forward_turns) % ctx_count * prefix_len)
    prefix_state, resp_state = states
    own_pos = jnp.arange(slot_len)
    own_causal = own_pos[None, :] <= own_pos[:, None]
    resp_parts = []
    for index_resp in range(RESP_DEV):
        first_row = index_resp * slot_len
        sub_state = tuple(
            (
                lax.slice_in_dim(member, first_row, first_row + slot_len, axis=1)
                for member in resp_state
            )
        )
        own_rows = placed[first_row : first_row + slot_len]
        sub_state = absorb(
            sub_state,
            resp_queries[first_row : first_row + slot_len],
            own_rows[:, query_span : query_span + HEAD],
            own_rows[:, query_span + HEAD :],
            own_causal,
        )
        weighted = finish(sub_state)
        live_rows = (own_pos < resp_len[0, index_resp])[:, None]
        resp_parts.append(jnp.where(live_rows, weighted, 0.0).astype(jnp.bfloat16))
    resp_out = jnp.stack(resp_parts, axis=0)[None]
    prefix_out = finish(prefix_state).astype(jnp.bfloat16)[None]
    return (prefix_out, resp_out)


def solution(mesh):
    placed = (
        P("prompt", "ctx", None),
        P("prompt", "ctx", None, None, None),
        P("prompt", "ctx", None),
        P("prompt", "ctx"),
    )
    return jax.shard_map(
        body,
        mesh=mesh,
        in_specs=placed,
        out_specs=(P("prompt", "ctx", None), P("prompt", "ctx", None, None)),
        check_vma=False,
    )
```

profile of v0, /device:TPU:0, one launch (start us, length us, event | category | flops | bytes accessed | tf_op | source)
XLA Modules:
  0.0 60.0 jit_solution(2229319968329799256)
XLA Ops:
  0.7 0.9 %slice.135 = bf16[128,256]{1,0:T(8,128)(2,1)S(1)} slice(bf16[128,768]{1,0:T(8,128)(2,1)} %bitcast.289), slice={[0:128], [512:768]} | slice | bytes 131072 | tf_op jit(solution)/shard_map/slice | solution.py:58
  1.6 5.0 %collective-permute-start.1 = (bf16[128,256]{1,0:T(8,128)(2,1)S(1)}, bf16[128,256]{1,0:T(8,128)(2,1)S(1)}, u32[]{:S(2)}, u32[]{:S(2)}) collective-permute-start(bf16[128,256]{1,0:T(8,128)(2,1)S(1)} %slice.135), channel_id=1, source_target_pairs={{0,3},{1,0},{2,1},{3,2},{4,7},{5,4},{6,5},{7,6},{8,11},{9,8},{10,9... | collective-permute-start | bytes 196616 | tf_op jit(solution)/shard_map/while/body/eval_jaxpr/ppermute | solution.py:17
  6.6 3.7 %all-to-all-start = ((bf16[1,1,8,128,768]{4,3,1,0,2:T(8,128)(2,1)}), bf16[1,1,8,128,768]{4,3,1,0,2:T(8,128)(2,1)S(1)}, u32[]{:S(2)}, u32[]{:S(2)}) async-start(bf16[1,1,8,128,768]{4,3,1,0,2:T(8,128)(2,1)} %bitcast.288), calls=%async_computation | async-start | bytes 3145728 | tf_op jit(solution)/shard_map/all_to_all | solution.py:61
  11.1 0.6 %iota_compare_fusion.2 = pred[512]{0:T(512)(128)(4,1)S(1)} fusion(s32[]{:T(128)} %bitcast.27), kind=kLoop, calls=%fused_computation.159 | loop fusion | flops 512 | bytes 516 | tf_op jit(solution)/shard_map/lt | solution.py:133
  12.3 0.7 %iota_compare_fusion.1 = pred[512]{0:T(512)(128)(4,1)S(1)} fusion(s32[]{:T(128)} %bitcast.48), kind=kLoop, calls=%fused_computation.158 | loop fusion | flops 512 | bytes 516 | tf_op jit(solution)/shard_map/lt | solution.py:133
  13.4 6.2 %collective-permute-done.2 = bf16[128,256]{1,0:T(8,128)(2,1)S(1)} collective-permute-done((bf16[128,256]{1,0:T(8,128)(2,1)S(1)}, bf16[128,256]{1,0:T(8,128)(2,1)S(1)}, u32[]{:S(2)}, u32[]{:S(2)}) %collective-permute-start.2) | collective-permute-done | bytes 65568 | tf_op jit(solution)/shard_map/ppermute | solution.py:17
  21.0 0.8 %copy.102 = bf16[1,128,512]{2,1,0:T(8,128)(2,1)} copy(bf16[1,128,512]{1,2,0:T(8,128)(2,1)S(1)} %bitcast.297) | data formatting | bytes 262144
  21.8 9.6 %all-to-all-done = bf16[1,1,8,128,768]{4,3,1,0,2:T(8,128)(2,1)S(1)} async-done(((bf16[1,1,8,128,768]{4,3,1,0,2:T(8,128)(2,1)}), bf16[1,1,8,128,768]{4,3,1,0,2:T(8,128)(2,1)S(1)}, u32[]{:S(2)}, u32[]{:S(2)}) %all-to-all-start) | async-done | bytes 1572896 | tf_op jit(solution)/shard_map/all_to_all | solution.py:61
  31.4 4.0 %gather_fusion = bf16[1024,768]{1,0:T(8,128)(2,1)S(1)} fusion(bf16[1024,768]{1,0:T(8,128)(2,1)S(1)} %bitcast.278, s32[1024]{0:T(1024)S(1)} %broadcast_clamp_fusion), kind=kCustom, calls=%fused_computation | custom fusion | bytes 3149824 | tf_op jit(solution)/shard_map/jit(_take)/gather | solution.py:63
  35.6 1.1 %slice.142 = bf16[1024,512]{1,0:T(8,128)(2,1)} slice(bf16[1024,768]{1,0:T(8,128)(2,1)S(1)} %broadcast_select_fusion), slice={[0:1024], [0:512]} | slice | bytes 2097152 | tf_op jit(solution)/shard_map/slice | solution.py:68
  36.6 1.0 %fusion.112 = (bf16[512,512]{1,0:T(8,128)(2,1)}, bf16[64,4,8,128]{3,2,1,0:T(8,128)(2,1)}) fusion(bf16[1024,768]{1,0:T(8,128)(2,1)S(1)} %broadcast_select_fusion), kind=kLoop, calls=%fused_computation.178 | loop fusion | bytes 2097152 | tf_op jit(solution)/shard_map/slice | solution.py:127
  37.7 1.7 %copy.80 = bf16[1024,512]{0,1:T(8,128)(2,1)S(1)} copy(bf16[1024,512]{1,0:T(8,128)(2,1)} %slice.142) | data formatting | bytes 2097152 | tf_op jit(solution)/shard_map/slice | solution.py:68
  39.4 1.3 %copy.93 = bf16[512,512]{0,1:T(8,128)(2,1)S(1)} copy(bf16[512,512]{1,0:T(8,128)(2,1)} %get-tuple-element.238) | data formatting | bytes 1048576 | tf_op jit(solution)/shard_map/slice | solution.py:127
  40.6 1.2 %bitcast_reduce_fusion.3 = (f32[4,1024]{1,0:T(4,128)S(1)}, f32[1024,4,128]{0,2,1:T(8,128)S(1)}) fusion(bf16[1024,4,128]{0,2,1:T(8,128)(2,1)S(1)} %bitcast.279, bf16[128,768]{1,0:T(8,128)(2,1)} %bitcast.290), kind=kOutput, calls=%fused_computation.21 | convolution fusion | flops 135262208 | bytes 3194880 | tf_op jit(solution)/shard_map/while/body/eval_jaxpr/rhd,kd->hrk/dot_general | solution.py:22
  41.8 0.9 %fusion.4 = (f32[4,512]{1,0:T(4,128)S(1)}, f32[512,512,4]{1,0,2:T(8,128)S(1)}) fusion(pred[512,512]{0,1:T(8,128)(4,1)S(1)} %iota_compare_fusion, bf16[512,4,128]{0,2,1:T(8,128)(2,1)S(1)} %bitcast.287, bf16[1024,768]{1,0:T(8,128)(2,1)S(1)} %broadcast_select_fusion), kind=kOutput, calls=%fused_computation.9 | convolution fusion | flops 271579136 | bytes 5120000 | tf_op jit(solution)/shard_map/rhd,kd->hrk/dot_general | solution.py:22
  45.2 1.8 %fusion = (f32[4,512]{1,0:T(4,128)S(1)}, f32[4,512]{1,0:T(4,128)S(1)}, f32[512,512,4]{1,0,2:T(8,128)S(1)}) fusion(f32[512,512,4]{1,0,2:T(8,128)S(1)} %get-tuple-element.283, f32[4,512]{1,0:T(4,128)S(1)} %slice_maximum_fusion.1, pred[512,512]{0,1:T(8,128)(4,1)S(1)} %iota_compare_fusion, bf16[64,4,8,128]{3,2,1,0:T(8,128)(2,1)S(1)} %copy-done.3, ...), kind=kOutput, calls=%fused_computation.5 | convolution fusion | flops 275771392 | bytes 9330688 | tf_op jit(solution)/shard_map/rhd,kd->hrk/dot_general | solution.py:22
  47.0 1.3 %fusion.46 = f32[4,1024,128]{1,2,0:T(8,128)S(1)} fusion(f32[1024,4,128]{0,2,1:T(8,128)S(1)} %get-tuple-element.281, f32[4,1024]{1,0:T(4,128)S(1)} %get-tuple-element.243, bf16[128,768]{1,0:T(8,128)(2,1)} %bitcast.291), kind=kOutput, calls=%fused_computation.64 | convolution fusion | flops 135790592 | bytes 4243456 | tf_op jit(solution)/shard_map/while/body/eval_jaxpr/hrk,kd->hrd/dot_general | solution.py:30
  48.3 0.8 %fusion.16 = (f32[4,1024]{1,0:T(4,128)S(1)}, f32[4,1024]{1,0:T(4,128)S(1)}) fusion(f32[1024,4,128]{0,2,1:T(8,128)S(1)} %get-tuple-element.281, f32[4,1024]{1,0:T(4,128)S(1)} %get-tuple-element.243, f32[4,1024]{1,0:T(4,128)S(1)} %get-tuple-element.218, f32[1024,4,128]{0,2,1:T(8,128)S(1)} %get-tuple-element.279), kind=kLoop, calls=%fused_computation.28 | loop fusion | flops 3137536 | bytes 4259840 | tf_op jit(solution)/shard_map/while/body/eval_jaxpr/reduce_sum | solution.py:29
  49.1 0.9 %fusion.2 = f32[4,512]{1,0:T(4,128)S(1)} fusion(f32[512,512,4]{1,0,2:T(8,128)S(1)} %get-tuple-element.284, f32[4,512]{1,0:T(4,128)S(1)} %slice_maximum_fusion, pred[512,512]{0,1:T(8,128)(4,1)S(1)} %iota_compare_fusion), kind=kLoop, calls=%fused_computation.7 | loop fusion | flops 4192256 | bytes 4472832 | tf_op jit(solution)/shard_map/reduce_sum | solution.py:29
  50.0 0.8 %fusion.20 = (f32[4,1024]{1,0:T(4,128)S(1)}, f32[4,1024]{1,0:T(4,128)S(1)}) fusion(f32[1024,4,128]{0,2,1:T(8,128)S(1)} %get-tuple-element.277, f32[4,1024]{1,0:T(4,128)S(1)} %get-tuple-element.217, f32[4,1024]{1,0:T(4,128)S(1)} %get-tuple-element.216, f32[1024,4,128]{0,2,1:T(8,128)S(1)} %get-tuple-element.275), kind=kLoop, calls=%fused_computation.32 | loop fusion | flops 3137536 | bytes 4259840 | tf_op jit(solution)/shard_map/while/body/eval_jaxpr/while/body/eval_jaxpr/reduce_sum | solution.py:29
  51.9 1.3 %multiply_add_fusion = f32[4,1024,128]{1,2,0:T(8,128)S(1)} fusion(f32[4,1024,128]{1,2,0:T(8,128)S(1)} %fusion.42, f32[4,1024,128]{1,2,0:T(8,128)S(1)} %fusion.44, f32[4,1024,128]{1,2,0:T(8,128)S(1)} %fusion.46, f32[1024,4,128]{0,2,1:T(8,128)S(1)} %get-tuple-element.275, f32[4,1024]{1,0:T(4,128)S(1)} %get-tuple-element.216, ...), kind=kOutput, calls=%fused_computation.23 | convolution fusion | flops 139460608 | bytes 10600448 | tf_op jit(solution)/shard_map/while/body/eval_jaxpr/hrk,kd->hrd/dot_general | solution.py:30
  53.2 1.2 %fusion.49 = bf16[4,512,128]{1,2,0:T(8,128)(2,1)S(1)} fusion(f32[4,1024,128]{1,2,0:T(8,128)S(1)} %multiply_add_fusion, f32[4,512]{1,0:T(4,128)S(1)} %get-tuple-element.240, f32[4,512]{1,0:T(4,128)S(1)} %get-tuple-element.241, bf16[1024,768]{1,0:T(8,128)(2,1)S(1)} %broadcast_select_fusion, f32[512,512,4]{1,0,2:T(8,128)S(1)} %get-tuple-element.284, ...), kind=kOutput, calls=%fused_computation.67 | convolution fusion | flops 273678336 | bytes 6184960 | tf_op jit(solution)/shard_map/hrk,kd->hrd/dot_general | solution.py:30
  54.7 3.6 %fusion.51 = bf16[4,512,128]{1,2,0:T(8,128)(2,1)S(1)} fusion(f32[4,1024,128]{1,2,0:T(8,128)} %copy-done.1, f32[4,512]{1,0:T(4,128)S(1)} %get-tuple-element.194, f32[4,512]{1,0:T(4,128)S(1)} %get-tuple-element.195, bf16[1024,768]{1,0:T(8,128)(2,1)S(1)} %broadcast_select_fusion, f32[512,512,4]{1,0,2:T(8,128)} %copy-done, ...), kind=kOutput, calls=%fused_computation.70 | convolution fusion | flops 273678336 | bytes 6184960 | tf_op jit(solution)/shard_map/hrk,kd->hrd/dot_general | solution.py:30
  58.9 1.1 %maximum_bitcast_fusion = bf16[1,2,512,512]{3,2,1,0:T(8,128)(2,1)} fusion(bf16[1,512,512]{2,1,0:T(8,128)(2,1)S(1)} %select_convert_fusion, bf16[1,512,512]{2,1,0:T(8,128)(2,1)S(1)} %select_convert_fusion.1), kind=kLoop, calls=%fused_computation.71 | loop fusion | flops 524288 | bytes 2097152 | tf_op jit(solution)/shard_map/broadcast_in_dim | solution.py:135
  (59 shorter events, 7.7 us)
Async XLA Ops:
  0.6 9.7 %copy-start.2 = (bf16[1,128,768]{2,1,0:T(8,128)(2,1)S(1)}, bf16[1,128,768]{2,1,0:T(8,128)(2,1)}, u32[]{:S(2)}) copy-start(bf16[1,128,768]{2,1,0:T(8,128)(2,1)} %param.4) | copy-start | bytes 589828
  0.6 9.8 %copy-start.6 = (s32[1,1,1024]{2,1,0:T(1,128)S(1)}, s32[1,1,1024]{2,1,0:T(1,128)}, u32[]{:S(2)}) copy-start(s32[1,1,1024]{2,1,0:T(1,128)} %param.6) | copy-start | bytes 12292
  0.7 9.9 %copy-start.7 = (s32[1,2]{1,0:T(1,128)S(1)}, s32[1,2]{1,0:T(1,128)}, u32[]{:S(2)}) copy-start(s32[1,2]{1,0:T(1,128)} %param.7) | copy-start | bytes 28
  1.6 11.6 %collective-permute-start.1 = (bf16[128,256]{1,0:T(8,128)(2,1)S(1)}, bf16[128,256]{1,0:T(8,128)(2,1)S(1)}, u32[]{:S(2)}, u32[]{:S(2)}) collective-permute-start(bf16[128,256]{1,0:T(8,128)(2,1)S(1)} %slice.135), channel_id=1, source_target_pairs={{0,3},{1,0},{2,1},{3,2},{4,7},{5,4},{6,5},{7,6},{8,11},{9,8},{10,9... | collective-permute-start | bytes 196616 | tf_op jit(solution)/shard_map/while/body/eval_jaxpr/ppermute | solution.py:17
  6.6 6.3 %collective-permute-start = (bf16[128,256]{1,0:T(8,128)(2,1)S(1)}, bf16[128,256]{1,0:T(8,128)(2,1)S(1)}, u32[]{:S(2)}, u32[]{:S(2)}) collective-permute-start(bf16[128,256]{1,0:T(8,128)(2,1)S(1)} %slice.135), channel_id=1, source_target_pairs={{0,1},{1,2},{2,3},{3,0},{4,5},{5,6},{6,7},{7,4},{8,9},{9,10},{10,1... | collective-permute-start | bytes 196616 | tf_op jit(solution)/shard_map/while/body/eval_jaxpr/ppermute | solution.py:17
  6.6 24.8 %all-to-all-start = ((bf16[1,1,8,128,768]{4,3,1,0,2:T(8,128)(2,1)}), bf16[1,1,8,128,768]{4,3,1,0,2:T(8,128)(2,1)S(1)}, u32[]{:S(2)}, u32[]{:S(2)}) async-start(bf16[1,1,8,128,768]{4,3,1,0,2:T(8,128)(2,1)} %bitcast.288), calls=%async_computation | async-start | bytes 3145728 | tf_op jit(solution)/shard_map/all_to_all | solution.py:61
  12.9 6.6 %collective-permute-start.2 = (bf16[128,256]{1,0:T(8,128)(2,1)S(1)}, bf16[128,256]{1,0:T(8,128)(2,1)S(1)}, u32[]{:S(2)}, u32[]{:S(2)}) collective-permute-start(bf16[128,256]{1,0:T(8,128)(2,1)S(1)} %collective-permute-done), channel_id=1, source_target_pairs={{0,1},{1,2},{2,3},{3,0},{4,5},{5,6},{6,7},{7,4},{8,9},{9,10},{10,1... | collective-permute-start | bytes 196616 | tf_op jit(solution)/shard_map/ppermute | solution.py:17
  19.6 1.4 %copy-start.4 = (bf16[128,256]{1,0:T(8,128)(2,1)}, bf16[128,256]{1,0:T(8,128)(2,1)S(1)}, u32[]{:S(2)}) copy-start(bf16[128,256]{1,0:T(8,128)(2,1)S(1)} %collective-permute-done.2) | copy-start | bytes 196612
  42.7 1.9 %copy-start = (f32[512,512,4]{1,0,2:T(8,128)}, f32[512,512,4]{1,0,2:T(8,128)S(1)}, u32[]{:S(2)}) copy-start(f32[512,512,4]{1,0,2:T(8,128)S(1)} %get-tuple-element.283) | copy-start | bytes 12582916
  43.2 0.9 %copy-start.5 = (bf16[128,256]{1,0:T(8,128)(2,1)S(1)}, bf16[128,256]{1,0:T(8,128)(2,1)}, u32[]{:S(2)}) copy-start(bf16[128,256]{1,0:T(8,128)(2,1)} %copy-done.4) | copy-start | bytes 196612
  44.1 1.1 %copy-start.3 = (bf16[64,4,8,128]{3,2,1,0:T(8,128)(2,1)S(1)}, bf16[64,4,8,128]{3,2,1,0:T(8,128)(2,1)}, u32[]{:S(2)}) copy-start(bf16[64,4,8,128]{3,2,1,0:T(8,128)(2,1)} %get-tuple-element.239) | copy-start | bytes 1572868
  53.1 1.3 %copy-start.1 = (f32[4,1024,128]{1,2,0:T(8,128)}, f32[4,1024,128]{1,2,0:T(8,128)S(1)}, u32[]{:S(2)}) copy-start(f32[4,1024,128]{1,2,0:T(8,128)S(1)} %multiply_add_fusion) | copy-start | bytes 6291460
where the time goes:
time: 60.5 us; the launch traced here: 60 us
  waiting for transfers between devices  15.8 us (26%)
  matrix products  15.2 us (25%)
  local copies, waits for them, and re-layouts  13.1 us (22%)
  starting transfers between devices  8.83 us (15%)
  other arithmetic  6.01 us (10%)
  between operations  1.07 us (2%)
    all_to_all x1, waiting for transfers between devices, body(): lax.all_to_all(rollout, 'prompt', split_axis=2, concat_axis=0, tiled=True)  9.59 us
    dot_general x10, matrix products, absorb(): jnp.einsum('hrk,kd->hrd', weights.astype(jnp.bfloat16), values, preferred...  9.29 us
    ppermute x3, waiting for transfers between devices, shifted(): return lax.ppermute(x, axis, [(i, (i + by) % peers) for i in range(peers)])  6.18 us
    dot_general x10, matrix products, absorb(): jnp.einsum('rhd,kd->hrk', queries, key_rows, preferred_element_type=jnp.f...  5.96 us
    ppermute x3, starting transfers between devices, shifted(): return lax.ppermute(x, axis, [(i, (i + by) % peers) for i in range(peers)])  5.11 us
    gather x1, local copies, waits for them, and re-layouts, body(): placed = jnp.take(arrived_rows, row_order, axis=0)  4 us
    all_to_all x1, starting transfers between devices, body(): lax.all_to_all(rollout, 'prompt', split_axis=2, concat_axis=0, tiled=True)  3.72 us
    slice x2, local copies, waits for them, and re-layouts, body(): resp_queries = placed[:, :query_span].reshape(resp_rows, head_count, HEAD)  2.71 us
  transfers between devices with their start and end apart: 4, of which 2 were waited for; matrix products, arithmetic and copies ran while one was open for 8% of the time, Pallas kernels for 0%

commit v1 on v0

v1 whole, which is shorter than its diff:
```python
import functools
import math

import jax
import jax.numpy as jnp
from jax import lax
from jax.experimental import pallas as pl
from jax.experimental.pallas import tpu as pltpu
from jax.sharding import PartitionSpec as P

HEAD = 128
MASKED_SCORE = -1e30
EXP2_SCALE = HEAD ** (-0.5) * math.log2(math.e)
VMEM_LIMIT = 24 * 1024 * 1024


def mix(a, b):
    return lax.dot_general(a, b, (((1,), (0,)), ((), ())), preferred_element_type=jnp.float32)


def match(a, b):
    return lax.dot_general(a, b, (((1,), (1,)), ((), ())), preferred_element_type=jnp.float32)


def with_ones(values):
    return jnp.concatenate([values, jnp.ones_like(values)], axis=1)


def attend(scores, values):
    top = functools.reduce(jnp.maximum, [jnp.max(s, axis=1, keepdims=True) for s in scores])
    total = None
    for s, v in zip(scores, values):
        weights = jnp.exp2((s - top) * EXP2_SCALE).astype(jnp.bfloat16)
        part = mix(weights, v)
        total = part if total is None else total + part
    return total[:, :HEAD] / total[:, HEAD:]


def prefix_kernel(starts_ref, rows_ref, *refs):
    pieces, out_ref = refs[:-1], refs[-1]
    row_count = rows_ref.shape[0]
    heads = rows_ref.shape[1] // HEAD - 2
    row_pos = starts_ref[0] + lax.broadcasted_iota(jnp.int32, (row_count, 1), 0)
    kv = [rows_ref[:, heads * HEAD :]] + [p[...] for p in pieces]
    values = [with_ones(p[:, HEAD:]) for p in kv]
    seen = []
    for t, p in enumerate(kv):
        key_pos = starts_ref[t] + lax.broadcasted_iota(jnp.int32, (1, p.shape[0]), 1)
        seen.append(key_pos <= row_pos)
    for h in range(heads):
        q = rows_ref[:, h * HEAD : (h + 1) * HEAD]
        scores = [jnp.where(ok, match(q, p[:, :HEAD]), MASKED_SCORE) for ok, p in zip(seen, kv)]
        out_ref[:, h * HEAD : (h + 1) * HEAD] = attend(scores, values).astype(jnp.bfloat16)


def prefix_attention(starts, rows, pieces):
    row_count, feat = rows.shape
    return pl.pallas_call(
        prefix_kernel,
        out_shape=jax.ShapeDtypeStruct((row_count, feat - 2 * HEAD), jnp.bfloat16),
        in_specs=[pl.BlockSpec(memory_space=pltpu.SMEM)]
        + [pl.BlockSpec(memory_space=pltpu.VMEM)] * (1 + len(pieces)),
        out_specs=pl.BlockSpec(memory_space=pltpu.VMEM),
        compiler_params=pltpu.CompilerParams(vmem_limit_bytes=VMEM_LIMIT),
        name="prefix_attention",
    )(starts, rows, *pieces)


def response_kernel(block_count, piece_count, len_ref, order_ref, *refs):
    blocks = refs[:block_count]
    pieces = refs[block_count : block_count + piece_count]
    out_ref = refs[block_count + piece_count]
    arrived_ref, pk_ref, pv_ref = refs[block_count + piece_count + 1 :]
    slot = order_ref.shape[0]
    feat = arrived_ref.shape[1]
    heads = feat // HEAD - 2
    span = heads * HEAD
    r = pl.program_id(0)

    @pl.when(r == 0)
    def _():
        first = 0
        for b in blocks:
            arrived_ref[first : first + b.shape[0], :] = b[...]
            first += b.shape[0]
        first = 0
        for p in pieces:
            pk_ref[first : first + p.shape[0], :] = p[:, :HEAD]
            pv_ref[first : first + p.shape[0], :] = with_ones(p[:, HEAD:])
            first += p.shape[0]

    arrived_count = arrived_ref.shape[0]
    chosen = lax.broadcasted_iota(jnp.int32, (slot, arrived_count), 1) == order_ref[...]
    chosen = jnp.where(chosen, 1.0, 0.0).astype(jnp.bfloat16)
    placed = mix(chosen, arrived_ref[...]).astype(jnp.bfloat16)
    own_k = placed[:, span : span + HEAD]
    own_v = with_ones(placed[:, span + HEAD :])
    step = math.gcd(slot, 256)
    causal = lax.broadcasted_iota(jnp.int32, (step, step), 1) <= lax.broadcasted_iota(
        jnp.int32, (step, step), 0
    )
    length = len_ref[r]
    for c in range(slot // step):
        low, high = c * step, (c + 1) * step
        live = low + lax.broadcasted_iota(jnp.int32, (step, 1), 0) < length
        for h in range(heads):
            q = placed[low:high, h * HEAD : (h + 1) * HEAD]
            scores = [match(q, pk_ref[...])]
            values = [pv_ref[...]]
            if c:
                scores.append(match(q, own_k[:low]))
                values.append(own_v[:low])
            scores.append(jnp.where(causal, match(q, own_k[low:high]), MASKED_SCORE))
            values.append(own_v[low:high])
            result = jnp.where(live, attend(scores, values), 0.0)
            out_ref[0, low:high, h * HEAD : (h + 1) * HEAD] = result.astype(jnp.bfloat16)


def response_attention(lengths, order, blocks, pieces):
    responses = lengths.shape[0]
    slot = order.shape[0] // responses
    feat = blocks[0].shape[1]
    arrived_count = sum(b.shape[0] for b in blocks)
    prefix_count = sum(p.shape[0] for p in pieces)
    whole = pl.BlockSpec(memory_space=pltpu.VMEM)
    return pl.pallas_call(
        functools.partial(response_kernel, len(blocks), len(pieces)),
        grid=(responses,),
        out_shape=jax.ShapeDtypeStruct((responses, slot, feat - 2 * HEAD), jnp.bfloat16),
        in_specs=[
            pl.BlockSpec(memory_space=pltpu.SMEM),
            pl.BlockSpec((slot, 1), lambda r: (r, 0)),
        ]
        + [whole] * (len(blocks) + len(pieces)),
        out_specs=pl.BlockSpec((1, slot, feat - 2 * HEAD), lambda r: (r, 0, 0)),
        scratch_shapes=[
            pltpu.VMEM((arrived_count, feat), jnp.bfloat16),
            pltpu.VMEM((prefix_count, HEAD), jnp.bfloat16),
            pltpu.VMEM((prefix_count, 2 * HEAD), jnp.bfloat16),
        ],
        compiler_params=pltpu.CompilerParams(vmem_limit_bytes=VMEM_LIMIT),
        name="response_attention",
    )(lengths, order, *blocks, *pieces)


def body(prefix_qkv, rollout, arrival_order, resp_len):
    peers = lax.axis_size("prompt")
    ctx_count = lax.axis_size("ctx")
    prompt_index = lax.axis_index("prompt")
    ctx_index = lax.axis_index("ctx")
    prefix_rows = prefix_qkv[0]
    prefix_len, feat = prefix_rows.shape
    sent = rollout[0, 0]
    rows_peer = sent.shape[1]
    assert peers & (peers - 1) == 0

    blocks = [lax.dynamic_index_in_dim(sent, prompt_index, 0, keepdims=False)]
    for k in range(1, peers):
        block = lax.dynamic_index_in_dim(sent, prompt_index ^ k, 0, keepdims=False)
        blocks.append(lax.ppermute(block, "prompt", [(j, j ^ k) for j in range(peers)]))
    order = (arrival_order[0, 0] ^ (prompt_index * rows_peer)).reshape(-1, 1)

    prefix_kv = prefix_rows[:, feat - 2 * HEAD :]
    shifted = [
        lax.ppermute(prefix_kv, "ctx", [(j, (j + t) % ctx_count) for j in range(ctx_count)])
        for t in range(1, ctx_count)
    ]
    starts = (ctx_index - jnp.arange(ctx_count, dtype=jnp.int32)) % ctx_count * prefix_len
    prefix_out = prefix_attention(starts, prefix_rows, shifted)
    resp_out = response_attention(resp_len[0], order, blocks, [prefix_kv] + shifted)
    return (prefix_out[None], resp_out[None])


def solution(mesh):
    placed = (
        P("prompt", "ctx", None),
        P("prompt", "ctx", None, None, None),
        P("prompt", "ctx", None),
        P("prompt", "ctx"),
    )
    return jax.shard_map(
        body,
        mesh=mesh,
        in_specs=placed,
        out_specs=(P("prompt", "ctx", None), P("prompt", "ctx", None, None)),
        check_vma=False,
    )
```

time: 60.5 us -> 42.7 us (0.71)
  matrix products: 15.2 us -> 0 us
  Pallas kernels: 0 us -> 11.7 us
  local copies, waits for them, and re-layouts: 13.1 us -> 1.88 us
  other arithmetic: 6.01 us -> 0.02 us
  starting transfers between devices: 8.83 us -> 13 us
  waiting for transfers between devices: 15.8 us -> 14.9 us
    dot_general x20 -> x0, matrix products: 15.2 us -> none  [the longest x10 9.29 us: absorb(): jnp.einsum('hrk,kd->hrd', weights.astype(jnp.bfloat16), values, preferred...]
    pallas_call x0 -> x2, Pallas kernels: none -> 11.7 us  [the longest x1 9.42 us: response_attention(): pl.pallas_call(functools.partial(response_kernel, len(blocks), len(pieces...]
    all_to_all x1 -> x0, waiting for transfers between devices: 9.59 us -> none  [body(): lax.all_to_all(rollout, 'prompt', split_axis=2, concat_axis=0, tiled=True)]
    ppermute x3 -> x10, waiting for transfers between devices: 6.18 us -> 14.9 us  [the longest x7 11.5 us: body(): lax.ppermute(block, 'prompt', [(j, j ^ k) for j in range(peers)])]
    ppermute x3 -> x10, starting transfers between devices: 5.11 us -> 13 us  [the longest x7 7.47 us: body(): lax.ppermute(block, 'prompt', [(j, j ^ k) for j in range(peers)])]
    slice x8 -> x1, local copies, waits for them, and re-layouts: 6.61 us -> 0.01 us  [body(): prefix_kv = prefix_rows[:, feat - 2 * HEAD:]]
    gather x1 -> x0, local copies, waits for them, and re-layouts: 4 us -> none  [body(): placed = jnp.take(arrived_rows, row_order, axis=0)]
    all_to_all x1 -> x0, starting transfers between devices: 3.72 us -> none  [body(): lax.all_to_all(rollout, 'prompt', split_axis=2, concat_axis=0, tiled=True)]
  transfers between devices with their start and end apart: 4 -> 10, of which waited for: 2 -> 4; matrix products, arithmetic and copies ran while one was open for 8% -> 1% of each run, Pallas kernels for 0% -> 5%
where the time goes in v1:
time: 42.7 us; the launch traced here: 42.3 us
  waiting for transfers between devices  14.9 us (35%)
  starting transfers between devices  13 us (30%)
  Pallas kernels  11.7 us (27%)
  local copies, waits for them, and re-layouts  1.88 us (4%)
  between operations  0.74 us (2%)
    ppermute x7, waiting for transfers between devices, body(): lax.ppermute(block, 'prompt', [(j, j ^ k) for j in range(peers)])  11.5 us
    pallas_call x1, Pallas kernels, response_attention(): pl.pallas_call(functools.partial(response_kernel, len(blocks), len(pieces...  9.42 us
    ppermute x7, starting transfers between devices, body(): lax.ppermute(block, 'prompt', [(j, j ^ k) for j in range(peers)])  7.47 us
    ppermute x3, starting transfers between devices, body(): lax.ppermute(prefix_kv, 'ctx', [(j, (j + t) % ctx_count) for j in range(c...  5.57 us
    ppermute x3, waiting for transfers between devices, body(): lax.ppermute(prefix_kv, 'ctx', [(j, (j + t) % ctx_count) for j in range(c...  3.41 us
    pallas_call x1, Pallas kernels, prefix_attention(): pl.pallas_call(prefix_kernel, out_shape=jax.ShapeDtypeStruct((row_count,...  2.28 us
    squeeze x1, local copies, waits for them, and re-layouts, body(): block = lax.dynamic_index_in_dim(sent, prompt_index ^ k, 0, keepdims=False)  1.64 us
  transfers between devices with their start and end apart: 10, of which 4 were waited for; matrix products, arithmetic and copies ran while one was open for 1% of the time, Pallas kernels for 5%

profile of v1, /device:TPU:0, one launch (start us, length us, event | category | flops | bytes accessed | tf_op | source)
XLA Modules:
  0.0 42.3 jit_solution(12737471117902170718)
XLA Ops:
  0.7 1.6 %dynamic-slice_bitcast_fusion = (bf16[128,768]{1,0:T(8,128)(2,1)S(1)}, bf16[128,768]{1,0:T(8,128)(2,1)S(1)}, bf16[128,768]{1,0:T(8,128)(2,1)S(1)}, bf16[128,768]...) fusion(bf16[1,1,8,128,768]{4,3,2,1,0:T(8,128)(2,1)} %param.5, ...), kind=kLoop, calls=%fused_computation | loop fusion | bytes 3145760 | tf_op jit(solution)/shard_map/jit(dynamic_index_in_dim)/squeeze | solution.py:159
  2.3 0.5 %collective-permute-start.3 = (bf16[128,768]{1,0:T(8,128)(2,1)S(1)}, bf16[128,768]{1,0:T(8,128)(2,1)S(1)}, u32[]{:S(2)}, u32[]{:S(2)}) collective-permute-start(bf16[128,768]{1,0:T(8,128)(2,1)S(1)} %get-tuple-element.7), channel_id=1, source_target_pairs={{0,4},{4,0},{8,12},{12,8},{16,20},{20,16},{24,28},{28,24},{1,5},{5... | collective-permute-start | bytes 589832 | tf_op jit(solution)/shard_map/ppermute | solution.py:160
  2.9 2.6 %collective-permute-start.4 = (bf16[128,768]{1,0:T(8,128)(2,1)S(1)}, bf16[128,768]{1,0:T(8,128)(2,1)S(1)}, u32[]{:S(2)}, u32[]{:S(2)}) collective-permute-start(bf16[128,768]{1,0:T(8,128)(2,1)S(1)} %get-tuple-element.6), channel_id=1, source_target_pairs={{0,8},{4,12},{8,0},{12,4},{16,24},{20,28},{24,16},{28,20},{1,9},{5... | collective-permute-start | bytes 589832 | tf_op jit(solution)/shard_map/ppermute | solution.py:160
  5.4 1.6 %collective-permute-start = (bf16[128,256]{1,0:T(8,128)(2,1)S(1)}, bf16[128,256]{1,0:T(8,128)(2,1)S(1)}, u32[]{:S(2)}, u32[]{:S(2)}) collective-permute-start(bf16[128,256]{1,0:T(8,128)(2,1)S(1)} %slice.4.refs_8_), channel_id=1, source_target_pairs={{0,1},{1,2},{2,3},{3,0},{4,5},{5,6},{6,7},{7,4},{8,9},{9,10},{10,1... | collective-permute-start | bytes 196616 | tf_op jit(solution)/shard_map/ppermute | solution.py:165
  7.1 2.6 %collective-permute-start.1 = (bf16[128,256]{1,0:T(8,128)(2,1)S(1)}, bf16[128,256]{1,0:T(8,128)(2,1)S(1)}, u32[]{:S(2)}, u32[]{:S(2)}) collective-permute-start(bf16[128,256]{1,0:T(8,128)(2,1)S(1)} %slice.4.refs_8_), channel_id=1, source_target_pairs={{0,2},{1,3},{2,0},{3,1},{4,6},{5,7},{6,4},{7,5},{8,10},{9,11},{10,... | collective-permute-start | bytes 196616 | tf_op jit(solution)/shard_map/ppermute | solution.py:165
  9.7 1.3 %collective-permute-start.2 = (bf16[128,256]{1,0:T(8,128)(2,1)S(1)}, bf16[128,256]{1,0:T(8,128)(2,1)S(1)}, u32[]{:S(2)}, u32[]{:S(2)}) collective-permute-start(bf16[128,256]{1,0:T(8,128)(2,1)S(1)} %slice.4.refs_8_), channel_id=1, source_target_pairs={{0,3},{1,0},{2,1},{3,2},{4,7},{5,4},{6,5},{7,6},{8,11},{9,8},{10,9... | collective-permute-start | bytes 196616 | tf_op jit(solution)/shard_map/ppermute | solution.py:165
  11.0 0.8 %collective-permute-done.refs_0_.refs_9_ = bf16[128,256]{1,0:T(8,128)(2,1)S(1)} collective-permute-done((bf16[128,256]{1,0:T(8,128)(2,1)S(1)}, bf16[128,256]{1,0:T(8,128)(2,1)S(1)}, u32[]{:S(2)}, u32[]{:S(2)}) %collective-permute-start) | collective-permute-done | bytes 65568 | tf_op jit(solution)/shard_map/ppermute | solution.py:165
  11.8 0.0 collective-permute-start.5
  11.8 2.7 %collective-permute-done.1.refs_1_.refs_10_ = bf16[128,256]{1,0:T(8,128)(2,1)S(1)} collective-permute-done((bf16[128,256]{1,0:T(8,128)(2,1)S(1)}, bf16[128,256]{1,0:T(8,128)(2,1)S(1)}, u32[]{:S(2)}, u32[]{:S(2)}) %collective-permute-start.1) | collective-permute-done | bytes 65568 | tf_op jit(solution)/shard_map/ppermute | solution.py:165
  14.4 1.5 %collective-permute-start.6 = (bf16[128,768]{1,0:T(8,128)(2,1)S(1)}, bf16[128,768]{1,0:T(8,128)(2,1)S(1)}, u32[]{:S(2)}, u32[]{:S(2)}) collective-permute-start(bf16[128,768]{1,0:T(8,128)(2,1)S(1)} %get-tuple-element.4), channel_id=1, source_target_pairs={{0,16},{4,20},{8,24},{12,28},{16,0},{20,4},{24,8},{28,12},{1,17},{... | collective-permute-start | bytes 589832 | tf_op jit(solution)/shard_map/ppermute | solution.py:160
  15.9 0.0 collective-permute-done.2.refs_2_.refs_11_
  15.9 0.0 collective-permute-start.7
  16.0 0.0 collective-permute-done.3.refs_1_
  16.0 1.2 %collective-permute-start.8 = (bf16[128,768]{1,0:T(8,128)(2,1)S(1)}, bf16[128,768]{1,0:T(8,128)(2,1)S(1)}, u32[]{:S(2)}, u32[]{:S(2)}) collective-permute-start(bf16[128,768]{1,0:T(8,128)(2,1)S(1)} %get-tuple-element.9), channel_id=1, source_target_pairs={{0,24},{4,28},{8,16},{12,20},{16,8},{20,12},{24,0},{28,4},{1,25},{... | collective-permute-start | bytes 589832 | tf_op jit(solution)/shard_map/ppermute | solution.py:160
  17.2 0.0 collective-permute-done.4.refs_2_
  17.2 1.6 %collective-permute-start.9 = (bf16[128,768]{1,0:T(8,128)(2,1)S(1)}, bf16[128,768]{1,0:T(8,128)(2,1)S(1)}, u32[]{:S(2)}, u32[]{:S(2)}) collective-permute-start(bf16[128,768]{1,0:T(8,128)(2,1)S(1)} %get-tuple-element.2), channel_id=1, source_target_pairs={{0,28},{4,24},{8,20},{12,16},{16,12},{20,8},{24,4},{28,0},{1,29},{... | collective-permute-start | bytes 589832 | tf_op jit(solution)/shard_map/ppermute | solution.py:160
  18.8 0.2 copy.6.order_ref
  19.1 2.3 %prefix_attention.1 = bf16[128,512]{1,0:T(8,128)(2,1)} custom-call(s32[4]{0:T(128)S(1)} %fusion.starts_ref, bf16[128,768]{1,0:T(8,128)(2,1)S(1)} %bitcast.23, bf16[128,256]{1,0:T(8,128)(2,1)S(1)} %collective-permute-done.refs_0_.refs_9_, bf16[128,256]{1,0:T(8,128)(2,1)S(1)} %collective-permute-done.1.refs_1_.refs_10_, ...), custom_call_target="tpu_custom_call" | custom-call | tf_op jit(solution)/shard_map/prefix_attention/pallas_call | solution.py:58
  21.4 0.0 collective-permute-done.5.refs_3_
  21.4 9.3 %collective-permute-done.6.refs_4_ = bf16[128,768]{1,0:T(8,128)(2,1)S(1)} collective-permute-done((bf16[128,768]{1,0:T(8,128)(2,1)S(1)}, bf16[128,768]{1,0:T(8,128)(2,1)S(1)}, u32[]{:S(2)}, u32[]{:S(2)}) %collective-permute-start.6) | collective-permute-done | bytes 196640 | tf_op jit(solution)/shard_map/ppermute | solution.py:160
  30.6 2.2 %collective-permute-done.7.refs_5_ = bf16[128,768]{1,0:T(8,128)(2,1)S(1)} collective-permute-done((bf16[128,768]{1,0:T(8,128)(2,1)S(1)}, bf16[128,768]{1,0:T(8,128)(2,1)S(1)}, u32[]{:S(2)}, u32[]{:S(2)}) %collective-permute-start.7) | collective-permute-done | bytes 196640 | tf_op jit(solution)/shard_map/ppermute | solution.py:160
  32.8 0.0 collective-permute-done.8.refs_6_
  32.8 0.0 collective-permute-done.9.refs_7_
  32.8 9.4 %response_attention.1 = bf16[2,512,512]{2,1,0:T(8,128)(2,1)} custom-call(s32[2]{0:T(128)S(1)} %bitcast.24, s32[1024,1]{1,0:T(8,128)S(1)} %copy.6.order_ref, bf16[128,768]{1,0:T(8,128)(2,1)S(1)} %get-tuple-element.8.refs_0_, bf16[128,768]{1,0:T(8,128)(2,1)S(1)} %collective-permute-done.3.refs_1_, bf16[128,768]{1,0:T(8,128)(2,1)S(1)} %collective-permute-done.4.refs_2_, ...), custom_call_target="tpu_custom_call" | custom-call | tf_op jit(solution)/shard_map/response_attention/pallas_call | solution.py:126
  (9 shorter events, 0.0 us)
Async XLA Ops:
  0.7 4.8 %copy-start = (bf16[1,128,768]{2,1,0:T(8,128)(2,1)S(1)}, bf16[1,128,768]{2,1,0:T(8,128)(2,1)}, u32[]{:S(2)}) copy-start(bf16[1,128,768]{2,1,0:T(8,128)(2,1)} %param.4) | copy-start | bytes 589828
  0.7 18.2 %copy-start.2 = (s32[1,1,1024]{2,1,0:T(1,128)S(1)}, s32[1,1,1024]{2,1,0:T(1,128)}, u32[]{:S(2)}) copy-start(s32[1,1,1024]{2,1,0:T(1,128)} %param.6) | copy-start | bytes 12292
  0.7 32.1 %copy-start.1 = (s32[1,2]{1,0:T(1,128)S(1)}, s32[1,2]{1,0:T(1,128)}, u32[]{:S(2)}) copy-start(s32[1,2]{1,0:T(1,128)} %param.7) | copy-start | bytes 28
  2.3 13.6 %collective-permute-start.3 = (bf16[128,768]{1,0:T(8,128)(2,1)S(1)}, bf16[128,768]{1,0:T(8,128)(2,1)S(1)}, u32[]{:S(2)}, u32[]{:S(2)}) collective-permute-start(bf16[128,768]{1,0:T(8,128)(2,1)S(1)} %get-tuple-element.7), channel_id=1, source_target_pairs={{0,4},{4,0},{8,12},{12,8},{16,20},{20,16},{24,28},{28,24},{1,5},{5... | collective-permute-start | bytes 589832 | tf_op jit(solution)/shard_map/ppermute | solution.py:160
  2.9 14.3 %collective-permute-start.4 = (bf16[128,768]{1,0:T(8,128)(2,1)S(1)}, bf16[128,768]{1,0:T(8,128)(2,1)S(1)}, u32[]{:S(2)}, u32[]{:S(2)}) collective-permute-start(bf16[128,768]{1,0:T(8,128)(2,1)S(1)} %get-tuple-element.6), channel_id=1, source_target_pairs={{0,8},{4,12},{8,0},{12,4},{16,24},{20,28},{24,16},{28,20},{1,9},{5... | collective-permute-start | bytes 589832 | tf_op jit(solution)/shard_map/ppermute | solution.py:160
  5.4 6.3 %collective-permute-start = (bf16[128,256]{1,0:T(8,128)(2,1)S(1)}, bf16[128,256]{1,0:T(8,128)(2,1)S(1)}, u32[]{:S(2)}, u32[]{:S(2)}) collective-permute-start(bf16[128,256]{1,0:T(8,128)(2,1)S(1)} %slice.4.refs_8_), channel_id=1, source_target_pairs={{0,1},{1,2},{2,3},{3,0},{4,5},{5,6},{6,7},{7,4},{8,9},{9,10},{10,1... | collective-permute-start | bytes 196616 | tf_op jit(solution)/shard_map/ppermute | solution.py:165
  7.1 7.4 %collective-permute-start.1 = (bf16[128,256]{1,0:T(8,128)(2,1)S(1)}, bf16[128,256]{1,0:T(8,128)(2,1)S(1)}, u32[]{:S(2)}, u32[]{:S(2)}) collective-permute-start(bf16[128,256]{1,0:T(8,128)(2,1)S(1)} %slice.4.refs_8_), channel_id=1, source_target_pairs={{0,2},{1,3},{2,0},{3,1},{4,6},{5,7},{6,4},{7,5},{8,10},{9,11},{10,... | collective-permute-start | bytes 196616 | tf_op jit(solution)/shard_map/ppermute | solution.py:165
  9.7 6.3 %collective-permute-start.2 = (bf16[128,256]{1,0:T(8,128)(2,1)S(1)}, bf16[128,256]{1,0:T(8,128)(2,1)S(1)}, u32[]{:S(2)}, u32[]{:S(2)}) collective-permute-start(bf16[128,256]{1,0:T(8,128)(2,1)S(1)} %slice.4.refs_8_), channel_id=1, source_target_pairs={{0,3},{1,0},{2,1},{3,2},{4,7},{5,4},{6,5},{7,6},{8,11},{9,8},{10,9... | collective-permute-start | bytes 196616 | tf_op jit(solution)/shard_map/ppermute | solution.py:165
  11.8 9.6 %collective-permute-start.5 = (bf16[128,768]{1,0:T(8,128)(2,1)S(1)}, bf16[128,768]{1,0:T(8,128)(2,1)S(1)}, u32[]{:S(2)}, u32[]{:S(2)}) collective-permute-start(bf16[128,768]{1,0:T(8,128)(2,1)S(1)} %get-tuple-element.5), channel_id=1, source_target_pairs={{0,12},{4,8},{8,4},{12,0},{16,28},{20,24},{24,20},{28,16},{1,13},{... | collective-permute-start | bytes 589832 | tf_op jit(solution)/shard_map/ppermute | solution.py:160
  14.4 16.2 %collective-permute-start.6 = (bf16[128,768]{1,0:T(8,128)(2,1)S(1)}, bf16[128,768]{1,0:T(8,128)(2,1)S(1)}, u32[]{:S(2)}, u32[]{:S(2)}) collective-permute-start(bf16[128,768]{1,0:T(8,128)(2,1)S(1)} %get-tuple-element.4), channel_id=1, source_target_pairs={{0,16},{4,20},{8,24},{12,28},{16,0},{20,4},{24,8},{28,12},{1,17},{... | collective-permute-start | bytes 589832 | tf_op jit(solution)/shard_map/ppermute | solution.py:160
  15.9 16.9 %collective-permute-start.7 = (bf16[128,768]{1,0:T(8,128)(2,1)S(1)}, bf16[128,768]{1,0:T(8,128)(2,1)S(1)}, u32[]{:S(2)}, u32[]{:S(2)}) collective-permute-start(bf16[128,768]{1,0:T(8,128)(2,1)S(1)} %get-tuple-element.3), channel_id=1, source_target_pairs={{0,20},{4,16},{8,28},{12,24},{16,4},{20,0},{24,12},{28,8},{1,21},{... | collective-permute-start | bytes 589832 | tf_op jit(solution)/shard_map/ppermute | solution.py:160
  16.0 16.9 %collective-permute-start.8 = (bf16[128,768]{1,0:T(8,128)(2,1)S(1)}, bf16[128,768]{1,0:T(8,128)(2,1)S(1)}, u32[]{:S(2)}, u32[]{:S(2)}) collective-permute-start(bf16[128,768]{1,0:T(8,128)(2,1)S(1)} %get-tuple-element.9), channel_id=1, source_target_pairs={{0,24},{4,28},{8,16},{12,20},{16,8},{20,12},{24,0},{28,4},{1,25},{... | collective-permute-start | bytes 589832 | tf_op jit(solution)/shard_map/ppermute | solution.py:160
  17.2 15.6 %collective-permute-start.9 = (bf16[128,768]{1,0:T(8,128)(2,1)S(1)}, bf16[128,768]{1,0:T(8,128)(2,1)S(1)}, u32[]{:S(2)}, u32[]{:S(2)}) collective-permute-start(bf16[128,768]{1,0:T(8,128)(2,1)S(1)} %get-tuple-element.2), channel_id=1, source_target_pairs={{0,28},{4,24},{8,20},{12,16},{16,12},{20,8},{24,4},{28,0},{1,29},{... | collective-permute-start | bytes 589832 | tf_op jit(solution)/shard_map/ppermute | solution.py:160

commit v2 on v1

--- a/solution.py
+++ b/solution.py
@@ -154,17 +154,37 @@
     rows_peer = sent.shape[1]
     assert peers & (peers - 1) == 0
 
-    blocks = [lax.dynamic_index_in_dim(sent, prompt_index, 0, keepdims=False)]
-    for k in range(1, peers):
-        block = lax.dynamic_index_in_dim(sent, prompt_index ^ k, 0, keepdims=False)
-        blocks.append(lax.ppermute(block, "prompt", [(j, j ^ k) for j in range(peers)]))
     order = (arrival_order[0, 0] ^ (prompt_index * rows_peer)).reshape(-1, 1)
 
-    prefix_kv = prefix_rows[:, feat - 2 * HEAD :]
+    def pick(index, k):
+        return lax.dynamic_index_in_dim(sent, index ^ k, 0, keepdims=False)
+
+    def swap(block, k):
+        return lax.ppermute(block, "prompt", [(j, j ^ k) for j in range(peers)])
+
+    def after(value, *done):
+        return lax.optimization_barrier((value, *done))[0]
+
+    ranks = sorted(range(1, peers), key=lambda k: (-(k >> 1).bit_count(), k))
+    lead, rest = ranks[:2], ranks[2:]
+    blocks = [None] * peers
+    picked = [pick(prompt_index, k) for k in lead]
+    *picked, index, prefix_kv = lax.optimization_barrier(
+        (*picked, prompt_index, prefix_rows[:, feat - 2 * HEAD :])
+    )
+    for k, block in zip(lead, picked):
+        blocks[k] = swap(block, k)
     shifted = [
         lax.ppermute(prefix_kv, "ctx", [(j, (j + t) % ctx_count) for j in range(ctx_count)])
         for t in range(1, ctx_count)
     ]
+    earlier = shifted + [blocks[k] for k in lead]
+    for n, k in enumerate(rest):
+        block = pick(index, k)
+        if n < len(earlier):
+            block = after(block, earlier[n])
+        blocks[k] = swap(block, k)
+    blocks[0] = pick(index, 0)
     starts = (ctx_index - jnp.arange(ctx_count, dtype=jnp.int32)) % ctx_count * prefix_len
     prefix_out = prefix_attention(starts, prefix_rows, shifted)
     resp_out = response_attention(resp_len[0], order, blocks, [prefix_kv] + shifted)

time: 42.7 us -> 35.6 us (0.83)
  waiting for transfers between devices: 14.9 us -> 5.07 us
  local copies, waits for them, and re-layouts: 1.88 us -> 3.57 us
  starting transfers between devices: 13 us -> 14.2 us
    ppermute x7, waiting for transfers between devices: 11.5 us -> 3.78 us  [swap(): return lax.ppermute(block, 'prompt', [(j, j ^ k) for j in range(peers)])]
    ppermute x3, waiting for transfers between devices: 3.41 us -> 1.29 us  [body(): lax.ppermute(prefix_kv, 'ctx', [(j, (j + t) % ctx_count) for j in range(c...]
    ppermute x7, starting transfers between devices: 7.47 us -> 9.55 us  [swap(): return lax.ppermute(block, 'prompt', [(j, j ^ k) for j in range(peers)])]
    ppermute x3, starting transfers between devices: 5.57 us -> 4.61 us  [body(): lax.ppermute(prefix_kv, 'ctx', [(j, (j + t) % ctx_count) for j in range(c...]
    slice x1, local copies, waits for them, and re-layouts: 0.01 us -> 0.85 us  [body(): prefix_rows[:, feat - 2 * HEAD:]]
    squeeze x1 -> x2, local copies, waits for them, and re-layouts: 1.64 us -> 2.48 us  [pick(): return lax.dynamic_index_in_dim(sent, index ^ k, 0, keepdims=False)]
  transfers between devices with their start and end apart: 10 -> 10, of which waited for: 4 -> 5; matrix products, arithmetic and copies ran while one was open for 1% -> 5% of each run, Pallas kernels for 5% -> 6%
where the time goes in v2:
time: 35.6 us; the launch traced here: 35.2 us
  starting transfers between devices  14.2 us (40%)
  Pallas kernels  11.7 us (33%)
  waiting for transfers between devices  5.07 us (14%)
  local copies, waits for them, and re-layouts  3.57 us (10%)
  between operations  0.7 us (2%)
    ppermute x7, starting transfers between devices, swap(): return lax.ppermute(block, 'prompt', [(j, j ^ k) for j in range(peers)])  9.55 us
    pallas_call x1, Pallas kernels, response_attention(): pl.pallas_call(functools.partial(response_kernel, len(blocks), len(pieces...  9.42 us
    ppermute x3, starting transfers between devices, body(): lax.ppermute(prefix_kv, 'ctx', [(j, (j + t) % ctx_count) for j in range(c...  4.61 us
    ppermute x7, waiting for transfers between devices, swap(): return lax.ppermute(block, 'prompt', [(j, j ^ k) for j in range(peers)])  3.78 us
    squeeze x2, local copies, waits for them, and re-layouts, pick(): return lax.dynamic_index_in_dim(sent, index ^ k, 0, keepdims=False)  2.48 us
    pallas_call x1, Pallas kernels, prefix_attention(): pl.pallas_call(prefix_kernel, out_shape=jax.ShapeDtypeStruct((row_count,...  2.27 us
    ppermute x3, waiting for transfers between devices, body(): lax.ppermute(prefix_kv, 'ctx', [(j, (j + t) % ctx_count) for j in range(c...  1.29 us
    slice x1, local copies, waits for them, and re-layouts, body(): prefix_rows[:, feat - 2 * HEAD:]  0.85 us
  transfers between devices with their start and end apart: 10, of which 5 were waited for; matrix products, arithmetic and copies ran while one was open for 5% of the time, Pallas kernels for 6%

profile of v2, /device:TPU:0, one launch (start us, length us, event | category | flops | bytes accessed | tf_op | source)
XLA Modules:
  0.0 35.2 jit_solution(4041645132793941631)
XLA Ops:
  0.6 0.8 %slice.4.refs_8_ = bf16[128,256]{1,0:T(8,128)(2,1)S(1)} slice(bf16[128,768]{1,0:T(8,128)(2,1)} %bitcast.22), slice={[0:128], [512:768]} | slice | bytes 131072 | tf_op jit(solution)/shard_map/slice | solution.py:173
  1.5 1.1 %dynamic-slice_bitcast_fusion.6 = (bf16[128,768]{1,0:T(8,128)(2,1)S(1)}, bf16[128,768]{1,0:T(8,128)(2,1)S(1)}) fusion(bf16[1,1,8,128,768]{4,3,2,1,0:T(8,128)(2,1)} %param.5, s32[]{:T(128)S(6)} %select_n.34, s32[]{:T(128)S(6)} %select_n.33), kind=kLoop, calls=%fused_computation.6 | loop fusion | bytes 786440 | tf_op jit(solution)/shard_map/jit(dynamic_index_in_dim)/squeeze | solution.py:160
  2.6 0.0 copy-start
  2.6 4.0 %collective-permute-start.8 = (bf16[128,768]{1,0:T(8,128)(2,1)S(1)}, bf16[128,768]{1,0:T(8,128)(2,1)S(1)}, u32[]{:S(2)}, u32[]{:S(2)}) collective-permute-start(bf16[128,768]{1,0:T(8,128)(2,1)S(1)} %get-tuple-element.18), channel_id=1, source_target_pairs={{0,24},{4,28},{8,16},{12,20},{16,8},{20,12},{24,0},{28,4},{1,25},{... | collective-permute-start | bytes 589832 | tf_op jit(solution)/shard_map/ppermute | solution.py:163
  6.5 0.0 collective-permute-start.3
  6.5 2.6 %collective-permute-start.1 = (bf16[128,256]{1,0:T(8,128)(2,1)S(1)}, bf16[128,256]{1,0:T(8,128)(2,1)S(1)}, u32[]{:S(2)}, u32[]{:S(2)}) collective-permute-start(bf16[128,256]{1,0:T(8,128)(2,1)S(1)} %slice.4.refs_8_), channel_id=1, source_target_pairs={{0,2},{1,3},{2,0},{3,1},{4,6},{5,7},{6,4},{7,5},{8,10},{9,11},{10,... | collective-permute-start | bytes 196616 | tf_op jit(solution)/shard_map/ppermute | solution.py:178
  9.1 1.3 %collective-permute-start.2 = (bf16[128,256]{1,0:T(8,128)(2,1)S(1)}, bf16[128,256]{1,0:T(8,128)(2,1)S(1)}, u32[]{:S(2)}, u32[]{:S(2)}) collective-permute-start(bf16[128,256]{1,0:T(8,128)(2,1)S(1)} %slice.4.refs_8_), channel_id=1, source_target_pairs={{0,3},{1,0},{2,1},{3,2},{4,7},{5,4},{6,5},{7,6},{8,11},{9,8},{10,9... | collective-permute-start | bytes 196616 | tf_op jit(solution)/shard_map/ppermute | solution.py:178
  10.5 0.7 %collective-permute-start = (bf16[128,256]{1,0:T(8,128)(2,1)S(1)}, bf16[128,256]{1,0:T(8,128)(2,1)S(1)}, u32[]{:S(2)}, u32[]{:S(2)}) collective-permute-start(bf16[128,256]{1,0:T(8,128)(2,1)S(1)} %slice.4.refs_8_), channel_id=1, source_target_pairs={{0,1},{1,2},{2,3},{3,0},{4,5},{5,6},{6,7},{7,4},{8,9},{9,10},{10,1... | collective-permute-start | bytes 196616 | tf_op jit(solution)/shard_map/ppermute | solution.py:178
  11.1 1.4 %dynamic-slice_bitcast_fusion = (bf16[128,768]{1,0:T(8,128)(2,1)S(1)}, bf16[128,768]{1,0:T(8,128)(2,1)S(1)}, bf16[128,768]{1,0:T(8,128)(2,1)S(1)}, bf16[128,768]...) fusion(bf16[1,1,8,128,768]{4,3,2,1,0:T(8,128)(2,1)} %param.5, s32[]{:T(128)S(6)} %select_n.40, ...), kind=kLoop, calls=%fused_computation | loop fusion | bytes 2359320 | tf_op jit(solution)/shard_map/jit(dynamic_index_in_dim)/squeeze | solution.py:160
  12.6 0.9 %collective-permute-done.1.refs_1_.refs_10_ = bf16[128,256]{1,0:T(8,128)(2,1)S(1)} collective-permute-done((bf16[128,256]{1,0:T(8,128)(2,1)S(1)}, bf16[128,256]{1,0:T(8,128)(2,1)S(1)}, u32[]{:S(2)}, u32[]{:S(2)}) %collective-permute-start.1) | collective-permute-done | bytes 65568 | tf_op jit(solution)/shard_map/ppermute | solution.py:178
  13.5 1.1 %collective-permute-start.6 = (bf16[128,768]{1,0:T(8,128)(2,1)S(1)}, bf16[128,768]{1,0:T(8,128)(2,1)S(1)}, u32[]{:S(2)}, u32[]{:S(2)}) collective-permute-start(bf16[128,768]{1,0:T(8,128)(2,1)S(1)} %get-tuple-element.16), channel_id=1, source_target_pairs={{0,12},{4,8},{8,4},{12,0},{16,28},{20,24},{24,20},{28,16},{1,13},{... | collective-permute-start | bytes 589832 | tf_op jit(solution)/shard_map/ppermute | solution.py:163
  14.6 1.5 %collective-permute-start.7 = (bf16[128,768]{1,0:T(8,128)(2,1)S(1)}, bf16[128,768]{1,0:T(8,128)(2,1)S(1)}, u32[]{:S(2)}, u32[]{:S(2)}) collective-permute-start(bf16[128,768]{1,0:T(8,128)(2,1)S(1)} %get-tuple-element.17), channel_id=1, source_target_pairs={{0,16},{4,20},{8,24},{12,28},{16,0},{20,4},{24,8},{28,12},{1,17},{... | collective-permute-start | bytes 589832 | tf_op jit(solution)/shard_map/ppermute | solution.py:163
  16.1 0.4 %collective-permute-done.refs_0_.refs_9_ = bf16[128,256]{1,0:T(8,128)(2,1)S(1)} collective-permute-done((bf16[128,256]{1,0:T(8,128)(2,1)S(1)}, bf16[128,256]{1,0:T(8,128)(2,1)S(1)}, u32[]{:S(2)}, u32[]{:S(2)}) %collective-permute-start) | collective-permute-done | bytes 65568 | tf_op jit(solution)/shard_map/ppermute | solution.py:178
  16.5 1.3 %collective-permute-start.5 = (bf16[128,768]{1,0:T(8,128)(2,1)S(1)}, bf16[128,768]{1,0:T(8,128)(2,1)S(1)}, u32[]{:S(2)}, u32[]{:S(2)}) collective-permute-start(bf16[128,768]{1,0:T(8,128)(2,1)S(1)} %get-tuple-element.15), channel_id=1, source_target_pairs={{0,8},{4,12},{8,0},{12,4},{16,24},{20,28},{24,16},{28,20},{1,9},{5... | collective-permute-start | bytes 589832 | tf_op jit(solution)/shard_map/ppermute | solution.py:163
  17.8 0.0 collective-permute-done.8.refs_6_
  17.8 0.5 %collective-permute-start.9 = (bf16[128,768]{1,0:T(8,128)(2,1)S(1)}, bf16[128,768]{1,0:T(8,128)(2,1)S(1)}, u32[]{:S(2)}, u32[]{:S(2)}) collective-permute-start(bf16[128,768]{1,0:T(8,128)(2,1)S(1)} %get-tuple-element.19), channel_id=1, source_target_pairs={{0,20},{4,16},{8,28},{12,24},{16,4},{20,0},{24,12},{28,8},{1,21},{... | collective-permute-start | bytes 589832 | tf_op jit(solution)/shard_map/ppermute | solution.py:163
  18.3 0.0 collective-permute-done.3.refs_7_
  18.3 1.2 %collective-permute-start.4 = (bf16[128,768]{1,0:T(8,128)(2,1)S(1)}, bf16[128,768]{1,0:T(8,128)(2,1)S(1)}, u32[]{:S(2)}, u32[]{:S(2)}) collective-permute-start(bf16[128,768]{1,0:T(8,128)(2,1)S(1)} %get-tuple-element.14), channel_id=1, source_target_pairs={{0,4},{4,0},{8,12},{12,8},{16,20},{20,16},{24,28},{28,24},{1,5},{5... | collective-permute-start | bytes 589832 | tf_op jit(solution)/shard_map/ppermute | solution.py:163
  19.5 0.2 copy.6.order_ref
  19.7 2.3 %prefix_attention.1 = bf16[128,512]{1,0:T(8,128)(2,1)} custom-call(s32[4]{0:T(128)S(1)} %fusion.starts_ref, bf16[128,768]{1,0:T(8,128)(2,1)S(1)} %bitcast.23, bf16[128,256]{1,0:T(8,128)(2,1)S(1)} %collective-permute-done.refs_0_.refs_9_, bf16[128,256]{1,0:T(8,128)(2,1)S(1)} %collective-permute-done.1.refs_1_.refs_10_, ...), custom_call_target="tpu_custom_call" | custom-call | tf_op jit(solution)/shard_map/prefix_attention/pallas_call | solution.py:58
  22.0 0.3 collective-permute-done.7.refs_4_
  22.3 2.6 %collective-permute-done.5.refs_2_ = bf16[128,768]{1,0:T(8,128)(2,1)S(1)} collective-permute-done((bf16[128,768]{1,0:T(8,128)(2,1)S(1)}, bf16[128,768]{1,0:T(8,128)(2,1)S(1)}, u32[]{:S(2)}, u32[]{:S(2)}) %collective-permute-start.5) | collective-permute-done | bytes 196640 | tf_op jit(solution)/shard_map/ppermute | solution.py:163
  24.9 0.9 %collective-permute-done.9.refs_5_ = bf16[128,768]{1,0:T(8,128)(2,1)S(1)} collective-permute-done((bf16[128,768]{1,0:T(8,128)(2,1)S(1)}, bf16[128,768]{1,0:T(8,128)(2,1)S(1)}, u32[]{:S(2)}, u32[]{:S(2)}) %collective-permute-start.9) | collective-permute-done | bytes 196640 | tf_op jit(solution)/shard_map/ppermute | solution.py:163
  25.8 9.4 %response_attention.1 = bf16[2,512,512]{2,1,0:T(8,128)(2,1)} custom-call(s32[2]{0:T(128)S(1)} %bitcast.24, s32[1024,1]{1,0:T(8,128)S(1)} %copy.6.order_ref, bf16[128,768]{1,0:T(8,128)(2,1)S(1)} %get-tuple-element.24.refs_0_, bf16[128,768]{1,0:T(8,128)(2,1)S(1)} %collective-permute-done.4.refs_1_, bf16[128,768]{1,0:T(8,128)(2,1)S(1)} %collective-permute-done.5.refs_2_, ...), custom_call_target="tpu_custom_call" | custom-call | tf_op jit(solution)/shard_map/response_attention/pallas_call | solution.py:126
  (10 shorter events, 0.0 us)
Async XLA Ops:
  1.5 18.0 %copy-start.2 = (s32[1,1,1024]{2,1,0:T(1,128)S(1)}, s32[1,1,1024]{2,1,0:T(1,128)}, u32[]{:S(2)}) copy-start(s32[1,1,1024]{2,1,0:T(1,128)} %param.6) | copy-start | bytes 12292
  2.6 17.2 %copy-start = (bf16[1,128,768]{2,1,0:T(8,128)(2,1)S(1)}, bf16[1,128,768]{2,1,0:T(8,128)(2,1)}, u32[]{:S(2)}) copy-start(bf16[1,128,768]{2,1,0:T(8,128)(2,1)} %param.4) | copy-start | bytes 589828
  2.6 15.3 %collective-permute-start.8 = (bf16[128,768]{1,0:T(8,128)(2,1)S(1)}, bf16[128,768]{1,0:T(8,128)(2,1)S(1)}, u32[]{:S(2)}, u32[]{:S(2)}) collective-permute-start(bf16[128,768]{1,0:T(8,128)(2,1)S(1)} %get-tuple-element.18), channel_id=1, source_target_pairs={{0,24},{4,28},{8,16},{12,20},{16,8},{20,12},{24,0},{28,4},{1,25},{... | collective-permute-start | bytes 589832 | tf_op jit(solution)/shard_map/ppermute | solution.py:163
  6.5 11.8 %collective-permute-start.3 = (bf16[128,768]{1,0:T(8,128)(2,1)S(1)}, bf16[128,768]{1,0:T(8,128)(2,1)S(1)}, u32[]{:S(2)}, u32[]{:S(2)}) collective-permute-start(bf16[128,768]{1,0:T(8,128)(2,1)S(1)} %get-tuple-element.13), channel_id=1, source_target_pairs={{0,28},{4,24},{8,20},{12,16},{16,12},{20,8},{24,4},{28,0},{1,29},{... | collective-permute-start | bytes 589832 | tf_op jit(solution)/shard_map/ppermute | solution.py:163
  6.5 6.9 %collective-permute-start.1 = (bf16[128,256]{1,0:T(8,128)(2,1)S(1)}, bf16[128,256]{1,0:T(8,128)(2,1)S(1)}, u32[]{:S(2)}, u32[]{:S(2)}) collective-permute-start(bf16[128,256]{1,0:T(8,128)(2,1)S(1)} %slice.4.refs_8_), channel_id=1, source_target_pairs={{0,2},{1,3},{2,0},{3,1},{4,6},{5,7},{6,4},{7,5},{8,10},{9,11},{10,... | collective-permute-start | bytes 196616 | tf_op jit(solution)/shard_map/ppermute | solution.py:178
  9.1 5.5 %collective-permute-start.2 = (bf16[128,256]{1,0:T(8,128)(2,1)S(1)}, bf16[128,256]{1,0:T(8,128)(2,1)S(1)}, u32[]{:S(2)}, u32[]{:S(2)}) collective-permute-start(bf16[128,256]{1,0:T(8,128)(2,1)S(1)} %slice.4.refs_8_), channel_id=1, source_target_pairs={{0,3},{1,0},{2,1},{3,2},{4,7},{5,4},{6,5},{7,6},{8,11},{9,8},{10,9... | collective-permute-start | bytes 196616 | tf_op jit(solution)/shard_map/ppermute | solution.py:178
  10.5 6.1 %collective-permute-start = (bf16[128,256]{1,0:T(8,128)(2,1)S(1)}, bf16[128,256]{1,0:T(8,128)(2,1)S(1)}, u32[]{:S(2)}, u32[]{:S(2)}) collective-permute-start(bf16[128,256]{1,0:T(8,128)(2,1)S(1)} %slice.4.refs_8_), channel_id=1, source_target_pairs={{0,1},{1,2},{2,3},{3,0},{4,5},{5,6},{6,7},{7,4},{8,9},{9,10},{10,1... | collective-permute-start | bytes 196616 | tf_op jit(solution)/shard_map/ppermute | solution.py:178
  11.1 14.6 %copy-start.1 = (s32[1,2]{1,0:T(1,128)S(1)}, s32[1,2]{1,0:T(1,128)}, u32[]{:S(2)}) copy-start(s32[1,2]{1,0:T(1,128)} %param.7) | copy-start | bytes 28
  13.5 8.5 %collective-permute-start.6 = (bf16[128,768]{1,0:T(8,128)(2,1)S(1)}, bf16[128,768]{1,0:T(8,128)(2,1)S(1)}, u32[]{:S(2)}, u32[]{:S(2)}) collective-permute-start(bf16[128,768]{1,0:T(8,128)(2,1)S(1)} %get-tuple-element.16), channel_id=1, source_target_pairs={{0,12},{4,8},{8,4},{12,0},{16,28},{20,24},{24,20},{28,16},{1,13},{... | collective-permute-start | bytes 589832 | tf_op jit(solution)/shard_map/ppermute | solution.py:163
  14.6 7.7 %collective-permute-start.7 = (bf16[128,768]{1,0:T(8,128)(2,1)S(1)}, bf16[128,768]{1,0:T(8,128)(2,1)S(1)}, u32[]{:S(2)}, u32[]{:S(2)}) collective-permute-start(bf16[128,768]{1,0:T(8,128)(2,1)S(1)} %get-tuple-element.17), channel_id=1, source_target_pairs={{0,16},{4,20},{8,24},{12,28},{16,0},{20,4},{24,8},{28,12},{1,17},{... | collective-permute-start | bytes 589832 | tf_op jit(solution)/shard_map/ppermute | solution.py:163
  16.5 8.4 %collective-permute-start.5 = (bf16[128,768]{1,0:T(8,128)(2,1)S(1)}, bf16[128,768]{1,0:T(8,128)(2,1)S(1)}, u32[]{:S(2)}, u32[]{:S(2)}) collective-permute-start(bf16[128,768]{1,0:T(8,128)(2,1)S(1)} %get-tuple-element.15), channel_id=1, source_target_pairs={{0,8},{4,12},{8,0},{12,4},{16,24},{20,28},{24,16},{28,20},{1,9},{5... | collective-permute-start | bytes 589832 | tf_op jit(solution)/shard_map/ppermute | solution.py:163
  17.8 8.0 %collective-permute-start.9 = (bf16[128,768]{1,0:T(8,128)(2,1)S(1)}, bf16[128,768]{1,0:T(8,128)(2,1)S(1)}, u32[]{:S(2)}, u32[]{:S(2)}) collective-permute-start(bf16[128,768]{1,0:T(8,128)(2,1)S(1)} %get-tuple-element.19), channel_id=1, source_target_pairs={{0,20},{4,16},{8,28},{12,24},{16,4},{20,0},{24,12},{28,8},{1,21},{... | collective-permute-start | bytes 589832 | tf_op jit(solution)/shard_map/ppermute | solution.py:163
  18.3 7.5 %collective-permute-start.4 = (bf16[128,768]{1,0:T(8,128)(2,1)S(1)}, bf16[128,768]{1,0:T(8,128)(2,1)S(1)}, u32[]{:S(2)}, u32[]{:S(2)}) collective-permute-start(bf16[128,768]{1,0:T(8,128)(2,1)S(1)} %get-tuple-element.14), channel_id=1, source_target_pairs={{0,4},{4,0},{8,12},{12,8},{16,20},{20,16},{24,28},{28,24},{1,5},{5... | collective-permute-start | bytes 589832 | tf_op jit(solution)/shard_map/ppermute | solution.py:163

commit v3 on v1

v3 whole, which is shorter than its diff:
```python
import functools
import math

import jax
import jax.numpy as jnp
from jax import lax
from jax.experimental import pallas as pl
from jax.experimental.pallas import tpu as pltpu
from jax.sharding import PartitionSpec as P

HEAD = 128
MASKED_SCORE = -1e30
EXP2_SCALE = HEAD ** (-0.5) * math.log2(math.e)
VMEM_LIMIT = 24 * 1024 * 1024


def mix(a, b):
    return lax.dot_general(a, b, (((1,), (0,)), ((), ())), preferred_element_type=jnp.float32)


def match(a, b):
    return lax.dot_general(a, b, (((1,), (1,)), ((), ())), preferred_element_type=jnp.float32)


def with_ones(values):
    return jnp.concatenate([values, jnp.ones_like(values)], axis=1)


def attend(scores, values):
    top = functools.reduce(jnp.maximum, [jnp.max(s, axis=1, keepdims=True) for s in scores])
    total = None
    for s, v in zip(scores, values):
        weights = jnp.exp2((s - top) * EXP2_SCALE).astype(jnp.bfloat16)
        part = mix(weights, v)
        total = part if total is None else total + part
    return total[:, :HEAD] / total[:, HEAD:]


def prefix_part(starts_ref, rows_ref, pk_ref, pv_ref, out_ref):
    row_count = rows_ref.shape[0]
    heads = rows_ref.shape[1] // HEAD - 2
    row_pos = starts_ref[0] + lax.broadcasted_iota(jnp.int32, (row_count, 1), 0)
    seen = []
    for first in range(0, pk_ref.shape[0], row_count):
        key_pos = starts_ref[first // row_count] + lax.broadcasted_iota(jnp.int32, (1, row_count), 1)
        seen.append(key_pos <= row_pos)
    seen = jnp.concatenate(seen, axis=1)
    seen = jnp.concatenate([seen] * heads, axis=0)
    q = jnp.concatenate([rows_ref[:, h * HEAD : (h + 1) * HEAD] for h in range(heads)], axis=0)
    scores = jnp.where(seen, match(q, pk_ref[...]), MASKED_SCORE)
    result = attend([scores], [pv_ref[...]]).astype(jnp.bfloat16)
    for h in range(heads):
        out_ref[:, h * HEAD : (h + 1) * HEAD] = result[h * row_count : (h + 1) * row_count]


def place(order_ref, arrived, r, slot):
    chosen = lax.broadcasted_iota(jnp.int32, (slot, arrived.shape[0]), 1)
    chosen = chosen == order_ref[r * slot : (r + 1) * slot, :]
    chosen = jnp.where(chosen, 1.0, 0.0).astype(jnp.bfloat16)
    return mix(chosen, arrived).astype(jnp.bfloat16)


def response_part(len_ref, queries, first_head, keys, values, pk_ref, pv_ref, hold_ref, out_ref, sems):
    slot = queries[0].shape[0]
    heads = queries[0].shape[1] // HEAD
    step = math.gcd(slot, 256)
    chunks = slot // step
    causal = lax.broadcasted_iota(jnp.int32, (step, step), 1) <= lax.broadcasted_iota(
        jnp.int32, (step, step), 0
    )
    items = [(r, c, h) for r in range(len(queries)) for c in range(chunks) for h in range(heads)]

    def scored(r, c, h):
        low, high = c * step, (c + 1) * step
        q = queries[r][low:high, h * HEAD : (h + 1) * HEAD]
        scores = [match(q, pk_ref[...])]
        if c:
            scores.append(match(q, keys[r][:low]))
        scores.append(jnp.where(causal, match(q, keys[r][low:high]), MASKED_SCORE))
        return scores

    columns = pl.ds(first_head * HEAD, heads * HEAD)
    copies = []
    ahead = scored(*items[0])
    for n, (r, c, h) in enumerate(items):
        scores = ahead
        if n + 1 < len(items):
            ahead = scored(*items[n + 1])
        low, high = c * step, (c + 1) * step
        value = [pv_ref[...]] + ([values[r][:low]] if c else []) + [values[r][low:high]]
        live = low + lax.broadcasted_iota(jnp.int32, (step, 1), 0) < len_ref[r]
        result = jnp.where(live, attend(scores, value), 0.0)
        hold_ref[r, low:high, h * HEAD : (h + 1) * HEAD] = result.astype(jnp.bfloat16)
        if h == heads - 1:
            copy = pltpu.make_async_copy(
                hold_ref.at[r, pl.ds(low, step)],
                out_ref.at[r, pl.ds(low, step), columns],
                sems.at[r, c],
            )
            copy.start()
            copies.append(copy)
    for copy in copies:
        copy.wait()


def load_prefix(pieces, pk_ref, pv_ref):
    first = 0
    for p in pieces:
        pk_ref[first : first + p.shape[0], :] = p[:, :HEAD]
        pv_ref[first : first + p.shape[0], :] = with_ones(p[:, HEAD:])
        first += p.shape[0]


def prefix_kernel(starts_ref, rows_ref, kv_ref, out_ref, pk_ref, pv_ref):
    load_prefix([kv_ref], pk_ref, pv_ref)
    prefix_part(starts_ref, rows_ref, pk_ref, pv_ref, out_ref)


def prefix_call(starts, rows, kv):
    return pl.pallas_call(
        prefix_kernel,
        out_shape=jax.ShapeDtypeStruct((rows.shape[0], rows.shape[1] - 2 * HEAD), jnp.bfloat16),
        in_specs=[SCALARS, WHOLE, WHOLE],
        out_specs=WHOLE,
        scratch_shapes=prefix_scratch(kv.shape[0]),
        compiler_params=pltpu.CompilerParams(vmem_limit_bytes=VMEM_LIMIT),
        cost_estimate=pl.CostEstimate(flops=10**9, bytes_accessed=10**6, transcendentals=0),
        name="prefix_attention",
    )(starts, rows, kv)


def response_kernel(len_ref, order_ref, sent_ref, prefix_ref, *refs):
    blocks = refs[:-7]
    out_ref, arrived_ref, pk_ref, pv_ref, hold_ref, sems, own_sem = refs[-7:]
    responses, slot, span = hold_ref.shape
    index = lax.axis_index("prompt")
    rows_peer = sent_ref.shape[1]
    first = pl.multiple_of(index * rows_peer, rows_peer)
    own = pltpu.make_async_copy(
        sent_ref.at[index], arrived_ref.at[pl.ds(first, rows_peer)], own_sem
    )
    own.start()
    load_prefix([prefix_ref], pk_ref, pv_ref)
    for k, b in enumerate(blocks, 1):
        first = pl.multiple_of((index ^ k) * rows_peer, rows_peer)
        arrived_ref[pl.ds(first, rows_peer), :] = b[...]
    own.wait()
    placed = [place(order_ref, arrived_ref[...], r, slot) for r in range(responses)]
    response_part(
        len_ref,
        [p[:, :span] for p in placed],
        0,
        [p[:, span : span + HEAD] for p in placed],
        [with_ones(p[:, span + HEAD :]) for p in placed],
        pk_ref,
        pv_ref,
        hold_ref,
        out_ref,
        sems,
    )


WHOLE = pl.BlockSpec(memory_space=pltpu.VMEM)
SCALARS = pl.BlockSpec(memory_space=pltpu.SMEM)
ANYWHERE = pl.BlockSpec(memory_space=pl.ANY)
IN_HBM = pl.BlockSpec(memory_space=pltpu.HBM)


def prefix_scratch(count):
    return [pltpu.VMEM((count, HEAD), jnp.bfloat16), pltpu.VMEM((count, 2 * HEAD), jnp.bfloat16)]


def response_call(lengths, order, sent, prefix_kv, blocks):
    responses = lengths.shape[0]
    slot = order.shape[0] // responses
    feat = sent.shape[2]
    span = feat - 2 * HEAD
    return pl.pallas_call(
        response_kernel,
        out_shape=jax.ShapeDtypeStruct((responses, slot, span), jnp.bfloat16),
        in_specs=[SCALARS, WHOLE, IN_HBM, WHOLE] + [WHOLE] * len(blocks),
        out_specs=ANYWHERE,
        scratch_shapes=[pltpu.VMEM((responses * slot, feat), jnp.bfloat16)]
        + prefix_scratch(prefix_kv.shape[0])
        + [
            pltpu.VMEM((responses, slot, span), jnp.bfloat16),
            pltpu.SemaphoreType.DMA((responses, slot // math.gcd(slot, 256))),
            pltpu.SemaphoreType.DMA,
        ],
        compiler_params=pltpu.CompilerParams(vmem_limit_bytes=VMEM_LIMIT),
        cost_estimate=pl.CostEstimate(flops=5 * 10**9, bytes_accessed=4 * 10**6, transcendentals=0),
        name="response_attention",
    )(lengths, order, sent, prefix_kv, *blocks)


def body(prefix_qkv, rollout, arrival_order, resp_len):
    peers = lax.axis_size("prompt")
    ctx_count = lax.axis_size("ctx")
    ctx_index = lax.axis_index("ctx")
    prefix_rows = prefix_qkv[0]
    prefix_len, feat = prefix_rows.shape
    sent = rollout[0, 0]
    assert peers & (peers - 1) == 0

    def after(value, *done):
        return lax.optimization_barrier((value, *done))[0]

    def pick(index, k):
        return lax.dynamic_index_in_dim(sent, index ^ k, 0, keepdims=False)

    ks = sorted(range(1, peers), key=lambda k: (-(k >> 1).bit_count(), k & 1, -k))
    first = pick(lax.axis_index("prompt"), ks[0])
    index, rows, first = lax.optimization_barrier((lax.axis_index("prompt"), prefix_rows, first))
    picked = {k: pick(index, k) for k in ks[1:]}
    picked[ks[0]] = first
    prefix_kv = rows[:, feat - 2 * HEAD :]

    swaps = [("prompt", k) for k in ks]
    shifts = [("ctx", t) for t in range(1, ctx_count)]
    plan = swaps[:3] + shifts[:2] + swaps[3:5] + shifts[2:] + swaps[5:]
    freed = plan[3:5] + plan[:3] + plan[5:]
    got = {}
    for n, (axis, by) in enumerate(plan):
        if axis == "ctx":
            value, pairs = prefix_kv, [(j, (j + by) % ctx_count) for j in range(ctx_count)]
        else:
            value, pairs = picked[by], [(j, j ^ by) for j in range(peers)]
        if n >= 5:
            value = after(value, got[freed[n - 5]])
        got[axis, by] = lax.ppermute(value, axis, pairs)
    blocks = [got["prompt", k] for k in range(1, peers)]
    prefix_kv = jnp.concatenate([prefix_kv] + [got[s] for s in shifts], axis=0)

    order = arrival_order[0, 0].reshape(-1, 1)
    starts = (ctx_index - jnp.arange(ctx_count, dtype=jnp.int32)) % ctx_count * prefix_len
    prefix_out = prefix_call(starts, prefix_rows, prefix_kv)
    resp_out = response_call(
        resp_len[0], order, sent, prefix_kv, blocks
    )
    return (prefix_out[None], resp_out[None])


def solution(mesh):
    placed = (
        P("prompt", "ctx", None),
        P("prompt", "ctx", None, None, None),
        P("prompt", "ctx", None),
        P("prompt", "ctx"),
    )
    return jax.shard_map(
        body,
        mesh=mesh,
        in_specs=placed,
        out_specs=(P("prompt", "ctx", None), P("prompt", "ctx", None, None)),
        check_vma=False,
    )
```

time: 42.7 us -> 33.1 us (0.78)
  waiting for transfers between devices: 14.9 us -> 5.11 us
  Pallas kernels: 11.7 us -> 9.83 us
  starting transfers between devices: 13 us -> 14.5 us
  local copies, waits for them, and re-layouts: 1.88 us -> 2.65 us
    ppermute x10, waiting for transfers between devices: 14.9 us -> 5.11 us  [body(): got[axis, by] = lax.ppermute(value, axis, pairs)]
    pallas_call x2, Pallas kernels: 11.7 us -> 9.83 us  [the longest x1 7.82 us: response_call(): pl.pallas_call(response_kernel, out_shape=jax.ShapeDtypeStruct((responses...]
    ppermute x10, starting transfers between devices: 13 us -> 14.5 us  [body(): got[axis, by] = lax.ppermute(value, axis, pairs)]
    squeeze x1 -> x2, local copies, waits for them, and re-layouts: 1.64 us -> 2.41 us  [pick(): return lax.dynamic_index_in_dim(sent, index ^ k, 0, keepdims=False)]
  transfers between devices with their start and end apart: 10 -> 10, of which waited for: 4 -> 5; matrix products, arithmetic and copies ran while one was open for 1% -> 5% of each run, Pallas kernels for 5% -> 6%
where the time goes in v3:
time: 33.1 us; the launch traced here: 32.9 us
  starting transfers between devices  14.5 us (44%)
  Pallas kernels  9.83 us (30%)
  waiting for transfers between devices  5.11 us (15%)
  local copies, waits for them, and re-layouts  2.65 us (8%)
  between operations  0.73 us (2%)
    ppermute x10, starting transfers between devices, body(): got[axis, by] = lax.ppermute(value, axis, pairs)  14.5 us
    pallas_call x1, Pallas kernels, response_call(): pl.pallas_call(response_kernel, out_shape=jax.ShapeDtypeStruct((responses...  7.82 us
    ppermute x10, waiting for transfers between devices, body(): got[axis, by] = lax.ppermute(value, axis, pairs)  5.11 us
    squeeze x2, local copies, waits for them, and re-layouts, pick(): return lax.dynamic_index_in_dim(sent, index ^ k, 0, keepdims=False)  2.41 us
    pallas_call x1, Pallas kernels, prefix_call(): pl.pallas_call(prefix_kernel, out_shape=jax.ShapeDtypeStruct((rows.shape[...  2.01 us
  transfers between devices with their start and end apart: 10, of which 5 were waited for; matrix products, arithmetic and copies ran while one was open for 5% of the time, Pallas kernels for 6%

profile of v3, /device:TPU:0, one launch (start us, length us, event | category | flops | bytes accessed | tf_op | source)
XLA Modules:
  0.0 32.9 jit_solution(18305737238257396172)
XLA Ops:
  0.7 1.0 %dynamic-slice_bitcast_fusion.6 = bf16[128,768]{1,0:T(8,128)(2,1)S(1)} fusion(bf16[1,1,8,128,768]{4,3,2,1,0:T(8,128)(2,1)} %param.5, s32[]{:T(128)S(6)} %select_n.30), kind=kLoop, calls=%fused_computation.7 | loop fusion | bytes 393220 | tf_op jit(solution)/shard_map/jit(dynamic_index_in_dim)/squeeze | solution.py:209
  1.7 4.0 %collective-permute-start.2 = (bf16[128,768]{1,0:T(8,128)(2,1)S(1)}, bf16[128,768]{1,0:T(8,128)(2,1)S(1)}, u32[]{:S(2)}, u32[]{:S(2)}) collective-permute-start(bf16[128,768]{1,0:T(8,128)(2,1)S(1)} %dynamic-slice_bitcast_fusion.6), channel_id=1, source_target_pairs={{0,24},{4,28},{8,16},{12,20},{16,8},{20,12},{24,0},{28,4},{1,25},{... | collective-permute-start | bytes 589832 | tf_op jit(solution)/shard_map/ppermute | solution.py:230
  5.6 1.4 %dynamic-slice_bitcast_fusion = (bf16[128,768]{1,0:T(8,128)(2,1)S(1)}, bf16[128,768]{1,0:T(8,128)(2,1)S(1)}, bf16[128,768]{1,0:T(8,128)(2,1)S(1)}, bf16[128,768]...) fusion(bf16[1,1,8,128,768]{4,3,2,1,0:T(8,128)(2,1)} %param.5, s32[]{:T(128)S(6)} %select_n.36, ...), kind=kLoop, calls=%fused_computation.1 | loop fusion | bytes 2359320 | tf_op jit(solution)/shard_map/jit(dynamic_index_in_dim)/squeeze | solution.py:209
  7.0 0.1 collective-permute-start.7
  7.1 1.1 %collective-permute-start.4 = (bf16[128,768]{1,0:T(8,128)(2,1)S(1)}, bf16[128,768]{1,0:T(8,128)(2,1)S(1)}, u32[]{:S(2)}, u32[]{:S(2)}) collective-permute-start(bf16[128,768]{1,0:T(8,128)(2,1)S(1)} %get-tuple-element.21), channel_id=1, source_target_pairs={{0,16},{4,20},{8,24},{12,28},{16,0},{20,4},{24,8},{28,12},{1,17},{... | collective-permute-start | bytes 589832 | tf_op jit(solution)/shard_map/ppermute | solution.py:230
  8.3 1.6 %collective-permute-start = (bf16[128,256]{1,0:T(8,128)(2,1)S(1)}, bf16[128,256]{1,0:T(8,128)(2,1)S(1)}, u32[]{:S(2)}, u32[]{:S(2)}) collective-permute-start(bf16[128,256]{1,0:T(8,128)(2,1)S(1)} %slice.3), channel_id=1, source_target_pairs={{0,1},{1,2},{2,3},{3,0},{4,5},{5,6},{6,7},{7,4},{8,9},{9,10},{10,1... | collective-permute-start | bytes 196616 | tf_op jit(solution)/shard_map/ppermute | solution.py:230
  9.9 2.6 %collective-permute-start.1 = (bf16[128,256]{1,0:T(8,128)(2,1)S(1)}, bf16[128,256]{1,0:T(8,128)(2,1)S(1)}, u32[]{:S(2)}, u32[]{:S(2)}) collective-permute-start(bf16[128,256]{1,0:T(8,128)(2,1)S(1)} %slice.3), channel_id=1, source_target_pairs={{0,2},{1,3},{2,0},{3,1},{4,6},{5,7},{6,4},{7,5},{8,10},{9,11},{10,... | collective-permute-start | bytes 196616 | tf_op jit(solution)/shard_map/ppermute | solution.py:230
  12.5 0.2 copy.6.order_ref
  12.7 1.8 %collective-permute-start.3 = (bf16[128,256]{1,0:T(8,128)(2,1)S(1)}, bf16[128,256]{1,0:T(8,128)(2,1)S(1)}, u32[]{:S(2)}, u32[]{:S(2)}) collective-permute-start(bf16[128,256]{1,0:T(8,128)(2,1)S(1)} %slice.3), channel_id=1, source_target_pairs={{0,3},{1,0},{2,1},{3,2},{4,7},{5,4},{6,5},{7,6},{8,11},{9,8},{10,9... | collective-permute-start | bytes 196616 | tf_op jit(solution)/shard_map/ppermute | solution.py:230
  14.5 0.4 %collective-permute-done = bf16[128,256]{1,0:T(8,128)(2,1)S(1)} collective-permute-done((bf16[128,256]{1,0:T(8,128)(2,1)S(1)}, bf16[128,256]{1,0:T(8,128)(2,1)S(1)}, u32[]{:S(2)}, u32[]{:S(2)}) %collective-permute-start) | collective-permute-done | bytes 65568 | tf_op jit(solution)/shard_map/ppermute | solution.py:230
  15.0 1.6 %collective-permute-start.6 = (bf16[128,768]{1,0:T(8,128)(2,1)S(1)}, bf16[128,768]{1,0:T(8,128)(2,1)S(1)}, u32[]{:S(2)}, u32[]{:S(2)}) collective-permute-start(bf16[128,768]{1,0:T(8,128)(2,1)S(1)} %get-tuple-element.15), channel_id=1, source_target_pairs={{0,8},{4,12},{8,0},{12,4},{16,24},{20,28},{24,16},{28,20},{1,9},{5... | collective-permute-start | bytes 589832 | tf_op jit(solution)/shard_map/ppermute | solution.py:230
  16.6 1.2 %collective-permute-done.1 = bf16[128,256]{1,0:T(8,128)(2,1)S(1)} collective-permute-done((bf16[128,256]{1,0:T(8,128)(2,1)S(1)}, bf16[128,256]{1,0:T(8,128)(2,1)S(1)}, u32[]{:S(2)}, u32[]{:S(2)}) %collective-permute-start.1) | collective-permute-done | bytes 65568 | tf_op jit(solution)/shard_map/ppermute | solution.py:230
  17.8 0.0 collective-permute-start.9
  17.8 0.0 collective-permute-done.7.refs_6_
  17.8 1.7 %collective-permute-start.8 = (bf16[128,768]{1,0:T(8,128)(2,1)S(1)}, bf16[128,768]{1,0:T(8,128)(2,1)S(1)}, u32[]{:S(2)}, u32[]{:S(2)}) collective-permute-start(bf16[128,768]{1,0:T(8,128)(2,1)S(1)} %get-tuple-element.16), channel_id=1, source_target_pairs={{0,12},{4,8},{8,4},{12,0},{16,28},{20,24},{24,20},{28,16},{1,13},{... | collective-permute-start | bytes 589832 | tf_op jit(solution)/shard_map/ppermute | solution.py:230
  19.5 0.0 collective-permute-done.4.refs_3_
  19.5 0.0 collective-permute-start.5
  19.5 0.0 copy-start
  19.5 0.0 copy-start.2
  19.6 2.0 %prefix_attention.1 = bf16[128,512]{1,0:T(8,128)(2,1)} custom-call(s32[4]{0:T(128)S(1)} %fusion.starts_ref, bf16[128,768]{1,0:T(8,128)(2,1)S(1)} %bitcast.22, bf16[512,256]{1,0:T(8,128)(2,1)S(1)} %pad_maximum_fusion.kv_ref.prefix_ref), custom_call_target="tpu_custom_call" | custom-call | flops 1000000000 | bytes 1000000 | tf_op jit(solution)/shard_map/prefix_attention/pallas_call | solution.py:120
  21.6 0.7 %collective-permute-done.6.refs_1_ = bf16[128,768]{1,0:T(8,128)(2,1)S(1)} collective-permute-done((bf16[128,768]{1,0:T(8,128)(2,1)S(1)}, bf16[128,768]{1,0:T(8,128)(2,1)S(1)}, u32[]{:S(2)}, u32[]{:S(2)}) %collective-permute-start.6) | collective-permute-done | bytes 196640 | tf_op jit(solution)/shard_map/ppermute | solution.py:230
  22.2 2.6 %collective-permute-done.9.refs_4_ = bf16[128,768]{1,0:T(8,128)(2,1)S(1)} collective-permute-done((bf16[128,768]{1,0:T(8,128)(2,1)S(1)}, bf16[128,768]{1,0:T(8,128)(2,1)S(1)}, u32[]{:S(2)}, u32[]{:S(2)}) %collective-permute-start.9) | collective-permute-done | bytes 196640 | tf_op jit(solution)/shard_map/ppermute | solution.py:230
  24.8 0.2 collective-permute-done.8.refs_2_
  25.1 7.8 %response_attention.1 = bf16[2,512,512]{2,1,0:T(8,128)(2,1)} custom-call(s32[2]{0:T(128)S(1)} %bitcast.23, s32[1024,1]{1,0:T(8,128)S(1)} %copy.6.order_ref, bf16[8,128,768]{2,1,0:T(8,128)(2,1)S(1)} %bitcast.20, bf16[512,256]{1,0:T(8,128)(2,1)S(1)} %pad_maximum_fusion.kv_ref.prefix_ref, bf16[128,768]{1,0:T(8,128)(2,1)S(1)} %collective-permute-done.5.refs_0_, ...), custom_call_target="tpu_custom_call" | custom-call | flops 5000000000 | bytes 4000000 | tf_op jit(solution)/shard_map/response_attention/pallas_call | solution.py:178
  (12 shorter events, 0.1 us)
Async XLA Ops:
  0.6 7.6 %copy-start.1 = (bf16[1,128,768]{2,1,0:T(8,128)(2,1)S(1)}, bf16[1,128,768]{2,1,0:T(8,128)(2,1)}, u32[]{:S(2)}) copy-start(bf16[1,128,768]{2,1,0:T(8,128)(2,1)} %param.4) | copy-start | bytes 589828
  0.6 11.8 %copy-start.3 = (s32[1,1,1024]{2,1,0:T(1,128)S(1)}, s32[1,1,1024]{2,1,0:T(1,128)}, u32[]{:S(2)}) copy-start(s32[1,1,1024]{2,1,0:T(1,128)} %param.6) | copy-start | bytes 12292
  1.7 11.1 %collective-permute-start.2 = (bf16[128,768]{1,0:T(8,128)(2,1)S(1)}, bf16[128,768]{1,0:T(8,128)(2,1)S(1)}, u32[]{:S(2)}, u32[]{:S(2)}) collective-permute-start(bf16[128,768]{1,0:T(8,128)(2,1)S(1)} %dynamic-slice_bitcast_fusion.6), channel_id=1, source_target_pairs={{0,24},{4,28},{8,16},{12,20},{16,8},{20,12},{24,0},{28,4},{1,25},{... | collective-permute-start | bytes 589832 | tf_op jit(solution)/shard_map/ppermute | solution.py:230
  7.0 10.8 %collective-permute-start.7 = (bf16[128,768]{1,0:T(8,128)(2,1)S(1)}, bf16[128,768]{1,0:T(8,128)(2,1)S(1)}, u32[]{:S(2)}, u32[]{:S(2)}) collective-permute-start(bf16[128,768]{1,0:T(8,128)(2,1)S(1)} %get-tuple-element.23), channel_id=1, source_target_pairs={{0,28},{4,24},{8,20},{12,16},{16,12},{20,8},{24,4},{28,0},{1,29},{... | collective-permute-start | bytes 589832 | tf_op jit(solution)/shard_map/ppermute | solution.py:230
  7.1 12.4 %collective-permute-start.4 = (bf16[128,768]{1,0:T(8,128)(2,1)S(1)}, bf16[128,768]{1,0:T(8,128)(2,1)S(1)}, u32[]{:S(2)}, u32[]{:S(2)}) collective-permute-start(bf16[128,768]{1,0:T(8,128)(2,1)S(1)} %get-tuple-element.21), channel_id=1, source_target_pairs={{0,16},{4,20},{8,24},{12,28},{16,0},{20,4},{24,8},{28,12},{1,17},{... | collective-permute-start | bytes 589832 | tf_op jit(solution)/shard_map/ppermute | solution.py:230
  8.3 6.7 %collective-permute-start = (bf16[128,256]{1,0:T(8,128)(2,1)S(1)}, bf16[128,256]{1,0:T(8,128)(2,1)S(1)}, u32[]{:S(2)}, u32[]{:S(2)}) collective-permute-start(bf16[128,256]{1,0:T(8,128)(2,1)S(1)} %slice.3), channel_id=1, source_target_pairs={{0,1},{1,2},{2,3},{3,0},{4,5},{5,6},{6,7},{7,4},{8,9},{9,10},{10,1... | collective-permute-start | bytes 196616 | tf_op jit(solution)/shard_map/ppermute | solution.py:230
  9.9 7.9 %collective-permute-start.1 = (bf16[128,256]{1,0:T(8,128)(2,1)S(1)}, bf16[128,256]{1,0:T(8,128)(2,1)S(1)}, u32[]{:S(2)}, u32[]{:S(2)}) collective-permute-start(bf16[128,256]{1,0:T(8,128)(2,1)S(1)} %slice.3), channel_id=1, source_target_pairs={{0,2},{1,3},{2,0},{3,1},{4,6},{5,7},{6,4},{7,5},{8,10},{9,11},{10,... | collective-permute-start | bytes 196616 | tf_op jit(solution)/shard_map/ppermute | solution.py:230
  12.7 6.8 %collective-permute-start.3 = (bf16[128,256]{1,0:T(8,128)(2,1)S(1)}, bf16[128,256]{1,0:T(8,128)(2,1)S(1)}, u32[]{:S(2)}, u32[]{:S(2)}) collective-permute-start(bf16[128,256]{1,0:T(8,128)(2,1)S(1)} %slice.3), channel_id=1, source_target_pairs={{0,3},{1,0},{2,1},{3,2},{4,7},{5,4},{6,5},{7,6},{8,11},{9,8},{10,9... | collective-permute-start | bytes 196616 | tf_op jit(solution)/shard_map/ppermute | solution.py:230
  15.0 7.3 %collective-permute-start.6 = (bf16[128,768]{1,0:T(8,128)(2,1)S(1)}, bf16[128,768]{1,0:T(8,128)(2,1)S(1)}, u32[]{:S(2)}, u32[]{:S(2)}) collective-permute-start(bf16[128,768]{1,0:T(8,128)(2,1)S(1)} %get-tuple-element.15), channel_id=1, source_target_pairs={{0,8},{4,12},{8,0},{12,4},{16,24},{20,28},{24,16},{28,20},{1,9},{5... | collective-permute-start | bytes 589832 | tf_op jit(solution)/shard_map/ppermute | solution.py:230
  17.8 7.1 %collective-permute-start.9 = (bf16[128,768]{1,0:T(8,128)(2,1)S(1)}, bf16[128,768]{1,0:T(8,128)(2,1)S(1)}, u32[]{:S(2)}, u32[]{:S(2)}) collective-permute-start(bf16[128,768]{1,0:T(8,128)(2,1)S(1)} %get-tuple-element.17), channel_id=1, source_target_pairs={{0,20},{4,16},{8,28},{12,24},{16,4},{20,0},{24,12},{28,8},{1,21},{... | collective-permute-start | bytes 589832 | tf_op jit(solution)/shard_map/ppermute | solution.py:230
  17.8 7.3 %collective-permute-start.8 = (bf16[128,768]{1,0:T(8,128)(2,1)S(1)}, bf16[128,768]{1,0:T(8,128)(2,1)S(1)}, u32[]{:S(2)}, u32[]{:S(2)}) collective-permute-start(bf16[128,768]{1,0:T(8,128)(2,1)S(1)} %get-tuple-element.16), channel_id=1, source_target_pairs={{0,12},{4,8},{8,4},{12,0},{16,28},{20,24},{24,20},{28,16},{1,13},{... | collective-permute-start | bytes 589832 | tf_op jit(solution)/shard_map/ppermute | solution.py:230
  19.5 5.6 %collective-permute-start.5 = (bf16[128,768]{1,0:T(8,128)(2,1)S(1)}, bf16[128,768]{1,0:T(8,128)(2,1)S(1)}, u32[]{:S(2)}, u32[]{:S(2)}) collective-permute-start(bf16[128,768]{1,0:T(8,128)(2,1)S(1)} %get-tuple-element.14), channel_id=1, source_target_pairs={{0,4},{4,0},{8,12},{12,8},{16,20},{20,16},{24,28},{28,24},{1,5},{5... | collective-permute-start | bytes 589832 | tf_op jit(solution)/shard_map/ppermute | solution.py:230
  19.5 5.5 %copy-start = (bf16[1,1,8,128,768]{4,3,2,1,0:T(8,128)(2,1)S(1)}, bf16[1,1,8,128,768]{4,3,2,1,0:T(8,128)(2,1)}, u32[]{:S(2)}) copy-start(bf16[1,1,8,128,768]{4,3,2,1,0:T(8,128)(2,1)} %param.5) | copy-start | bytes 4718596
  19.5 5.5 %copy-start.2 = (s32[1,2]{1,0:T(1,128)S(1)}, s32[1,2]{1,0:T(1,128)}, u32[]{:S(2)}) copy-start(s32[1,2]{1,0:T(1,128)} %param.7) | copy-start | bytes 28

commit v4 on v3

--- a/solution.py
+++ b/solution.py
@@ -205,30 +205,50 @@
     def after(value, *done):
         return lax.optimization_barrier((value, *done))[0]
 
-    def pick(index, k):
+    chips = range(1, peers // 2)
+    near = [2 * m for m in chips if m.bit_count() == 1]
+    far = [2 * m for m in chips if m.bit_count() > 1]
+    pairs = [("pair", k) for k in far]
+    evens = [("one", k) for k in near]
+    odds = [("one", k + 1) for k in near]
+    shifts = [("ctx", t) for t in range(1, ctx_count)]
+    plan = pairs[:1] + evens[:2] + shifts[:2] + shifts[2:] + odds + evens[2:] + pairs[1:]
+    plan += [("one", 1)] if peers > 1 else []
+    freed = plan[3:5] + plan[:1] * 2 + plan[1:3] + plan[5:]
+
+    def pick(index, step):
+        kind, k = step
+        if kind == "pair":
+            return lax.dynamic_slice_in_dim(sent, (index ^ k) & -2, 2, 0)
         return lax.dynamic_index_in_dim(sent, index ^ k, 0, keepdims=False)
 
-    ks = sorted(range(1, peers), key=lambda k: (-(k >> 1).bit_count(), k & 1, -k))
-    first = pick(lax.axis_index("prompt"), ks[0])
-    index, rows, first = lax.optimization_barrier((lax.axis_index("prompt"), prefix_rows, first))
-    picked = {k: pick(index, k) for k in ks[1:]}
-    picked[ks[0]] = first
+    own_index = lax.axis_index("prompt")
+    core = own_index & 1
+    swaps = [step for step in plan if step[0] != "ctx"]
+    lead = pick(own_index, swaps[0])
+    index, rows, lead = lax.optimization_barrier((own_index, prefix_rows, lead))
+    picked = {step: pick(index, step) for step in swaps[1:]}
+    picked[swaps[0]] = lead
     prefix_kv = rows[:, feat - 2 * HEAD :]
 
-    swaps = [("prompt", k) for k in ks]
-    shifts = [("ctx", t) for t in range(1, ctx_count)]
-    plan = swaps[:3] + shifts[:2] + swaps[3:5] + shifts[2:] + swaps[5:]
-    freed = plan[3:5] + plan[:3] + plan[5:]
-    got = {}
-    for n, (axis, by) in enumerate(plan):
-        if axis == "ctx":
-            value, pairs = prefix_kv, [(j, (j + by) % ctx_count) for j in range(ctx_count)]
+    got, blocks = {}, {}
+    for n, step in enumerate(plan):
+        kind, by = step
+        if kind == "ctx":
+            value, route = prefix_kv, [(j, (j + by) % ctx_count) for j in range(ctx_count)]
         else:
-            value, pairs = picked[by], [(j, j ^ by) for j in range(peers)]
+            value, route = picked[step], [(j, j ^ by) for j in range(peers)]
         if n >= 5:
             value = after(value, got[freed[n - 5]])
-        got[axis, by] = lax.ppermute(value, axis, pairs)
-    blocks = [got["prompt", k] for k in range(1, peers)]
+        got[step] = lax.ppermute(value, "ctx" if kind == "ctx" else "prompt", route)
+        if kind == "one":
+            blocks[by] = got[step]
+    for _, k in pairs:
+        came = got["pair", k]
+        blocks[k] = lax.dynamic_index_in_dim(came, core, 0, keepdims=False)
+        other = lax.dynamic_index_in_dim(came, 1 - core, 0, keepdims=False)
+        blocks[k + 1] = lax.ppermute(other, "prompt", [(j, j ^ 1) for j in range(peers)])
+    blocks = [blocks[k] for k in range(1, peers)]
     prefix_kv = jnp.concatenate([prefix_kv] + [got[s] for s in shifts], axis=0)
 
     order = arrival_order[0, 0].reshape(-1, 1)

time: 33.1 us -> 31.2 us (0.943)
  starting transfers between devices: 14.5 us -> 12.3 us
  local copies, waits for them, and re-layouts: 2.65 us -> 3.51 us
  waiting for transfers between devices: 5.11 us -> 4.52 us
    ppermute x10, starting transfers between devices: 14.5 us -> 12.3 us  [the longest x9 12.3 us: body(): got[step] = lax.ppermute(value, 'ctx' if kind == 'ctx' else 'prompt', route)]
    squeeze x2 -> x1, local copies, waits for them, and re-layouts: 2.41 us -> 1.37 us  [pick(): return lax.dynamic_index_in_dim(sent, index ^ k, 0, keepdims=False)]
    dynamic_slice x0 -> x1, local copies, waits for them, and re-layouts: none -> 1.03 us  [pick(): return lax.dynamic_slice_in_dim(sent, (index ^ k) & -2, 2, 0)]
    slice x1, local copies, waits for them, and re-layouts: 0.01 us -> 0.84 us  [body(): prefix_kv = rows[:, feat - 2 * HEAD:]]
    ppermute x10, waiting for transfers between devices: 5.11 us -> 4.52 us  [the longest x9 4.52 us: body(): got[step] = lax.ppermute(value, 'ctx' if kind == 'ctx' else 'prompt', route)]
  transfers between devices with their start and end apart: 10 -> 10, of which waited for: 5 -> 4; matrix products, arithmetic and copies ran while one was open for 5% -> 8% of each run, Pallas kernels for 6% -> 6%
where the time goes in v4:
time: 31.2 us; the launch traced here: 31 us
  starting transfers between devices  12.3 us (39%)
  Pallas kernels  9.83 us (32%)
  waiting for transfers between devices  4.52 us (14%)
  local copies, waits for them, and re-layouts  3.51 us (11%)
  between operations  0.74 us (2%)
    ppermute x9, starting transfers between devices, body(): got[step] = lax.ppermute(value, 'ctx' if kind == 'ctx' else 'prompt', route)  12.3 us
    pallas_call x1, Pallas kernels, response_call(): pl.pallas_call(response_kernel, out_shape=jax.ShapeDtypeStruct((responses...  7.82 us
    ppermute x9, waiting for transfers between devices, body(): got[step] = lax.ppermute(value, 'ctx' if kind == 'ctx' else 'prompt', route)  4.52 us
    pallas_call x1, Pallas kernels, prefix_call(): pl.pallas_call(prefix_kernel, out_shape=jax.ShapeDtypeStruct((rows.shape[...  2.01 us
    squeeze x1, local copies, waits for them, and re-layouts, pick(): return lax.dynamic_index_in_dim(sent, index ^ k, 0, keepdims=False)  1.37 us
    dynamic_slice x1, local copies, waits for them, and re-layouts, pick(): return lax.dynamic_slice_in_dim(sent, (index ^ k) & -2, 2, 0)  1.03 us
    slice x1, local copies, waits for them, and re-layouts, body(): prefix_kv = rows[:, feat - 2 * HEAD:]  0.84 us
  transfers between devices with their start and end apart: 10, of which 4 were waited for; matrix products, arithmetic and copies ran while one was open for 8% of the time, Pallas kernels for 6%

profile of v4, /device:TPU:0, one launch (start us, length us, event | category | flops | bytes accessed | tf_op | source)
XLA Modules:
  0.0 31.0 jit_solution(10541757992470862922)
XLA Ops:
  0.7 1.0 %dynamic-slice_bitcast_fusion = bf16[2,128,768]{2,1,0:T(8,128)(2,1)S(1)} fusion(bf16[1,1,8,128,768]{4,3,2,1,0:T(8,128)(2,1)} %param.5, s32[]{:T(128)S(6)} %select_n.34), kind=kLoop, calls=%fused_computation | loop fusion | bytes 786436 | tf_op jit(solution)/shard_map/dynamic_slice | solution.py:222
  1.7 4.0 %collective-permute-start.3 = (bf16[2,128,768]{2,1,0:T(8,128)(2,1)S(1)}, bf16[2,128,768]{2,1,0:T(8,128)(2,1)S(1)}, u32[]{:S(2)}, u32[]{:S(2)}) collective-permute-start(bf16[2,128,768]{2,1,0:T(8,128)(2,1)S(1)} %dynamic-slice_bitcast_fusion), channel_id=1, source_target_pairs={{0,24},{4,28},{8,16},{12,20},{16,8},{20,12},{24,0},{28,4},{1,25},{... | collective-permute-start | bytes 1179656 | tf_op jit(solution)/shard_map/ppermute | solution.py:243
  5.6 0.8 %slice.3 = bf16[128,256]{1,0:T(8,128)(2,1)S(1)} slice(bf16[128,768]{1,0:T(8,128)(2,1)} %bitcast.23), slice={[0:128], [512:768]} | slice | bytes 131072 | tf_op jit(solution)/shard_map/slice | solution.py:232
  6.5 2.6 %collective-permute-start.1 = (bf16[128,256]{1,0:T(8,128)(2,1)S(1)}, bf16[128,256]{1,0:T(8,128)(2,1)S(1)}, u32[]{:S(2)}, u32[]{:S(2)}) collective-permute-start(bf16[128,256]{1,0:T(8,128)(2,1)S(1)} %slice.3), channel_id=1, source_target_pairs={{0,2},{1,3},{2,0},{3,1},{4,6},{5,7},{6,4},{7,5},{8,10},{9,11},{10,... | collective-permute-start | bytes 196616 | tf_op jit(solution)/shard_map/ppermute | solution.py:243
  9.1 1.6 %collective-permute-start = (bf16[128,256]{1,0:T(8,128)(2,1)S(1)}, bf16[128,256]{1,0:T(8,128)(2,1)S(1)}, u32[]{:S(2)}, u32[]{:S(2)}) collective-permute-start(bf16[128,256]{1,0:T(8,128)(2,1)S(1)} %slice.3), channel_id=1, source_target_pairs={{0,1},{1,2},{2,3},{3,0},{4,5},{5,6},{6,7},{7,4},{8,9},{9,10},{10,1... | collective-permute-start | bytes 196616 | tf_op jit(solution)/shard_map/ppermute | solution.py:243
  10.7 1.4 %dynamic-slice_bitcast_fusion.3 = (bf16[128,768]{1,0:T(8,128)(2,1)S(1)}, bf16[128,768]{1,0:T(8,128)(2,1)S(1)}, bf16[128,768]{1,0:T(8,128)(2,1)S(1)}, bf16[128,768]{1,0:T(8,128)(2,1)S(1)}, bf16[128,768]{1,0:T(8,128)(2,1)S(1)}) fusion(bf16[1,1,8,128,768]{4,3,2,1,0:T(8,128)(2,1)} %param.5, s32[]{:T(128)S(6)} %select_n.39, s32[]{:T(128)S(6)} %select_n.37, ...), kind=kLoop, calls=%fused_computation.4 | loop fusion | bytes 1966100 | tf_op jit(solution)/shard_map/jit(dynamic_index_in_dim)/squeeze | solution.py:223
  12.0 0.6 %collective-permute-start.5 = (bf16[128,768]{1,0:T(8,128)(2,1)S(1)}, bf16[128,768]{1,0:T(8,128)(2,1)S(1)}, u32[]{:S(2)}, u32[]{:S(2)}) collective-permute-start(bf16[128,768]{1,0:T(8,128)(2,1)S(1)} %get-tuple-element.18), channel_id=1, source_target_pairs={{0,8},{4,12},{8,0},{12,4},{16,24},{20,28},{24,16},{28,20},{1,9},{5... | collective-permute-start | bytes 589832 | tf_op jit(solution)/shard_map/ppermute | solution.py:243
  12.6 0.5 %collective-permute-start.7 = (bf16[128,768]{1,0:T(8,128)(2,1)S(1)}, bf16[128,768]{1,0:T(8,128)(2,1)S(1)}, u32[]{:S(2)}, u32[]{:S(2)}) collective-permute-start(bf16[128,768]{1,0:T(8,128)(2,1)S(1)} %get-tuple-element.20), channel_id=1, source_target_pairs={{0,16},{4,20},{8,24},{12,28},{16,0},{20,4},{24,8},{28,12},{1,17},{... | collective-permute-start | bytes 589832 | tf_op jit(solution)/shard_map/ppermute | solution.py:243
  13.1 0.2 copy.6.order_ref
  13.4 0.1 collective-permute-start.6
  13.5 1.7 %collective-permute-done = bf16[128,256]{1,0:T(8,128)(2,1)S(1)} collective-permute-done((bf16[128,256]{1,0:T(8,128)(2,1)S(1)}, bf16[128,256]{1,0:T(8,128)(2,1)S(1)}, u32[]{:S(2)}, u32[]{:S(2)}) %collective-permute-start) | collective-permute-done | bytes 65568 | tf_op jit(solution)/shard_map/ppermute | solution.py:243
  15.1 1.4 %collective-permute-start.2 = (bf16[128,256]{1,0:T(8,128)(2,1)S(1)}, bf16[128,256]{1,0:T(8,128)(2,1)S(1)}, u32[]{:S(2)}, u32[]{:S(2)}) collective-permute-start(bf16[128,256]{1,0:T(8,128)(2,1)S(1)} %slice.3), channel_id=1, source_target_pairs={{0,3},{1,0},{2,1},{3,2},{4,7},{5,4},{6,5},{7,6},{8,11},{9,8},{10,9... | collective-permute-start | bytes 196616 | tf_op jit(solution)/shard_map/ppermute | solution.py:243
  16.5 0.0 collective-permute-done.3
  16.5 1.6 %collective-permute-start.8 = (bf16[128,768]{1,0:T(8,128)(2,1)S(1)}, bf16[128,768]{1,0:T(8,128)(2,1)S(1)}, u32[]{:S(2)}, u32[]{:S(2)}) collective-permute-start(bf16[128,768]{1,0:T(8,128)(2,1)S(1)} %get-tuple-element.15), channel_id=1, source_target_pairs={{0,20},{4,16},{8,28},{12,24},{16,4},{20,0},{24,12},{28,8},{1,21},{... | collective-permute-start | bytes 589832 | tf_op jit(solution)/shard_map/ppermute | solution.py:243
  18.2 1.2 %collective-permute-done.2 = bf16[128,256]{1,0:T(8,128)(2,1)S(1)} collective-permute-done((bf16[128,256]{1,0:T(8,128)(2,1)S(1)}, bf16[128,256]{1,0:T(8,128)(2,1)S(1)}, u32[]{:S(2)}, u32[]{:S(2)}) %collective-permute-start.2) | collective-permute-done | bytes 65568 | tf_op jit(solution)/shard_map/ppermute | solution.py:243
  19.4 0.0 collective-permute-start.4
  19.4 1.0 %collective-permute-done.5.refs_1_ = bf16[128,768]{1,0:T(8,128)(2,1)S(1)} collective-permute-done((bf16[128,768]{1,0:T(8,128)(2,1)S(1)}, bf16[128,768]{1,0:T(8,128)(2,1)S(1)}, u32[]{:S(2)}, u32[]{:S(2)}) %collective-permute-start.5) | collective-permute-done | bytes 196640 | tf_op jit(solution)/shard_map/ppermute | solution.py:243
  20.4 0.0 collective-permute-start.9
  20.4 0.0 copy-start
  20.4 0.0 copy-start.2
  20.4 2.0 %prefix_attention.1 = bf16[128,512]{1,0:T(8,128)(2,1)} custom-call(s32[4]{0:T(128)S(1)} %fusion.starts_ref, bf16[128,768]{1,0:T(8,128)(2,1)S(1)} %bitcast.24, bf16[512,256]{1,0:T(8,128)(2,1)S(1)} %pad_maximum_fusion.kv_ref.prefix_ref), custom_call_target="tpu_custom_call" | custom-call | flops 1000000000 | bytes 1000000 | tf_op jit(solution)/shard_map/prefix_attention/pallas_call | solution.py:120
  22.4 0.0 collective-permute-done.6.refs_2_
  22.4 0.7 %collective-permute-done.8.refs_4_ = bf16[128,768]{1,0:T(8,128)(2,1)S(1)} collective-permute-done((bf16[128,768]{1,0:T(8,128)(2,1)S(1)}, bf16[128,768]{1,0:T(8,128)(2,1)S(1)}, u32[]{:S(2)}, u32[]{:S(2)}) %collective-permute-start.8) | collective-permute-done | bytes 196640 | tf_op jit(solution)/shard_map/ppermute | solution.py:243
  23.1 7.8 %response_attention.1 = bf16[2,512,512]{2,1,0:T(8,128)(2,1)} custom-call(s32[2]{0:T(128)S(1)} %bitcast.25, s32[1024,1]{1,0:T(8,128)S(1)} %copy.6.order_ref, bf16[8,128,768]{2,1,0:T(8,128)(2,1)S(1)} %bitcast.22, bf16[512,256]{1,0:T(8,128)(2,1)S(1)} %pad_maximum_fusion.kv_ref.prefix_ref, bf16[128,768]{1,0:T(8,128)(2,1)S(1)} %collective-permute-done.4.refs_0_, ...), custom_call_target="tpu_custom_call" | custom-call | flops 5000000000 | bytes 4000000 | tf_op jit(solution)/shard_map/response_attention/pallas_call | solution.py:178
  (13 shorter events, 0.1 us)
Async XLA Ops:
  0.6 12.5 %copy-start.3 = (s32[1,1,1024]{2,1,0:T(1,128)S(1)}, s32[1,1,1024]{2,1,0:T(1,128)}, u32[]{:S(2)}) copy-start(s32[1,1,1024]{2,1,0:T(1,128)} %param.6) | copy-start | bytes 12292
  1.7 14.9 %collective-permute-start.3 = (bf16[2,128,768]{2,1,0:T(8,128)(2,1)S(1)}, bf16[2,128,768]{2,1,0:T(8,128)(2,1)S(1)}, u32[]{:S(2)}, u32[]{:S(2)}) collective-permute-start(bf16[2,128,768]{2,1,0:T(8,128)(2,1)S(1)} %dynamic-slice_bitcast_fusion), channel_id=1, source_target_pairs={{0,24},{4,28},{8,16},{12,20},{16,8},{20,12},{24,0},{28,4},{1,25},{... | collective-permute-start | bytes 1179656 | tf_op jit(solution)/shard_map/ppermute | solution.py:243
  6.5 6.9 %collective-permute-start.1 = (bf16[128,256]{1,0:T(8,128)(2,1)S(1)}, bf16[128,256]{1,0:T(8,128)(2,1)S(1)}, u32[]{:S(2)}, u32[]{:S(2)}) collective-permute-start(bf16[128,256]{1,0:T(8,128)(2,1)S(1)} %slice.3), channel_id=1, source_target_pairs={{0,2},{1,3},{2,0},{3,1},{4,6},{5,7},{6,4},{7,5},{8,10},{9,11},{10,... | collective-permute-start | bytes 196616 | tf_op jit(solution)/shard_map/ppermute | solution.py:243
  9.1 6.1 %collective-permute-start = (bf16[128,256]{1,0:T(8,128)(2,1)S(1)}, bf16[128,256]{1,0:T(8,128)(2,1)S(1)}, u32[]{:S(2)}, u32[]{:S(2)}) collective-permute-start(bf16[128,256]{1,0:T(8,128)(2,1)S(1)} %slice.3), channel_id=1, source_target_pairs={{0,1},{1,2},{2,3},{3,0},{4,5},{5,6},{6,7},{7,4},{8,9},{9,10},{10,1... | collective-permute-start | bytes 196616 | tf_op jit(solution)/shard_map/ppermute | solution.py:243
  10.7 9.7 %copy-start.1 = (bf16[1,128,768]{2,1,0:T(8,128)(2,1)S(1)}, bf16[1,128,768]{2,1,0:T(8,128)(2,1)}, u32[]{:S(2)}) copy-start(bf16[1,128,768]{2,1,0:T(8,128)(2,1)} %param.4) | copy-start | bytes 589828
  12.0 8.3 %collective-permute-start.5 = (bf16[128,768]{1,0:T(8,128)(2,1)S(1)}, bf16[128,768]{1,0:T(8,128)(2,1)S(1)}, u32[]{:S(2)}, u32[]{:S(2)}) collective-permute-start(bf16[128,768]{1,0:T(8,128)(2,1)S(1)} %get-tuple-element.18), channel_id=1, source_target_pairs={{0,8},{4,12},{8,0},{12,4},{16,24},{20,28},{24,16},{28,20},{1,9},{5... | collective-permute-start | bytes 589832 | tf_op jit(solution)/shard_map/ppermute | solution.py:243
  12.6 9.8 %collective-permute-start.7 = (bf16[128,768]{1,0:T(8,128)(2,1)S(1)}, bf16[128,768]{1,0:T(8,128)(2,1)S(1)}, u32[]{:S(2)}, u32[]{:S(2)}) collective-permute-start(bf16[128,768]{1,0:T(8,128)(2,1)S(1)} %get-tuple-element.20), channel_id=1, source_target_pairs={{0,16},{4,20},{8,24},{12,28},{16,0},{20,4},{24,8},{28,12},{1,17},{... | collective-permute-start | bytes 589832 | tf_op jit(solution)/shard_map/ppermute | solution.py:243
  13.4 9.0 %collective-permute-start.6 = (bf16[128,768]{1,0:T(8,128)(2,1)S(1)}, bf16[128,768]{1,0:T(8,128)(2,1)S(1)}, u32[]{:S(2)}, u32[]{:S(2)}) collective-permute-start(bf16[128,768]{1,0:T(8,128)(2,1)S(1)} %get-tuple-element.14), channel_id=1, source_target_pairs={{0,12},{4,8},{8,4},{12,0},{16,28},{20,24},{24,20},{28,16},{1,13},{... | collective-permute-start | bytes 589832 | tf_op jit(solution)/shard_map/ppermute | solution.py:243
  15.1 4.3 %collective-permute-start.2 = (bf16[128,256]{1,0:T(8,128)(2,1)S(1)}, bf16[128,256]{1,0:T(8,128)(2,1)S(1)}, u32[]{:S(2)}, u32[]{:S(2)}) collective-permute-start(bf16[128,256]{1,0:T(8,128)(2,1)S(1)} %slice.3), channel_id=1, source_target_pairs={{0,3},{1,0},{2,1},{3,2},{4,7},{5,4},{6,5},{7,6},{8,11},{9,8},{10,9... | collective-permute-start | bytes 196616 | tf_op jit(solution)/shard_map/ppermute | solution.py:243
  16.5 6.6 %collective-permute-start.8 = (bf16[128,768]{1,0:T(8,128)(2,1)S(1)}, bf16[128,768]{1,0:T(8,128)(2,1)S(1)}, u32[]{:S(2)}, u32[]{:S(2)}) collective-permute-start(bf16[128,768]{1,0:T(8,128)(2,1)S(1)} %get-tuple-element.15), channel_id=1, source_target_pairs={{0,20},{4,16},{8,28},{12,24},{16,4},{20,0},{24,12},{28,8},{1,21},{... | collective-permute-start | bytes 589832 | tf_op jit(solution)/shard_map/ppermute | solution.py:243
  19.4 3.7 %collective-permute-start.4 = (bf16[128,768]{1,0:T(8,128)(2,1)S(1)}, bf16[128,768]{1,0:T(8,128)(2,1)S(1)}, u32[]{:S(2)}, u32[]{:S(2)}) collective-permute-start(bf16[128,768]{1,0:T(8,128)(2,1)S(1)} %get-tuple-element.13), channel_id=1, source_target_pairs={{0,4},{4,0},{8,12},{12,8},{16,20},{20,16},{24,28},{28,24},{1,5},{5... | collective-permute-start | bytes 589832 | tf_op jit(solution)/shard_map/ppermute | solution.py:243
  20.4 2.8 %collective-permute-start.9 = (bf16[128,768]{1,0:T(8,128)(2,1)S(1)}, bf16[128,768]{1,0:T(8,128)(2,1)S(1)}, u32[]{:S(2)}, u32[]{:S(2)}) collective-permute-start(bf16[128,768]{1,0:T(8,128)(2,1)S(1)} %get-tuple-element.21), channel_id=1, source_target_pairs={{0,4},{4,0},{8,12},{12,8},{16,20},{20,16},{24,28},{28,24},{1,5},{5... | collective-permute-start | bytes 589832 | tf_op jit(solution)/shard_map/ppermute | solution.py:250
  20.4 2.7 %copy-start = (bf16[1,1,8,128,768]{4,3,2,1,0:T(8,128)(2,1)S(1)}, bf16[1,1,8,128,768]{4,3,2,1,0:T(8,128)(2,1)}, u32[]{:S(2)}) copy-start(bf16[1,1,8,128,768]{4,3,2,1,0:T(8,128)(2,1)} %param.5) | copy-start | bytes 4718596
  20.4 2.7 %copy-start.2 = (s32[1,2]{1,0:T(1,128)S(1)}, s32[1,2]{1,0:T(1,128)}, u32[]{:S(2)}) copy-start(s32[1,2]{1,0:T(1,128)} %param.7) | copy-start | bytes 28

commit v5 on v4

--- a/solution.py
+++ b/solution.py
@@ -211,7 +211,8 @@
     pairs = [("pair", k) for k in far]
     evens = [("one", k) for k in near]
     odds = [("one", k + 1) for k in near]
-    shifts = [("ctx", t) for t in range(1, ctx_count)]
+    turns = sorted(range(1, ctx_count), key=lambda t: -min(t, ctx_count - t))
+    shifts = [("ctx", t) for t in turns]
     plan = pairs[:1] + evens[:2] + shifts[:2] + shifts[2:] + odds + evens[2:] + pairs[1:]
     plan += [("one", 1)] if peers > 1 else []
     freed = plan[3:5] + plan[:1] * 2 + plan[1:3] + plan[5:]
@@ -249,7 +250,7 @@
         other = lax.dynamic_index_in_dim(came, 1 - core, 0, keepdims=False)
         blocks[k + 1] = lax.ppermute(other, "prompt", [(j, j ^ 1) for j in range(peers)])
     blocks = [blocks[k] for k in range(1, peers)]
-    prefix_kv = jnp.concatenate([prefix_kv] + [got[s] for s in shifts], axis=0)
+    prefix_kv = jnp.concatenate([prefix_kv] + [got["ctx", t] for t in range(1, ctx_count)], axis=0)
 
     order = arrival_order[0, 0].reshape(-1, 1)
     starts = (ctx_index - jnp.arange(ctx_count, dtype=jnp.int32)) % ctx_count * prefix_len

time: 31.2 us -> 30.9 us (level)
  starting transfers between devices: 12.3 us -> 11.9 us
    ppermute x9, starting transfers between devices: 12.3 us -> 11.9 us  [body(): got[step] = lax.ppermute(value, 'ctx' if kind == 'ctx' else 'prompt', route)]
  transfers between devices with their start and end apart: 10 -> 10, of which waited for: 4 -> 4; matrix products, arithmetic and copies ran while one was open for 8% -> 8% of each run, Pallas kernels for 6% -> 7%
where the time goes in v5:
time: 30.9 us; the launch traced here: 30.7 us
  starting transfers between devices  11.9 us (39%)
  Pallas kernels  9.83 us (32%)
  waiting for transfers between devices  4.72 us (15%)
  local copies, waits for them, and re-layouts  3.51 us (11%)
  between operations  0.74 us (2%)
    ppermute x9, starting transfers between devices, body(): got[step] = lax.ppermute(value, 'ctx' if kind == 'ctx' else 'prompt', route)  11.9 us
    pallas_call x1, Pallas kernels, response_call(): pl.pallas_call(response_kernel, out_shape=jax.ShapeDtypeStruct((responses...  7.82 us
    ppermute x9, waiting for transfers between devices, body(): got[step] = lax.ppermute(value, 'ctx' if kind == 'ctx' else 'prompt', route)  4.71 us
    pallas_call x1, Pallas kernels, prefix_call(): pl.pallas_call(prefix_kernel, out_shape=jax.ShapeDtypeStruct((rows.shape[...  2.01 us
    squeeze x1, local copies, waits for them, and re-layouts, pick(): return lax.dynamic_index_in_dim(sent, index ^ k, 0, keepdims=False)  1.37 us
    dynamic_slice x1, local copies, waits for them, and re-layouts, pick(): return lax.dynamic_slice_in_dim(sent, (index ^ k) & -2, 2, 0)  1.03 us
    slice x1, local copies, waits for them, and re-layouts, body(): prefix_kv = rows[:, feat - 2 * HEAD:]  0.84 us
  transfers between devices with their start and end apart: 10, of which 4 were waited for; matrix products, arithmetic and copies ran while one was open for 8% of the time, Pallas kernels for 7%

profile of v5, /device:TPU:0, one launch (start us, length us, event | category | flops | bytes accessed | tf_op | source)
XLA Modules:
  0.0 30.7 jit_solution(9759431007129976869)
XLA Ops:
  0.7 1.0 %dynamic-slice_bitcast_fusion = bf16[2,128,768]{2,1,0:T(8,128)(2,1)S(1)} fusion(bf16[1,1,8,128,768]{4,3,2,1,0:T(8,128)(2,1)} %param.5, s32[]{:T(128)S(6)} %select_n.34), kind=kLoop, calls=%fused_computation | loop fusion | bytes 786436 | tf_op jit(solution)/shard_map/dynamic_slice | solution.py:223
  1.7 4.0 %collective-permute-start.3 = (bf16[2,128,768]{2,1,0:T(8,128)(2,1)S(1)}, bf16[2,128,768]{2,1,0:T(8,128)(2,1)S(1)}, u32[]{:S(2)}, u32[]{:S(2)}) collective-permute-start(bf16[2,128,768]{2,1,0:T(8,128)(2,1)S(1)} %dynamic-slice_bitcast_fusion), channel_id=1, source_target_pairs={{0,24},{4,28},{8,16},{12,20},{16,8},{20,12},{24,0},{28,4},{1,25},{... | collective-permute-start | bytes 1179656 | tf_op jit(solution)/shard_map/ppermute | solution.py:244
  5.6 0.8 %slice.3 = bf16[128,256]{1,0:T(8,128)(2,1)S(1)} slice(bf16[128,768]{1,0:T(8,128)(2,1)} %bitcast.23), slice={[0:128], [512:768]} | slice | bytes 131072 | tf_op jit(solution)/shard_map/slice | solution.py:233
  6.5 1.6 %collective-permute-start = (bf16[128,256]{1,0:T(8,128)(2,1)S(1)}, bf16[128,256]{1,0:T(8,128)(2,1)S(1)}, u32[]{:S(2)}, u32[]{:S(2)}) collective-permute-start(bf16[128,256]{1,0:T(8,128)(2,1)S(1)} %slice.3), channel_id=1, source_target_pairs={{0,1},{1,2},{2,3},{3,0},{4,5},{5,6},{6,7},{7,4},{8,9},{9,10},{10,1... | collective-permute-start | bytes 196616 | tf_op jit(solution)/shard_map/ppermute | solution.py:244
  8.1 2.6 %collective-permute-start.1 = (bf16[128,256]{1,0:T(8,128)(2,1)S(1)}, bf16[128,256]{1,0:T(8,128)(2,1)S(1)}, u32[]{:S(2)}, u32[]{:S(2)}) collective-permute-start(bf16[128,256]{1,0:T(8,128)(2,1)S(1)} %slice.3), channel_id=1, source_target_pairs={{0,2},{1,3},{2,0},{3,1},{4,6},{5,7},{6,4},{7,5},{8,10},{9,11},{10,... | collective-permute-start | bytes 196616 | tf_op jit(solution)/shard_map/ppermute | solution.py:244
  10.7 1.4 %dynamic-slice_bitcast_fusion.3 = (bf16[128,768]{1,0:T(8,128)(2,1)S(1)}, bf16[128,768]{1,0:T(8,128)(2,1)S(1)}, bf16[128,768]{1,0:T(8,128)(2,1)S(1)}, bf16[128,768]{1,0:T(8,128)(2,1)S(1)}, bf16[128,768]{1,0:T(8,128)(2,1)S(1)}) fusion(bf16[1,1,8,128,768]{4,3,2,1,0:T(8,128)(2,1)} %param.5, s32[]{:T(128)S(6)} %select_n.39, s32[]{:T(128)S(6)} %select_n.37, ...), kind=kLoop, calls=%fused_computation.4 | loop fusion | bytes 1966100 | tf_op jit(solution)/shard_map/jit(dynamic_index_in_dim)/squeeze | solution.py:224
  12.0 0.6 %collective-permute-start.5 = (bf16[128,768]{1,0:T(8,128)(2,1)S(1)}, bf16[128,768]{1,0:T(8,128)(2,1)S(1)}, u32[]{:S(2)}, u32[]{:S(2)}) collective-permute-start(bf16[128,768]{1,0:T(8,128)(2,1)S(1)} %get-tuple-element.18), channel_id=1, source_target_pairs={{0,8},{4,12},{8,0},{12,4},{16,24},{20,28},{24,16},{28,20},{1,9},{5... | collective-permute-start | bytes 589832 | tf_op jit(solution)/shard_map/ppermute | solution.py:244
  12.6 0.5 %collective-permute-start.7 = (bf16[128,768]{1,0:T(8,128)(2,1)S(1)}, bf16[128,768]{1,0:T(8,128)(2,1)S(1)}, u32[]{:S(2)}, u32[]{:S(2)}) collective-permute-start(bf16[128,768]{1,0:T(8,128)(2,1)S(1)} %get-tuple-element.20), channel_id=1, source_target_pairs={{0,16},{4,20},{8,24},{12,28},{16,0},{20,4},{24,8},{28,12},{1,17},{... | collective-permute-start | bytes 589832 | tf_op jit(solution)/shard_map/ppermute | solution.py:244
  13.1 0.2 copy.6.order_ref
  13.4 0.0 collective-permute-done
  13.4 0.1 collective-permute-start.6
  13.5 1.2 %collective-permute-done.1 = bf16[128,256]{1,0:T(8,128)(2,1)S(1)} collective-permute-done((bf16[128,256]{1,0:T(8,128)(2,1)S(1)}, bf16[128,256]{1,0:T(8,128)(2,1)S(1)}, u32[]{:S(2)}, u32[]{:S(2)}) %collective-permute-start.1) | collective-permute-done | bytes 65568 | tf_op jit(solution)/shard_map/ppermute | solution.py:244
  14.7 1.2 %collective-permute-start.2 = (bf16[128,256]{1,0:T(8,128)(2,1)S(1)}, bf16[128,256]{1,0:T(8,128)(2,1)S(1)}, u32[]{:S(2)}, u32[]{:S(2)}) collective-permute-start(bf16[128,256]{1,0:T(8,128)(2,1)S(1)} %slice.3), channel_id=1, source_target_pairs={{0,3},{1,0},{2,1},{3,2},{4,7},{5,4},{6,5},{7,6},{8,11},{9,8},{10,9... | collective-permute-start | bytes 196616 | tf_op jit(solution)/shard_map/ppermute | solution.py:244
  15.9 1.3 %collective-permute-start.8 = (bf16[128,768]{1,0:T(8,128)(2,1)S(1)}, bf16[128,768]{1,0:T(8,128)(2,1)S(1)}, u32[]{:S(2)}, u32[]{:S(2)}) collective-permute-start(bf16[128,768]{1,0:T(8,128)(2,1)S(1)} %get-tuple-element.15), channel_id=1, source_target_pairs={{0,20},{4,16},{8,28},{12,24},{16,4},{20,0},{24,12},{28,8},{1,21},{... | collective-permute-start | bytes 589832 | tf_op jit(solution)/shard_map/ppermute | solution.py:244
  17.3 1.8 %collective-permute-done.2 = bf16[128,256]{1,0:T(8,128)(2,1)S(1)} collective-permute-done((bf16[128,256]{1,0:T(8,128)(2,1)S(1)}, bf16[128,256]{1,0:T(8,128)(2,1)S(1)}, u32[]{:S(2)}, u32[]{:S(2)}) %collective-permute-start.2) | collective-permute-done | bytes 65568 | tf_op jit(solution)/shard_map/ppermute | solution.py:244
  19.1 1.3 %collective-permute-done.5.refs_1_ = bf16[128,768]{1,0:T(8,128)(2,1)S(1)} collective-permute-done((bf16[128,768]{1,0:T(8,128)(2,1)S(1)}, bf16[128,768]{1,0:T(8,128)(2,1)S(1)}, u32[]{:S(2)}, u32[]{:S(2)}) %collective-permute-start.5) | collective-permute-done | bytes 196640 | tf_op jit(solution)/shard_map/ppermute | solution.py:244
  20.4 0.0 collective-permute-start.9
  20.4 0.0 copy-start
  20.4 0.0 copy-start.2
  20.4 2.0 %prefix_attention.1 = bf16[128,512]{1,0:T(8,128)(2,1)} custom-call(s32[4]{0:T(128)S(1)} %fusion.starts_ref, bf16[128,768]{1,0:T(8,128)(2,1)S(1)} %bitcast.24, bf16[512,256]{1,0:T(8,128)(2,1)S(1)} %pad_maximum_fusion.kv_ref.prefix_ref), custom_call_target="tpu_custom_call" | custom-call | flops 1000000000 | bytes 1000000 | tf_op jit(solution)/shard_map/prefix_attention/pallas_call | solution.py:120
  22.4 0.0 collective-permute-done.7.refs_3_
  22.4 0.0 collective-permute-done.6.refs_2_
  22.4 0.4 %collective-permute-done.8.refs_4_ = bf16[128,768]{1,0:T(8,128)(2,1)S(1)} collective-permute-done((bf16[128,768]{1,0:T(8,128)(2,1)S(1)}, bf16[128,768]{1,0:T(8,128)(2,1)S(1)}, u32[]{:S(2)}, u32[]{:S(2)}) %collective-permute-start.8) | collective-permute-done | bytes 196640 | tf_op jit(solution)/shard_map/ppermute | solution.py:244
  22.9 7.8 %response_attention.1 = bf16[2,512,512]{2,1,0:T(8,128)(2,1)} custom-call(s32[2]{0:T(128)S(1)} %bitcast.25, s32[1024,1]{1,0:T(8,128)S(1)} %copy.6.order_ref, bf16[8,128,768]{2,1,0:T(8,128)(2,1)S(1)} %bitcast.22, bf16[512,256]{1,0:T(8,128)(2,1)S(1)} %pad_maximum_fusion.kv_ref.prefix_ref, bf16[128,768]{1,0:T(8,128)(2,1)S(1)} %collective-permute-done.4.refs_0_, ...), custom_call_target="tpu_custom_call" | custom-call | flops 5000000000 | bytes 4000000 | tf_op jit(solution)/shard_map/response_attention/pallas_call | solution.py:178
  (13 shorter events, 0.1 us)
Async XLA Ops:
  0.6 12.5 %copy-start.3 = (s32[1,1,1024]{2,1,0:T(1,128)S(1)}, s32[1,1,1024]{2,1,0:T(1,128)}, u32[]{:S(2)}) copy-start(s32[1,1,1024]{2,1,0:T(1,128)} %param.6) | copy-start | bytes 12292
  1.7 14.3 %collective-permute-start.3 = (bf16[2,128,768]{2,1,0:T(8,128)(2,1)S(1)}, bf16[2,128,768]{2,1,0:T(8,128)(2,1)S(1)}, u32[]{:S(2)}, u32[]{:S(2)}) collective-permute-start(bf16[2,128,768]{2,1,0:T(8,128)(2,1)S(1)} %dynamic-slice_bitcast_fusion), channel_id=1, source_target_pairs={{0,24},{4,28},{8,16},{12,20},{16,8},{20,12},{24,0},{28,4},{1,25},{... | collective-permute-start | bytes 1179656 | tf_op jit(solution)/shard_map/ppermute | solution.py:244
  6.5 6.9 %collective-permute-start = (bf16[128,256]{1,0:T(8,128)(2,1)S(1)}, bf16[128,256]{1,0:T(8,128)(2,1)S(1)}, u32[]{:S(2)}, u32[]{:S(2)}) collective-permute-start(bf16[128,256]{1,0:T(8,128)(2,1)S(1)} %slice.3), channel_id=1, source_target_pairs={{0,1},{1,2},{2,3},{3,0},{4,5},{5,6},{6,7},{7,4},{8,9},{9,10},{10,1... | collective-permute-start | bytes 196616 | tf_op jit(solution)/shard_map/ppermute | solution.py:244
  8.1 6.6 %collective-permute-start.1 = (bf16[128,256]{1,0:T(8,128)(2,1)S(1)}, bf16[128,256]{1,0:T(8,128)(2,1)S(1)}, u32[]{:S(2)}, u32[]{:S(2)}) collective-permute-start(bf16[128,256]{1,0:T(8,128)(2,1)S(1)} %slice.3), channel_id=1, source_target_pairs={{0,2},{1,3},{2,0},{3,1},{4,6},{5,7},{6,4},{7,5},{8,10},{9,11},{10,... | collective-permute-start | bytes 196616 | tf_op jit(solution)/shard_map/ppermute | solution.py:244
  10.7 9.7 %copy-start.1 = (bf16[1,128,768]{2,1,0:T(8,128)(2,1)S(1)}, bf16[1,128,768]{2,1,0:T(8,128)(2,1)}, u32[]{:S(2)}) copy-start(bf16[1,128,768]{2,1,0:T(8,128)(2,1)} %param.4) | copy-start | bytes 589828
  12.0 8.3 %collective-permute-start.5 = (bf16[128,768]{1,0:T(8,128)(2,1)S(1)}, bf16[128,768]{1,0:T(8,128)(2,1)S(1)}, u32[]{:S(2)}, u32[]{:S(2)}) collective-permute-start(bf16[128,768]{1,0:T(8,128)(2,1)S(1)} %get-tuple-element.18), channel_id=1, source_target_pairs={{0,8},{4,12},{8,0},{12,4},{16,24},{20,28},{24,16},{28,20},{1,9},{5... | collective-permute-start | bytes 589832 | tf_op jit(solution)/shard_map/ppermute | solution.py:244
  12.6 9.8 %collective-permute-start.7 = (bf16[128,768]{1,0:T(8,128)(2,1)S(1)}, bf16[128,768]{1,0:T(8,128)(2,1)S(1)}, u32[]{:S(2)}, u32[]{:S(2)}) collective-permute-start(bf16[128,768]{1,0:T(8,128)(2,1)S(1)} %get-tuple-element.20), channel_id=1, source_target_pairs={{0,16},{4,20},{8,24},{12,28},{16,0},{20,4},{24,8},{28,12},{1,17},{... | collective-permute-start | bytes 589832 | tf_op jit(solution)/shard_map/ppermute | solution.py:244
  13.4 9.0 %collective-permute-start.6 = (bf16[128,768]{1,0:T(8,128)(2,1)S(1)}, bf16[128,768]{1,0:T(8,128)(2,1)S(1)}, u32[]{:S(2)}, u32[]{:S(2)}) collective-permute-start(bf16[128,768]{1,0:T(8,128)(2,1)S(1)} %get-tuple-element.14), channel_id=1, source_target_pairs={{0,12},{4,8},{8,4},{12,0},{16,28},{20,24},{24,20},{28,16},{1,13},{... | collective-permute-start | bytes 589832 | tf_op jit(solution)/shard_map/ppermute | solution.py:244
  14.7 4.4 %collective-permute-start.2 = (bf16[128,256]{1,0:T(8,128)(2,1)S(1)}, bf16[128,256]{1,0:T(8,128)(2,1)S(1)}, u32[]{:S(2)}, u32[]{:S(2)}) collective-permute-start(bf16[128,256]{1,0:T(8,128)(2,1)S(1)} %slice.3), channel_id=1, source_target_pairs={{0,3},{1,0},{2,1},{3,2},{4,7},{5,4},{6,5},{7,6},{8,11},{9,8},{10,9... | collective-permute-start | bytes 196616 | tf_op jit(solution)/shard_map/ppermute | solution.py:244
  15.9 6.9 %collective-permute-start.8 = (bf16[128,768]{1,0:T(8,128)(2,1)S(1)}, bf16[128,768]{1,0:T(8,128)(2,1)S(1)}, u32[]{:S(2)}, u32[]{:S(2)}) collective-permute-start(bf16[128,768]{1,0:T(8,128)(2,1)S(1)} %get-tuple-element.15), channel_id=1, source_target_pairs={{0,20},{4,16},{8,28},{12,24},{16,4},{20,0},{24,12},{28,8},{1,21},{... | collective-permute-start | bytes 589832 | tf_op jit(solution)/shard_map/ppermute | solution.py:244
  19.1 3.8 %collective-permute-start.4 = (bf16[128,768]{1,0:T(8,128)(2,1)S(1)}, bf16[128,768]{1,0:T(8,128)(2,1)S(1)}, u32[]{:S(2)}, u32[]{:S(2)}) collective-permute-start(bf16[128,768]{1,0:T(8,128)(2,1)S(1)} %get-tuple-element.13), channel_id=1, source_target_pairs={{0,4},{4,0},{8,12},{12,8},{16,20},{20,16},{24,28},{28,24},{1,5},{5... | collective-permute-start | bytes 589832 | tf_op jit(solution)/shard_map/ppermute | solution.py:244
  20.4 2.5 %collective-permute-start.9 = (bf16[128,768]{1,0:T(8,128)(2,1)S(1)}, bf16[128,768]{1,0:T(8,128)(2,1)S(1)}, u32[]{:S(2)}, u32[]{:S(2)}) collective-permute-start(bf16[128,768]{1,0:T(8,128)(2,1)S(1)} %get-tuple-element.21), channel_id=1, source_target_pairs={{0,4},{4,0},{8,12},{12,8},{16,20},{20,16},{24,28},{28,24},{1,5},{5... | collective-permute-start | bytes 589832 | tf_op jit(solution)/shard_map/ppermute | solution.py:251
  20.4 2.5 %copy-start = (bf16[1,1,8,128,768]{4,3,2,1,0:T(8,128)(2,1)S(1)}, bf16[1,1,8,128,768]{4,3,2,1,0:T(8,128)(2,1)}, u32[]{:S(2)}) copy-start(bf16[1,1,8,128,768]{4,3,2,1,0:T(8,128)(2,1)} %param.5) | copy-start | bytes 4718596
  20.4 2.4 %copy-start.2 = (s32[1,2]{1,0:T(1,128)S(1)}, s32[1,2]{1,0:T(1,128)}, u32[]{:S(2)}) copy-start(s32[1,2]{1,0:T(1,128)} %param.7) | copy-start | bytes 28

commit v6 on v5

--- a/solution.py
+++ b/solution.py
@@ -26,11 +26,27 @@
     return jnp.concatenate([values, jnp.ones_like(values)], axis=1)
 
 
+def upright(values):
+    ones = jnp.ones((16, values.shape[0]), jnp.bfloat16)
+    return jnp.concatenate([values.T, ones], axis=0)
+
+
+def scaled_keys(keys):
+    scaled = keys.astype(jnp.float32) * EXP2_SCALE
+    high = scaled.astype(jnp.bfloat16)
+    low = (scaled - high.astype(jnp.float32)).astype(jnp.bfloat16)
+    return jnp.concatenate([high, low], axis=1)
+
+
+def twice(queries):
+    return jnp.concatenate([queries, queries], axis=1)
+
+
 def attend(scores, values):
     top = functools.reduce(jnp.maximum, [jnp.max(s, axis=1, keepdims=True) for s in scores])
     total = None
     for s, v in zip(scores, values):
-        weights = jnp.exp2((s - top) * EXP2_SCALE).astype(jnp.bfloat16)
+        weights = jnp.exp2(s - top).astype(jnp.bfloat16)
         part = mix(weights, v)
         total = part if total is None else total + part
     return total[:, :HEAD] / total[:, HEAD:]
@@ -47,7 +63,7 @@
     seen = jnp.concatenate(seen, axis=1)
     seen = jnp.concatenate([seen] * heads, axis=0)
     q = jnp.concatenate([rows_ref[:, h * HEAD : (h + 1) * HEAD] for h in range(heads)], axis=0)
-    scores = jnp.where(seen, match(q, pk_ref[...]), MASKED_SCORE)
+    scores = jnp.where(seen, match(twice(q), pk_ref[...]), MASKED_SCORE)
     result = attend([scores], [pv_ref[...]]).astype(jnp.bfloat16)
     for h in range(heads):
         out_ref[:, h * HEAD : (h + 1) * HEAD] = result[h * row_count : (h + 1) * row_count]
@@ -60,42 +76,56 @@
     return mix(chosen, arrived).astype(jnp.bfloat16)
 
 
-def response_part(len_ref, queries, first_head, keys, values, pk_ref, pv_ref, hold_ref, out_ref, sems):
+def response_part(len_ref, queries, keys, values, pk_ref, pv_ref, hold_ref, out_ref, sems):
     slot = queries[0].shape[0]
     heads = queries[0].shape[1] // HEAD
     step = math.gcd(slot, 256)
     chunks = slot // step
-    causal = lax.broadcasted_iota(jnp.int32, (step, step), 1) <= lax.broadcasted_iota(
-        jnp.int32, (step, step), 0
+    causal = lax.broadcasted_iota(jnp.int32, (step, step), 0) <= lax.broadcasted_iota(
+        jnp.int32, (step, step), 1
     )
     items = [(r, c, h) for r in range(len(queries)) for c in range(chunks) for h in range(heads)]
+    prefix_values = upright(pv_ref[:, :HEAD])
+    own_values = [upright(v) for v in values]
 
     def scored(r, c, h):
         low, high = c * step, (c + 1) * step
-        q = queries[r][low:high, h * HEAD : (h + 1) * HEAD]
-        scores = [match(q, pk_ref[...])]
+        q = twice(queries[r][low:high, h * HEAD : (h + 1) * HEAD])
+        scores = [match(pk_ref[...], q)]
         if c:
-            scores.append(match(q, keys[r][:low]))
-        scores.append(jnp.where(causal, match(q, keys[r][low:high]), MASKED_SCORE))
+            scores.append(match(keys[r][:low], q))
+        scores.append(jnp.where(causal, match(keys[r][low:high], q), MASKED_SCORE))
         return scores
 
-    columns = pl.ds(first_head * HEAD, heads * HEAD)
+    def weighed(scores):
+        top = functools.reduce(jnp.maximum, [jnp.max(s, axis=0, keepdims=True) for s in scores])
+        return [jnp.exp2(s - top).astype(jnp.bfloat16) for s in scores]
+
+    def summed(weights, values, live):
+        total = functools.reduce(jnp.add, [mix(v, w) for w, v in zip(weights, values)])
+        share = jnp.where(live, 1.0 / total[HEAD : HEAD + 1], 0.0)
+        return (total[:HEAD] * share).astype(jnp.bfloat16).T
+
     copies = []
-    ahead = scored(*items[0])
+    ready = weighed(scored(*items[0]))
+    ahead = scored(*items[1]) if len(items) > 1 else None
     for n, (r, c, h) in enumerate(items):
-        scores = ahead
+        weights, scores = ready, ahead
+        if n + 2 < len(items):
+            ahead = scored(*items[n + 2])
         if n + 1 < len(items):
-            ahead = scored(*items[n + 1])
+            ready = weighed(scores)
         low, high = c * step, (c + 1) * step
-        value = [pv_ref[...]] + ([values[r][:low]] if c else []) + [values[r][low:high]]
-        live = low + lax.broadcasted_iota(jnp.int32, (step, 1), 0) < len_ref[r]
-        result = jnp.where(live, attend(scores, value), 0.0)
-        hold_ref[r, low:high, h * HEAD : (h + 1) * HEAD] = result.astype(jnp.bfloat16)
+        value = [prefix_values]
+        if c:
+            value.append(own_values[r][:, :low])
+        value.append(own_values[r][:, low:high])
+        live = low + lax.broadcasted_iota(jnp.int32, (1, step), 1) < len_ref[r]
+        result = summed(weights, value, live).astype(jnp.bfloat16)
+        hold_ref[r, low:high, h * HEAD : (h + 1) * HEAD] = result
         if h == heads - 1:
             copy = pltpu.make_async_copy(
-                hold_ref.at[r, pl.ds(low, step)],
-                out_ref.at[r, pl.ds(low, step), columns],
-                sems.at[r, c],
+                hold_ref.at[r, pl.ds(low, step)], out_ref.at[r, pl.ds(low, step)], sems.at[r, c]
             )
             copy.start()
             copies.append(copy)
@@ -106,7 +136,7 @@
 def load_prefix(pieces, pk_ref, pv_ref):
     first = 0
     for p in pieces:
-        pk_ref[first : first + p.shape[0], :] = p[:, :HEAD]
+        pk_ref[first : first + p.shape[0], :] = scaled_keys(p[:, :HEAD])
         pv_ref[first : first + p.shape[0], :] = with_ones(p[:, HEAD:])
         first += p.shape[0]
 
@@ -149,9 +179,8 @@
     response_part(
         len_ref,
         [p[:, :span] for p in placed],
-        0,
-        [p[:, span : span + HEAD] for p in placed],
-        [with_ones(p[:, span + HEAD :]) for p in placed],
+        [scaled_keys(p[:, span : span + HEAD]) for p in placed],
+        [p[:, span + HEAD :] for p in placed],
         pk_ref,
         pv_ref,
         hold_ref,
@@ -167,7 +196,7 @@
 
 
 def prefix_scratch(count):
-    return [pltpu.VMEM((count, HEAD), jnp.bfloat16), pltpu.VMEM((count, 2 * HEAD), jnp.bfloat16)]
+    return [pltpu.VMEM((count, 2 * HEAD), jnp.bfloat16)] * 2
 
 
 def response_call(lengths, order, sent, prefix_kv, blocks):

time: 30.9 us -> 30.7 us (level)
  no operation moved by 1% of the time
where the time goes in v6:
time: 30.7 us; the launch traced here: 30.5 us
  starting transfers between devices  11.9 us (39%)
  Pallas kernels  9.61 us (31%)
  waiting for transfers between devices  4.7 us (15%)
  local copies, waits for them, and re-layouts  3.51 us (11%)
  between operations  0.74 us (2%)
    ppermute x9, starting transfers between devices, body(): got[step] = lax.ppermute(value, 'ctx' if kind == 'ctx' else 'prompt', route)  11.9 us
    pallas_call x1, Pallas kernels, response_call(): pl.pallas_call(response_kernel, out_shape=jax.ShapeDtypeStruct((responses...  7.58 us
    ppermute x9, waiting for transfers between devices, body(): got[step] = lax.ppermute(value, 'ctx' if kind == 'ctx' else 'prompt', route)  4.7 us
    pallas_call x1, Pallas kernels, prefix_call(): pl.pallas_call(prefix_kernel, out_shape=jax.ShapeDtypeStruct((rows.shape[...  2.02 us
    squeeze x1, local copies, waits for them, and re-layouts, pick(): return lax.dynamic_index_in_dim(sent, index ^ k, 0, keepdims=False)  1.37 us
    dynamic_slice x1, local copies, waits for them, and re-layouts, pick(): return lax.dynamic_slice_in_dim(sent, (index ^ k) & -2, 2, 0)  1.03 us
    slice x1, local copies, waits for them, and re-layouts, body(): prefix_kv = rows[:, feat - 2 * HEAD:]  0.84 us
  transfers between devices with their start and end apart: 10, of which 4 were waited for; matrix products, arithmetic and copies ran while one was open for 8% of the time, Pallas kernels for 7%

profile of v6, /device:TPU:0, one launch (start us, length us, event | category | flops | bytes accessed | tf_op | source)
XLA Modules:
  0.0 30.5 jit_solution(9565306830516908049)
XLA Ops:
  0.7 1.0 %dynamic-slice_bitcast_fusion = bf16[2,128,768]{2,1,0:T(8,128)(2,1)S(1)} fusion(bf16[1,1,8,128,768]{4,3,2,1,0:T(8,128)(2,1)} %param.5, s32[]{:T(128)S(6)} %select_n.34), kind=kLoop, calls=%fused_computation | loop fusion | bytes 786436 | tf_op jit(solution)/shard_map/dynamic_slice | solution.py:252
  1.7 4.0 %collective-permute-start.3 = (bf16[2,128,768]{2,1,0:T(8,128)(2,1)S(1)}, bf16[2,128,768]{2,1,0:T(8,128)(2,1)S(1)}, u32[]{:S(2)}, u32[]{:S(2)}) collective-permute-start(bf16[2,128,768]{2,1,0:T(8,128)(2,1)S(1)} %dynamic-slice_bitcast_fusion), channel_id=1, source_target_pairs={{0,24},{4,28},{8,16},{12,20},{16,8},{20,12},{24,0},{28,4},{1,25},{... | collective-permute-start | bytes 1179656 | tf_op jit(solution)/shard_map/ppermute | solution.py:273
  5.6 0.8 %slice.3 = bf16[128,256]{1,0:T(8,128)(2,1)S(1)} slice(bf16[128,768]{1,0:T(8,128)(2,1)} %bitcast.23), slice={[0:128], [512:768]} | slice | bytes 131072 | tf_op jit(solution)/shard_map/slice | solution.py:262
  6.5 1.6 %collective-permute-start = (bf16[128,256]{1,0:T(8,128)(2,1)S(1)}, bf16[128,256]{1,0:T(8,128)(2,1)S(1)}, u32[]{:S(2)}, u32[]{:S(2)}) collective-permute-start(bf16[128,256]{1,0:T(8,128)(2,1)S(1)} %slice.3), channel_id=1, source_target_pairs={{0,1},{1,2},{2,3},{3,0},{4,5},{5,6},{6,7},{7,4},{8,9},{9,10},{10,1... | collective-permute-start | bytes 196616 | tf_op jit(solution)/shard_map/ppermute | solution.py:273
  8.1 2.6 %collective-permute-start.1 = (bf16[128,256]{1,0:T(8,128)(2,1)S(1)}, bf16[128,256]{1,0:T(8,128)(2,1)S(1)}, u32[]{:S(2)}, u32[]{:S(2)}) collective-permute-start(bf16[128,256]{1,0:T(8,128)(2,1)S(1)} %slice.3), channel_id=1, source_target_pairs={{0,2},{1,3},{2,0},{3,1},{4,6},{5,7},{6,4},{7,5},{8,10},{9,11},{10,... | collective-permute-start | bytes 196616 | tf_op jit(solution)/shard_map/ppermute | solution.py:273
  10.7 1.4 %dynamic-slice_bitcast_fusion.3 = (bf16[128,768]{1,0:T(8,128)(2,1)S(1)}, bf16[128,768]{1,0:T(8,128)(2,1)S(1)}, bf16[128,768]{1,0:T(8,128)(2,1)S(1)}, bf16[128,768]{1,0:T(8,128)(2,1)S(1)}, bf16[128,768]{1,0:T(8,128)(2,1)S(1)}) fusion(bf16[1,1,8,128,768]{4,3,2,1,0:T(8,128)(2,1)} %param.5, s32[]{:T(128)S(6)} %select_n.39, s32[]{:T(128)S(6)} %select_n.37, ...), kind=kLoop, calls=%fused_computation.4 | loop fusion | bytes 1966100 | tf_op jit(solution)/shard_map/jit(dynamic_index_in_dim)/squeeze | solution.py:253
  12.0 0.6 %collective-permute-start.5 = (bf16[128,768]{1,0:T(8,128)(2,1)S(1)}, bf16[128,768]{1,0:T(8,128)(2,1)S(1)}, u32[]{:S(2)}, u32[]{:S(2)}) collective-permute-start(bf16[128,768]{1,0:T(8,128)(2,1)S(1)} %get-tuple-element.18), channel_id=1, source_target_pairs={{0,8},{4,12},{8,0},{12,4},{16,24},{20,28},{24,16},{28,20},{1,9},{5... | collective-permute-start | bytes 589832 | tf_op jit(solution)/shard_map/ppermute | solution.py:273
  12.6 0.5 %collective-permute-start.7 = (bf16[128,768]{1,0:T(8,128)(2,1)S(1)}, bf16[128,768]{1,0:T(8,128)(2,1)S(1)}, u32[]{:S(2)}, u32[]{:S(2)}) collective-permute-start(bf16[128,768]{1,0:T(8,128)(2,1)S(1)} %get-tuple-element.20), channel_id=1, source_target_pairs={{0,16},{4,20},{8,24},{12,28},{16,0},{20,4},{24,8},{28,12},{1,17},{... | collective-permute-start | bytes 589832 | tf_op jit(solution)/shard_map/ppermute | solution.py:273
  13.1 0.2 copy.6.order_ref
  13.4 0.0 collective-permute-done
  13.4 0.1 collective-permute-start.6
  13.5 1.2 %collective-permute-done.1 = bf16[128,256]{1,0:T(8,128)(2,1)S(1)} collective-permute-done((bf16[128,256]{1,0:T(8,128)(2,1)S(1)}, bf16[128,256]{1,0:T(8,128)(2,1)S(1)}, u32[]{:S(2)}, u32[]{:S(2)}) %collective-permute-start.1) | collective-permute-done | bytes 65568 | tf_op jit(solution)/shard_map/ppermute | solution.py:273
  14.7 1.2 %collective-permute-start.2 = (bf16[128,256]{1,0:T(8,128)(2,1)S(1)}, bf16[128,256]{1,0:T(8,128)(2,1)S(1)}, u32[]{:S(2)}, u32[]{:S(2)}) collective-permute-start(bf16[128,256]{1,0:T(8,128)(2,1)S(1)} %slice.3), channel_id=1, source_target_pairs={{0,3},{1,0},{2,1},{3,2},{4,7},{5,4},{6,5},{7,6},{8,11},{9,8},{10,9... | collective-permute-start | bytes 196616 | tf_op jit(solution)/shard_map/ppermute | solution.py:273
  15.9 1.3 %collective-permute-start.8 = (bf16[128,768]{1,0:T(8,128)(2,1)S(1)}, bf16[128,768]{1,0:T(8,128)(2,1)S(1)}, u32[]{:S(2)}, u32[]{:S(2)}) collective-permute-start(bf16[128,768]{1,0:T(8,128)(2,1)S(1)} %get-tuple-element.15), channel_id=1, source_target_pairs={{0,20},{4,16},{8,28},{12,24},{16,4},{20,0},{24,12},{28,8},{1,21},{... | collective-permute-start | bytes 589832 | tf_op jit(solution)/shard_map/ppermute | solution.py:273
  17.3 1.8 %collective-permute-done.2 = bf16[128,256]{1,0:T(8,128)(2,1)S(1)} collective-permute-done((bf16[128,256]{1,0:T(8,128)(2,1)S(1)}, bf16[128,256]{1,0:T(8,128)(2,1)S(1)}, u32[]{:S(2)}, u32[]{:S(2)}) %collective-permute-start.2) | collective-permute-done | bytes 65568 | tf_op jit(solution)/shard_map/ppermute | solution.py:273
  19.1 0.0 collective-permute-start.4
  19.1 1.3 %collective-permute-done.5.refs_1_ = bf16[128,768]{1,0:T(8,128)(2,1)S(1)} collective-permute-done((bf16[128,768]{1,0:T(8,128)(2,1)S(1)}, bf16[128,768]{1,0:T(8,128)(2,1)S(1)}, u32[]{:S(2)}, u32[]{:S(2)}) %collective-permute-start.5) | collective-permute-done | bytes 196640 | tf_op jit(solution)/shard_map/ppermute | solution.py:273
  20.4 0.0 copy-start
  20.4 0.0 copy-start.2
  20.4 2.0 %prefix_attention.1 = bf16[128,512]{1,0:T(8,128)(2,1)} custom-call(s32[4]{0:T(128)S(1)} %fusion.starts_ref, bf16[128,768]{1,0:T(8,128)(2,1)S(1)} %bitcast.24, bf16[512,256]{1,0:T(8,128)(2,1)S(1)} %pad_maximum_fusion.kv_ref.prefix_ref), custom_call_target="tpu_custom_call" | custom-call | flops 1000000000 | bytes 1000000 | tf_op jit(solution)/shard_map/prefix_attention/pallas_call | solution.py:150
  22.4 0.0 collective-permute-done.7.refs_3_
  22.4 0.0 collective-permute-done.6.refs_2_
  22.5 0.4 %collective-permute-done.8.refs_4_ = bf16[128,768]{1,0:T(8,128)(2,1)S(1)} collective-permute-done((bf16[128,768]{1,0:T(8,128)(2,1)S(1)}, bf16[128,768]{1,0:T(8,128)(2,1)S(1)}, u32[]{:S(2)}, u32[]{:S(2)}) %collective-permute-start.8) | collective-permute-done | bytes 196640 | tf_op jit(solution)/shard_map/ppermute | solution.py:273
  22.9 7.6 %response_attention.1 = bf16[2,512,512]{2,1,0:T(8,128)(2,1)} custom-call(s32[2]{0:T(128)S(1)} %bitcast.25, s32[1024,1]{1,0:T(8,128)S(1)} %copy.6.order_ref, bf16[8,128,768]{2,1,0:T(8,128)(2,1)S(1)} %bitcast.22, bf16[512,256]{1,0:T(8,128)(2,1)S(1)} %pad_maximum_fusion.kv_ref.prefix_ref, bf16[128,768]{1,0:T(8,128)(2,1)S(1)} %collective-permute-done.4.refs_0_, ...), custom_call_target="tpu_custom_call" | custom-call | flops 5000000000 | bytes 4000000 | tf_op jit(solution)/shard_map/response_attention/pallas_call | solution.py:207
  (13 shorter events, 0.1 us)
Async XLA Ops:
  0.6 12.5 %copy-start.3 = (s32[1,1,1024]{2,1,0:T(1,128)S(1)}, s32[1,1,1024]{2,1,0:T(1,128)}, u32[]{:S(2)}) copy-start(s32[1,1,1024]{2,1,0:T(1,128)} %param.6) | copy-start | bytes 12292
  1.7 14.3 %collective-permute-start.3 = (bf16[2,128,768]{2,1,0:T(8,128)(2,1)S(1)}, bf16[2,128,768]{2,1,0:T(8,128)(2,1)S(1)}, u32[]{:S(2)}, u32[]{:S(2)}) collective-permute-start(bf16[2,128,768]{2,1,0:T(8,128)(2,1)S(1)} %dynamic-slice_bitcast_fusion), channel_id=1, source_target_pairs={{0,24},{4,28},{8,16},{12,20},{16,8},{20,12},{24,0},{28,4},{1,25},{... | collective-permute-start | bytes 1179656 | tf_op jit(solution)/shard_map/ppermute | solution.py:273
  6.5 6.9 %collective-permute-start = (bf16[128,256]{1,0:T(8,128)(2,1)S(1)}, bf16[128,256]{1,0:T(8,128)(2,1)S(1)}, u32[]{:S(2)}, u32[]{:S(2)}) collective-permute-start(bf16[128,256]{1,0:T(8,128)(2,1)S(1)} %slice.3), channel_id=1, source_target_pairs={{0,1},{1,2},{2,3},{3,0},{4,5},{5,6},{6,7},{7,4},{8,9},{9,10},{10,1... | collective-permute-start | bytes 196616 | tf_op jit(solution)/shard_map/ppermute | solution.py:273
  8.1 6.6 %collective-permute-start.1 = (bf16[128,256]{1,0:T(8,128)(2,1)S(1)}, bf16[128,256]{1,0:T(8,128)(2,1)S(1)}, u32[]{:S(2)}, u32[]{:S(2)}) collective-permute-start(bf16[128,256]{1,0:T(8,128)(2,1)S(1)} %slice.3), channel_id=1, source_target_pairs={{0,2},{1,3},{2,0},{3,1},{4,6},{5,7},{6,4},{7,5},{8,10},{9,11},{10,... | collective-permute-start | bytes 196616 | tf_op jit(solution)/shard_map/ppermute | solution.py:273
  10.7 9.7 %copy-start.1 = (bf16[1,128,768]{2,1,0:T(8,128)(2,1)S(1)}, bf16[1,128,768]{2,1,0:T(8,128)(2,1)}, u32[]{:S(2)}) copy-start(bf16[1,128,768]{2,1,0:T(8,128)(2,1)} %param.4) | copy-start | bytes 589828
  12.0 8.3 %collective-permute-start.5 = (bf16[128,768]{1,0:T(8,128)(2,1)S(1)}, bf16[128,768]{1,0:T(8,128)(2,1)S(1)}, u32[]{:S(2)}, u32[]{:S(2)}) collective-permute-start(bf16[128,768]{1,0:T(8,128)(2,1)S(1)} %get-tuple-element.18), channel_id=1, source_target_pairs={{0,8},{4,12},{8,0},{12,4},{16,24},{20,28},{24,16},{28,20},{1,9},{5... | collective-permute-start | bytes 589832 | tf_op jit(solution)/shard_map/ppermute | solution.py:273
  12.6 9.8 %collective-permute-start.7 = (bf16[128,768]{1,0:T(8,128)(2,1)S(1)}, bf16[128,768]{1,0:T(8,128)(2,1)S(1)}, u32[]{:S(2)}, u32[]{:S(2)}) collective-permute-start(bf16[128,768]{1,0:T(8,128)(2,1)S(1)} %get-tuple-element.20), channel_id=1, source_target_pairs={{0,16},{4,20},{8,24},{12,28},{16,0},{20,4},{24,8},{28,12},{1,17},{... | collective-permute-start | bytes 589832 | tf_op jit(solution)/shard_map/ppermute | solution.py:273
  13.4 9.1 %collective-permute-start.6 = (bf16[128,768]{1,0:T(8,128)(2,1)S(1)}, bf16[128,768]{1,0:T(8,128)(2,1)S(1)}, u32[]{:S(2)}, u32[]{:S(2)}) collective-permute-start(bf16[128,768]{1,0:T(8,128)(2,1)S(1)} %get-tuple-element.14), channel_id=1, source_target_pairs={{0,12},{4,8},{8,4},{12,0},{16,28},{20,24},{24,20},{28,16},{1,13},{... | collective-permute-start | bytes 589832 | tf_op jit(solution)/shard_map/ppermute | solution.py:273
  14.7 4.4 %collective-permute-start.2 = (bf16[128,256]{1,0:T(8,128)(2,1)S(1)}, bf16[128,256]{1,0:T(8,128)(2,1)S(1)}, u32[]{:S(2)}, u32[]{:S(2)}) collective-permute-start(bf16[128,256]{1,0:T(8,128)(2,1)S(1)} %slice.3), channel_id=1, source_target_pairs={{0,3},{1,0},{2,1},{3,2},{4,7},{5,4},{6,5},{7,6},{8,11},{9,8},{10,9... | collective-permute-start | bytes 196616 | tf_op jit(solution)/shard_map/ppermute | solution.py:273
  15.9 6.9 %collective-permute-start.8 = (bf16[128,768]{1,0:T(8,128)(2,1)S(1)}, bf16[128,768]{1,0:T(8,128)(2,1)S(1)}, u32[]{:S(2)}, u32[]{:S(2)}) collective-permute-start(bf16[128,768]{1,0:T(8,128)(2,1)S(1)} %get-tuple-element.15), channel_id=1, source_target_pairs={{0,20},{4,16},{8,28},{12,24},{16,4},{20,0},{24,12},{28,8},{1,21},{... | collective-permute-start | bytes 589832 | tf_op jit(solution)/shard_map/ppermute | solution.py:273
  19.1 3.8 %collective-permute-start.4 = (bf16[128,768]{1,0:T(8,128)(2,1)S(1)}, bf16[128,768]{1,0:T(8,128)(2,1)S(1)}, u32[]{:S(2)}, u32[]{:S(2)}) collective-permute-start(bf16[128,768]{1,0:T(8,128)(2,1)S(1)} %get-tuple-element.13), channel_id=1, source_target_pairs={{0,4},{4,0},{8,12},{12,8},{16,20},{20,16},{24,28},{28,24},{1,5},{5... | collective-permute-start | bytes 589832 | tf_op jit(solution)/shard_map/ppermute | solution.py:273
  20.4 2.5 %collective-permute-start.9 = (bf16[128,768]{1,0:T(8,128)(2,1)S(1)}, bf16[128,768]{1,0:T(8,128)(2,1)S(1)}, u32[]{:S(2)}, u32[]{:S(2)}) collective-permute-start(bf16[128,768]{1,0:T(8,128)(2,1)S(1)} %get-tuple-element.21), channel_id=1, source_target_pairs={{0,4},{4,0},{8,12},{12,8},{16,20},{20,16},{24,28},{28,24},{1,5},{5... | collective-permute-start | bytes 589832 | tf_op jit(solution)/shard_map/ppermute | solution.py:280
  20.4 2.5 %copy-start = (bf16[1,1,8,128,768]{4,3,2,1,0:T(8,128)(2,1)S(1)}, bf16[1,1,8,128,768]{4,3,2,1,0:T(8,128)(2,1)}, u32[]{:S(2)}) copy-start(bf16[1,1,8,128,768]{4,3,2,1,0:T(8,128)(2,1)} %param.5) | copy-start | bytes 4718596
  20.4 2.4 %copy-start.2 = (s32[1,2]{1,0:T(1,128)S(1)}, s32[1,2]{1,0:T(1,128)}, u32[]{:S(2)}) copy-start(s32[1,2]{1,0:T(1,128)} %param.7) | copy-start | bytes 28

commit v7 on v6

--- a/solution.py
+++ b/solution.py
@@ -86,7 +86,7 @@
     )
     items = [(r, c, h) for r in range(len(queries)) for c in range(chunks) for h in range(heads)]
     prefix_values = upright(pv_ref[:, :HEAD])
-    own_values = [upright(v) for v in values]
+    all_values = [jnp.concatenate([prefix_values, upright(v)], axis=1) for v in values]
 
     def scored(r, c, h):
         low, high = c * step, (c + 1) * step
@@ -102,7 +102,7 @@
         return [jnp.exp2(s - top).astype(jnp.bfloat16) for s in scores]
 
     def summed(weights, values, live):
-        total = functools.reduce(jnp.add, [mix(v, w) for w, v in zip(weights, values)])
+        total = mix(values, jnp.concatenate(weights, axis=0))
         share = jnp.where(live, 1.0 / total[HEAD : HEAD + 1], 0.0)
         return (total[:HEAD] * share).astype(jnp.bfloat16).T
 
@@ -116,10 +116,7 @@
         if n + 1 < len(items):
             ready = weighed(scores)
         low, high = c * step, (c + 1) * step
-        value = [prefix_values]
-        if c:
-            value.append(own_values[r][:, :low])
-        value.append(own_values[r][:, low:high])
+        value = all_values[r][:, : prefix_values.shape[1] + high]
         live = low + lax.broadcasted_iota(jnp.int32, (1, step), 1) < len_ref[r]
         result = summed(weights, value, live).astype(jnp.bfloat16)
         hold_ref[r, low:high, h * HEAD : (h + 1) * HEAD] = result

time: 30.7 us -> 30.7 us (level)
  no operation moved by 1% of the time
where the time goes in v7:
time: 30.7 us; the launch traced here: 30.5 us
  starting transfers between devices  11.9 us (39%)
  Pallas kernels  9.61 us (31%)
  waiting for transfers between devices  4.7 us (15%)
  local copies, waits for them, and re-layouts  3.51 us (11%)
  between operations  0.74 us (2%)
    ppermute x9, starting transfers between devices, body(): got[step] = lax.ppermute(value, 'ctx' if kind == 'ctx' else 'prompt', route)  11.9 us
    pallas_call x1, Pallas kernels, response_call(): pl.pallas_call(response_kernel, out_shape=jax.ShapeDtypeStruct((responses...  7.59 us
    ppermute x9, waiting for transfers between devices, body(): got[step] = lax.ppermute(value, 'ctx' if kind == 'ctx' else 'prompt', route)  4.7 us
    pallas_call x1, Pallas kernels, prefix_call(): pl.pallas_call(prefix_kernel, out_shape=jax.ShapeDtypeStruct((rows.shape[...  2.02 us
    squeeze x1, local copies, waits for them, and re-layouts, pick(): return lax.dynamic_index_in_dim(sent, index ^ k, 0, keepdims=False)  1.37 us
    dynamic_slice x1, local copies, waits for them, and re-layouts, pick(): return lax.dynamic_slice_in_dim(sent, (index ^ k) & -2, 2, 0)  1.03 us
    slice x1, local copies, waits for them, and re-layouts, body(): prefix_kv = rows[:, feat - 2 * HEAD:]  0.84 us
  transfers between devices with their start and end apart: 10, of which 4 were waited for; matrix products, arithmetic and copies ran while one was open for 8% of the time, Pallas kernels for 7%

profile of v7, /device:TPU:0, one launch (start us, length us, event | category | flops | bytes accessed | tf_op | source)
XLA Modules:
  0.0 30.5 jit_solution(8765832193158066902)
XLA Ops:
  0.7 1.0 %dynamic-slice_bitcast_fusion = bf16[2,128,768]{2,1,0:T(8,128)(2,1)S(1)} fusion(bf16[1,1,8,128,768]{4,3,2,1,0:T(8,128)(2,1)} %param.5, s32[]{:T(128)S(6)} %select_n.34), kind=kLoop, calls=%fused_computation | loop fusion | bytes 786436 | tf_op jit(solution)/shard_map/dynamic_slice | solution.py:249
  1.7 4.0 %collective-permute-start.3 = (bf16[2,128,768]{2,1,0:T(8,128)(2,1)S(1)}, bf16[2,128,768]{2,1,0:T(8,128)(2,1)S(1)}, u32[]{:S(2)}, u32[]{:S(2)}) collective-permute-start(bf16[2,128,768]{2,1,0:T(8,128)(2,1)S(1)} %dynamic-slice_bitcast_fusion), channel_id=1, source_target_pairs={{0,24},{4,28},{8,16},{12,20},{16,8},{20,12},{24,0},{28,4},{1,25},{... | collective-permute-start | bytes 1179656 | tf_op jit(solution)/shard_map/ppermute | solution.py:270
  5.6 0.8 %slice.3 = bf16[128,256]{1,0:T(8,128)(2,1)S(1)} slice(bf16[128,768]{1,0:T(8,128)(2,1)} %bitcast.23), slice={[0:128], [512:768]} | slice | bytes 131072 | tf_op jit(solution)/shard_map/slice | solution.py:259
  6.5 1.6 %collective-permute-start = (bf16[128,256]{1,0:T(8,128)(2,1)S(1)}, bf16[128,256]{1,0:T(8,128)(2,1)S(1)}, u32[]{:S(2)}, u32[]{:S(2)}) collective-permute-start(bf16[128,256]{1,0:T(8,128)(2,1)S(1)} %slice.3), channel_id=1, source_target_pairs={{0,1},{1,2},{2,3},{3,0},{4,5},{5,6},{6,7},{7,4},{8,9},{9,10},{10,1... | collective-permute-start | bytes 196616 | tf_op jit(solution)/shard_map/ppermute | solution.py:270
  8.1 2.6 %collective-permute-start.1 = (bf16[128,256]{1,0:T(8,128)(2,1)S(1)}, bf16[128,256]{1,0:T(8,128)(2,1)S(1)}, u32[]{:S(2)}, u32[]{:S(2)}) collective-permute-start(bf16[128,256]{1,0:T(8,128)(2,1)S(1)} %slice.3), channel_id=1, source_target_pairs={{0,2},{1,3},{2,0},{3,1},{4,6},{5,7},{6,4},{7,5},{8,10},{9,11},{10,... | collective-permute-start | bytes 196616 | tf_op jit(solution)/shard_map/ppermute | solution.py:270
  10.7 1.4 %dynamic-slice_bitcast_fusion.3 = (bf16[128,768]{1,0:T(8,128)(2,1)S(1)}, bf16[128,768]{1,0:T(8,128)(2,1)S(1)}, bf16[128,768]{1,0:T(8,128)(2,1)S(1)}, bf16[128,768]{1,0:T(8,128)(2,1)S(1)}, bf16[128,768]{1,0:T(8,128)(2,1)S(1)}) fusion(bf16[1,1,8,128,768]{4,3,2,1,0:T(8,128)(2,1)} %param.5, s32[]{:T(128)S(6)} %select_n.39, s32[]{:T(128)S(6)} %select_n.37, ...), kind=kLoop, calls=%fused_computation.4 | loop fusion | bytes 1966100 | tf_op jit(solution)/shard_map/jit(dynamic_index_in_dim)/squeeze | solution.py:250
  12.0 0.6 %collective-permute-start.5 = (bf16[128,768]{1,0:T(8,128)(2,1)S(1)}, bf16[128,768]{1,0:T(8,128)(2,1)S(1)}, u32[]{:S(2)}, u32[]{:S(2)}) collective-permute-start(bf16[128,768]{1,0:T(8,128)(2,1)S(1)} %get-tuple-element.18), channel_id=1, source_target_pairs={{0,8},{4,12},{8,0},{12,4},{16,24},{20,28},{24,16},{28,20},{1,9},{5... | collective-permute-start | bytes 589832 | tf_op jit(solution)/shard_map/ppermute | solution.py:270
  12.6 0.5 %collective-permute-start.7 = (bf16[128,768]{1,0:T(8,128)(2,1)S(1)}, bf16[128,768]{1,0:T(8,128)(2,1)S(1)}, u32[]{:S(2)}, u32[]{:S(2)}) collective-permute-start(bf16[128,768]{1,0:T(8,128)(2,1)S(1)} %get-tuple-element.20), channel_id=1, source_target_pairs={{0,16},{4,20},{8,24},{12,28},{16,0},{20,4},{24,8},{28,12},{1,17},{... | collective-permute-start | bytes 589832 | tf_op jit(solution)/shard_map/ppermute | solution.py:270
  13.1 0.2 copy.6.order_ref
  13.4 0.0 collective-permute-done
  13.4 0.1 collective-permute-start.6
  13.5 1.2 %collective-permute-done.1 = bf16[128,256]{1,0:T(8,128)(2,1)S(1)} collective-permute-done((bf16[128,256]{1,0:T(8,128)(2,1)S(1)}, bf16[128,256]{1,0:T(8,128)(2,1)S(1)}, u32[]{:S(2)}, u32[]{:S(2)}) %collective-permute-start.1) | collective-permute-done | bytes 65568 | tf_op jit(solution)/shard_map/ppermute | solution.py:270
  14.7 1.2 %collective-permute-start.2 = (bf16[128,256]{1,0:T(8,128)(2,1)S(1)}, bf16[128,256]{1,0:T(8,128)(2,1)S(1)}, u32[]{:S(2)}, u32[]{:S(2)}) collective-permute-start(bf16[128,256]{1,0:T(8,128)(2,1)S(1)} %slice.3), channel_id=1, source_target_pairs={{0,3},{1,0},{2,1},{3,2},{4,7},{5,4},{6,5},{7,6},{8,11},{9,8},{10,9... | collective-permute-start | bytes 196616 | tf_op jit(solution)/shard_map/ppermute | solution.py:270
  15.9 1.3 %collective-permute-start.8 = (bf16[128,768]{1,0:T(8,128)(2,1)S(1)}, bf16[128,768]{1,0:T(8,128)(2,1)S(1)}, u32[]{:S(2)}, u32[]{:S(2)}) collective-permute-start(bf16[128,768]{1,0:T(8,128)(2,1)S(1)} %get-tuple-element.15), channel_id=1, source_target_pairs={{0,20},{4,16},{8,28},{12,24},{16,4},{20,0},{24,12},{28,8},{1,21},{... | collective-permute-start | bytes 589832 | tf_op jit(solution)/shard_map/ppermute | solution.py:270
  17.3 1.8 %collective-permute-done.2 = bf16[128,256]{1,0:T(8,128)(2,1)S(1)} collective-permute-done((bf16[128,256]{1,0:T(8,128)(2,1)S(1)}, bf16[128,256]{1,0:T(8,128)(2,1)S(1)}, u32[]{:S(2)}, u32[]{:S(2)}) %collective-permute-start.2) | collective-permute-done | bytes 65568 | tf_op jit(solution)/shard_map/ppermute | solution.py:270
  19.1 0.0 collective-permute-start.4
  19.1 1.3 %collective-permute-done.5.refs_1_ = bf16[128,768]{1,0:T(8,128)(2,1)S(1)} collective-permute-done((bf16[128,768]{1,0:T(8,128)(2,1)S(1)}, bf16[128,768]{1,0:T(8,128)(2,1)S(1)}, u32[]{:S(2)}, u32[]{:S(2)}) %collective-permute-start.5) | collective-permute-done | bytes 196640 | tf_op jit(solution)/shard_map/ppermute | solution.py:270
  20.4 0.0 copy-start
  20.4 0.0 copy-start.2
  20.4 2.0 %prefix_attention.1 = bf16[128,512]{1,0:T(8,128)(2,1)} custom-call(s32[4]{0:T(128)S(1)} %fusion.starts_ref, bf16[128,768]{1,0:T(8,128)(2,1)S(1)} %bitcast.24, bf16[512,256]{1,0:T(8,128)(2,1)S(1)} %pad_maximum_fusion.kv_ref.prefix_ref), custom_call_target="tpu_custom_call" | custom-call | flops 1000000000 | bytes 1000000 | tf_op jit(solution)/shard_map/prefix_attention/pallas_call | solution.py:147
  22.4 0.0 collective-permute-done.7.refs_3_
  22.4 0.0 collective-permute-done.6.refs_2_
  22.5 0.4 %collective-permute-done.8.refs_4_ = bf16[128,768]{1,0:T(8,128)(2,1)S(1)} collective-permute-done((bf16[128,768]{1,0:T(8,128)(2,1)S(1)}, bf16[128,768]{1,0:T(8,128)(2,1)S(1)}, u32[]{:S(2)}, u32[]{:S(2)}) %collective-permute-start.8) | collective-permute-done | bytes 196640 | tf_op jit(solution)/shard_map/ppermute | solution.py:270
  22.9 7.6 %response_attention.1 = bf16[2,512,512]{2,1,0:T(8,128)(2,1)} custom-call(s32[2]{0:T(128)S(1)} %bitcast.25, s32[1024,1]{1,0:T(8,128)S(1)} %copy.6.order_ref, bf16[8,128,768]{2,1,0:T(8,128)(2,1)S(1)} %bitcast.22, bf16[512,256]{1,0:T(8,128)(2,1)S(1)} %pad_maximum_fusion.kv_ref.prefix_ref, bf16[128,768]{1,0:T(8,128)(2,1)S(1)} %collective-permute-done.4.refs_0_, ...), custom_call_target="tpu_custom_call" | custom-call | flops 5000000000 | bytes 4000000 | tf_op jit(solution)/shard_map/response_attention/pallas_call | solution.py:204
  (13 shorter events, 0.1 us)
Async XLA Ops:
  0.6 12.5 %copy-start.3 = (s32[1,1,1024]{2,1,0:T(1,128)S(1)}, s32[1,1,1024]{2,1,0:T(1,128)}, u32[]{:S(2)}) copy-start(s32[1,1,1024]{2,1,0:T(1,128)} %param.6) | copy-start | bytes 12292
  1.7 14.3 %collective-permute-start.3 = (bf16[2,128,768]{2,1,0:T(8,128)(2,1)S(1)}, bf16[2,128,768]{2,1,0:T(8,128)(2,1)S(1)}, u32[]{:S(2)}, u32[]{:S(2)}) collective-permute-start(bf16[2,128,768]{2,1,0:T(8,128)(2,1)S(1)} %dynamic-slice_bitcast_fusion), channel_id=1, source_target_pairs={{0,24},{4,28},{8,16},{12,20},{16,8},{20,12},{24,0},{28,4},{1,25},{... | collective-permute-start | bytes 1179656 | tf_op jit(solution)/shard_map/ppermute | solution.py:270
  6.5 6.9 %collective-permute-start = (bf16[128,256]{1,0:T(8,128)(2,1)S(1)}, bf16[128,256]{1,0:T(8,128)(2,1)S(1)}, u32[]{:S(2)}, u32[]{:S(2)}) collective-permute-start(bf16[128,256]{1,0:T(8,128)(2,1)S(1)} %slice.3), channel_id=1, source_target_pairs={{0,1},{1,2},{2,3},{3,0},{4,5},{5,6},{6,7},{7,4},{8,9},{9,10},{10,1... | collective-permute-start | bytes 196616 | tf_op jit(solution)/shard_map/ppermute | solution.py:270
  8.1 6.6 %collective-permute-start.1 = (bf16[128,256]{1,0:T(8,128)(2,1)S(1)}, bf16[128,256]{1,0:T(8,128)(2,1)S(1)}, u32[]{:S(2)}, u32[]{:S(2)}) collective-permute-start(bf16[128,256]{1,0:T(8,128)(2,1)S(1)} %slice.3), channel_id=1, source_target_pairs={{0,2},{1,3},{2,0},{3,1},{4,6},{5,7},{6,4},{7,5},{8,10},{9,11},{10,... | collective-permute-start | bytes 196616 | tf_op jit(solution)/shard_map/ppermute | solution.py:270
  10.7 9.7 %copy-start.1 = (bf16[1,128,768]{2,1,0:T(8,128)(2,1)S(1)}, bf16[1,128,768]{2,1,0:T(8,128)(2,1)}, u32[]{:S(2)}) copy-start(bf16[1,128,768]{2,1,0:T(8,128)(2,1)} %param.4) | copy-start | bytes 589828
  12.0 8.3 %collective-permute-start.5 = (bf16[128,768]{1,0:T(8,128)(2,1)S(1)}, bf16[128,768]{1,0:T(8,128)(2,1)S(1)}, u32[]{:S(2)}, u32[]{:S(2)}) collective-permute-start(bf16[128,768]{1,0:T(8,128)(2,1)S(1)} %get-tuple-element.18), channel_id=1, source_target_pairs={{0,8},{4,12},{8,0},{12,4},{16,24},{20,28},{24,16},{28,20},{1,9},{5... | collective-permute-start | bytes 589832 | tf_op jit(solution)/shard_map/ppermute | solution.py:270
  12.6 9.8 %collective-permute-start.7 = (bf16[128,768]{1,0:T(8,128)(2,1)S(1)}, bf16[128,768]{1,0:T(8,128)(2,1)S(1)}, u32[]{:S(2)}, u32[]{:S(2)}) collective-permute-start(bf16[128,768]{1,0:T(8,128)(2,1)S(1)} %get-tuple-element.20), channel_id=1, source_target_pairs={{0,16},{4,20},{8,24},{12,28},{16,0},{20,4},{24,8},{28,12},{1,17},{... | collective-permute-start | bytes 589832 | tf_op jit(solution)/shard_map/ppermute | solution.py:270
  13.4 9.1 %collective-permute-start.6 = (bf16[128,768]{1,0:T(8,128)(2,1)S(1)}, bf16[128,768]{1,0:T(8,128)(2,1)S(1)}, u32[]{:S(2)}, u32[]{:S(2)}) collective-permute-start(bf16[128,768]{1,0:T(8,128)(2,1)S(1)} %get-tuple-element.14), channel_id=1, source_target_pairs={{0,12},{4,8},{8,4},{12,0},{16,28},{20,24},{24,20},{28,16},{1,13},{... | collective-permute-start | bytes 589832 | tf_op jit(solution)/shard_map/ppermute | solution.py:270
  14.7 4.4 %collective-permute-start.2 = (bf16[128,256]{1,0:T(8,128)(2,1)S(1)}, bf16[128,256]{1,0:T(8,128)(2,1)S(1)}, u32[]{:S(2)}, u32[]{:S(2)}) collective-permute-start(bf16[128,256]{1,0:T(8,128)(2,1)S(1)} %slice.3), channel_id=1, source_target_pairs={{0,3},{1,0},{2,1},{3,2},{4,7},{5,4},{6,5},{7,6},{8,11},{9,8},{10,9... | collective-permute-start | bytes 196616 | tf_op jit(solution)/shard_map/ppermute | solution.py:270
  15.9 6.9 %collective-permute-start.8 = (bf16[128,768]{1,0:T(8,128)(2,1)S(1)}, bf16[128,768]{1,0:T(8,128)(2,1)S(1)}, u32[]{:S(2)}, u32[]{:S(2)}) collective-permute-start(bf16[128,768]{1,0:T(8,128)(2,1)S(1)} %get-tuple-element.15), channel_id=1, source_target_pairs={{0,20},{4,16},{8,28},{12,24},{16,4},{20,0},{24,12},{28,8},{1,21},{... | collective-permute-start | bytes 589832 | tf_op jit(solution)/shard_map/ppermute | solution.py:270
  19.1 3.8 %collective-permute-start.4 = (bf16[128,768]{1,0:T(8,128)(2,1)S(1)}, bf16[128,768]{1,0:T(8,128)(2,1)S(1)}, u32[]{:S(2)}, u32[]{:S(2)}) collective-permute-start(bf16[128,768]{1,0:T(8,128)(2,1)S(1)} %get-tuple-element.13), channel_id=1, source_target_pairs={{0,4},{4,0},{8,12},{12,8},{16,20},{20,16},{24,28},{28,24},{1,5},{5... | collective-permute-start | bytes 589832 | tf_op jit(solution)/shard_map/ppermute | solution.py:270
  20.4 2.5 %collective-permute-start.9 = (bf16[128,768]{1,0:T(8,128)(2,1)S(1)}, bf16[128,768]{1,0:T(8,128)(2,1)S(1)}, u32[]{:S(2)}, u32[]{:S(2)}) collective-permute-start(bf16[128,768]{1,0:T(8,128)(2,1)S(1)} %get-tuple-element.21), channel_id=1, source_target_pairs={{0,4},{4,0},{8,12},{12,8},{16,20},{20,16},{24,28},{28,24},{1,5},{5... | collective-permute-start | bytes 589832 | tf_op jit(solution)/shard_map/ppermute | solution.py:277
  20.4 2.5 %copy-start = (bf16[1,1,8,128,768]{4,3,2,1,0:T(8,128)(2,1)S(1)}, bf16[1,1,8,128,768]{4,3,2,1,0:T(8,128)(2,1)}, u32[]{:S(2)}) copy-start(bf16[1,1,8,128,768]{4,3,2,1,0:T(8,128)(2,1)} %param.5) | copy-start | bytes 4718596
  20.4 2.4 %copy-start.2 = (s32[1,2]{1,0:T(1,128)S(1)}, s32[1,2]{1,0:T(1,128)}, u32[]{:S(2)}) copy-start(s32[1,2]{1,0:T(1,128)} %param.7) | copy-start | bytes 28

commit v8 on v7

--- a/solution.py
+++ b/solution.py
@@ -84,7 +84,7 @@
     causal = lax.broadcasted_iota(jnp.int32, (step, step), 0) <= lax.broadcasted_iota(
         jnp.int32, (step, step), 1
     )
-    items = [(r, c, h) for r in range(len(queries)) for c in range(chunks) for h in range(heads)]
+    items = [(r, c, h) for r in range(len(queries)) for c in reversed(range(chunks)) for h in range(heads)]
     prefix_values = upright(pv_ref[:, :HEAD])
     all_values = [jnp.concatenate([prefix_values, upright(v)], axis=1) for v in values]
 

time: 30.7 us -> 30.6 us (level)
  no operation moved by 1% of the time
where the time goes in v8:
time: 30.6 us; the launch traced here: 30.3 us
  starting transfers between devices  11.9 us (39%)
  Pallas kernels  9.5 us (31%)
  waiting for transfers between devices  4.7 us (15%)
  local copies, waits for them, and re-layouts  3.51 us (11%)
  between operations  0.74 us (2%)
    ppermute x9, starting transfers between devices, body(): got[step] = lax.ppermute(value, 'ctx' if kind == 'ctx' else 'prompt', route)  11.9 us
    pallas_call x1, Pallas kernels, response_call(): pl.pallas_call(response_kernel, out_shape=jax.ShapeDtypeStruct((responses...  7.47 us
    ppermute x9, waiting for transfers between devices, body(): got[step] = lax.ppermute(value, 'ctx' if kind == 'ctx' else 'prompt', route)  4.7 us
    pallas_call x1, Pallas kernels, prefix_call(): pl.pallas_call(prefix_kernel, out_shape=jax.ShapeDtypeStruct((rows.shape[...  2.02 us
    squeeze x1, local copies, waits for them, and re-layouts, pick(): return lax.dynamic_index_in_dim(sent, index ^ k, 0, keepdims=False)  1.37 us
    dynamic_slice x1, local copies, waits for them, and re-layouts, pick(): return lax.dynamic_slice_in_dim(sent, (index ^ k) & -2, 2, 0)  1.03 us
    slice x1, local copies, waits for them, and re-layouts, body(): prefix_kv = rows[:, feat - 2 * HEAD:]  0.84 us
  transfers between devices with their start and end apart: 10, of which 4 were waited for; matrix products, arithmetic and copies ran while one was open for 8% of the time, Pallas kernels for 7%

profile of v8, /device:TPU:0, one launch (start us, length us, event | category | flops | bytes accessed | tf_op | source)
XLA Modules:
  0.0 30.3 jit_solution(16078470294081518424)
XLA Ops:
  0.7 1.0 %dynamic-slice_bitcast_fusion = bf16[2,128,768]{2,1,0:T(8,128)(2,1)S(1)} fusion(bf16[1,1,8,128,768]{4,3,2,1,0:T(8,128)(2,1)} %param.5, s32[]{:T(128)S(6)} %select_n.34), kind=kLoop, calls=%fused_computation | loop fusion | bytes 786436 | tf_op jit(solution)/shard_map/dynamic_slice | solution.py:249
  1.7 4.0 %collective-permute-start.3 = (bf16[2,128,768]{2,1,0:T(8,128)(2,1)S(1)}, bf16[2,128,768]{2,1,0:T(8,128)(2,1)S(1)}, u32[]{:S(2)}, u32[]{:S(2)}) collective-permute-start(bf16[2,128,768]{2,1,0:T(8,128)(2,1)S(1)} %dynamic-slice_bitcast_fusion), channel_id=1, source_target_pairs={{0,24},{4,28},{8,16},{12,20},{16,8},{20,12},{24,0},{28,4},{1,25},{... | collective-permute-start | bytes 1179656 | tf_op jit(solution)/shard_map/ppermute | solution.py:270
  5.6 0.8 %slice.3 = bf16[128,256]{1,0:T(8,128)(2,1)S(1)} slice(bf16[128,768]{1,0:T(8,128)(2,1)} %bitcast.23), slice={[0:128], [512:768]} | slice | bytes 131072 | tf_op jit(solution)/shard_map/slice | solution.py:259
  6.5 1.6 %collective-permute-start = (bf16[128,256]{1,0:T(8,128)(2,1)S(1)}, bf16[128,256]{1,0:T(8,128)(2,1)S(1)}, u32[]{:S(2)}, u32[]{:S(2)}) collective-permute-start(bf16[128,256]{1,0:T(8,128)(2,1)S(1)} %slice.3), channel_id=1, source_target_pairs={{0,1},{1,2},{2,3},{3,0},{4,5},{5,6},{6,7},{7,4},{8,9},{9,10},{10,1... | collective-permute-start | bytes 196616 | tf_op jit(solution)/shard_map/ppermute | solution.py:270
  8.1 2.6 %collective-permute-start.1 = (bf16[128,256]{1,0:T(8,128)(2,1)S(1)}, bf16[128,256]{1,0:T(8,128)(2,1)S(1)}, u32[]{:S(2)}, u32[]{:S(2)}) collective-permute-start(bf16[128,256]{1,0:T(8,128)(2,1)S(1)} %slice.3), channel_id=1, source_target_pairs={{0,2},{1,3},{2,0},{3,1},{4,6},{5,7},{6,4},{7,5},{8,10},{9,11},{10,... | collective-permute-start | bytes 196616 | tf_op jit(solution)/shard_map/ppermute | solution.py:270
  10.7 1.4 %dynamic-slice_bitcast_fusion.3 = (bf16[128,768]{1,0:T(8,128)(2,1)S(1)}, bf16[128,768]{1,0:T(8,128)(2,1)S(1)}, bf16[128,768]{1,0:T(8,128)(2,1)S(1)}, bf16[128,768]{1,0:T(8,128)(2,1)S(1)}, bf16[128,768]{1,0:T(8,128)(2,1)S(1)}) fusion(bf16[1,1,8,128,768]{4,3,2,1,0:T(8,128)(2,1)} %param.5, s32[]{:T(128)S(6)} %select_n.39, s32[]{:T(128)S(6)} %select_n.37, ...), kind=kLoop, calls=%fused_computation.4 | loop fusion | bytes 1966100 | tf_op jit(solution)/shard_map/jit(dynamic_index_in_dim)/squeeze | solution.py:250
  12.0 0.6 %collective-permute-start.5 = (bf16[128,768]{1,0:T(8,128)(2,1)S(1)}, bf16[128,768]{1,0:T(8,128)(2,1)S(1)}, u32[]{:S(2)}, u32[]{:S(2)}) collective-permute-start(bf16[128,768]{1,0:T(8,128)(2,1)S(1)} %get-tuple-element.18), channel_id=1, source_target_pairs={{0,8},{4,12},{8,0},{12,4},{16,24},{20,28},{24,16},{28,20},{1,9},{5... | collective-permute-start | bytes 589832 | tf_op jit(solution)/shard_map/ppermute | solution.py:270
  12.6 0.5 %collective-permute-start.7 = (bf16[128,768]{1,0:T(8,128)(2,1)S(1)}, bf16[128,768]{1,0:T(8,128)(2,1)S(1)}, u32[]{:S(2)}, u32[]{:S(2)}) collective-permute-start(bf16[128,768]{1,0:T(8,128)(2,1)S(1)} %get-tuple-element.20), channel_id=1, source_target_pairs={{0,16},{4,20},{8,24},{12,28},{16,0},{20,4},{24,8},{28,12},{1,17},{... | collective-permute-start | bytes 589832 | tf_op jit(solution)/shard_map/ppermute | solution.py:270
  13.1 0.2 copy.6.order_ref
  13.4 0.0 collective-permute-done
  13.4 0.1 collective-permute-start.6
  13.5 1.2 %collective-permute-done.1 = bf16[128,256]{1,0:T(8,128)(2,1)S(1)} collective-permute-done((bf16[128,256]{1,0:T(8,128)(2,1)S(1)}, bf16[128,256]{1,0:T(8,128)(2,1)S(1)}, u32[]{:S(2)}, u32[]{:S(2)}) %collective-permute-start.1) | collective-permute-done | bytes 65568 | tf_op jit(solution)/shard_map/ppermute | solution.py:270
  14.7 1.2 %collective-permute-start.2 = (bf16[128,256]{1,0:T(8,128)(2,1)S(1)}, bf16[128,256]{1,0:T(8,128)(2,1)S(1)}, u32[]{:S(2)}, u32[]{:S(2)}) collective-permute-start(bf16[128,256]{1,0:T(8,128)(2,1)S(1)} %slice.3), channel_id=1, source_target_pairs={{0,3},{1,0},{2,1},{3,2},{4,7},{5,4},{6,5},{7,6},{8,11},{9,8},{10,9... | collective-permute-start | bytes 196616 | tf_op jit(solution)/shard_map/ppermute | solution.py:270
  15.9 1.3 %collective-permute-start.8 = (bf16[128,768]{1,0:T(8,128)(2,1)S(1)}, bf16[128,768]{1,0:T(8,128)(2,1)S(1)}, u32[]{:S(2)}, u32[]{:S(2)}) collective-permute-start(bf16[128,768]{1,0:T(8,128)(2,1)S(1)} %get-tuple-element.15), channel_id=1, source_target_pairs={{0,20},{4,16},{8,28},{12,24},{16,4},{20,0},{24,12},{28,8},{1,21},{... | collective-permute-start | bytes 589832 | tf_op jit(solution)/shard_map/ppermute | solution.py:270
  17.3 1.8 %collective-permute-done.2 = bf16[128,256]{1,0:T(8,128)(2,1)S(1)} collective-permute-done((bf16[128,256]{1,0:T(8,128)(2,1)S(1)}, bf16[128,256]{1,0:T(8,128)(2,1)S(1)}, u32[]{:S(2)}, u32[]{:S(2)}) %collective-permute-start.2) | collective-permute-done | bytes 65568 | tf_op jit(solution)/shard_map/ppermute | solution.py:270
  19.1 1.3 %collective-permute-done.5.refs_1_ = bf16[128,768]{1,0:T(8,128)(2,1)S(1)} collective-permute-done((bf16[128,768]{1,0:T(8,128)(2,1)S(1)}, bf16[128,768]{1,0:T(8,128)(2,1)S(1)}, u32[]{:S(2)}, u32[]{:S(2)}) %collective-permute-start.5) | collective-permute-done | bytes 196640 | tf_op jit(solution)/shard_map/ppermute | solution.py:270
  20.4 0.0 copy-start
  20.4 0.0 copy-start.2
  20.4 2.0 %prefix_attention.1 = bf16[128,512]{1,0:T(8,128)(2,1)} custom-call(s32[4]{0:T(128)S(1)} %fusion.starts_ref, bf16[128,768]{1,0:T(8,128)(2,1)S(1)} %bitcast.24, bf16[512,256]{1,0:T(8,128)(2,1)S(1)} %pad_maximum_fusion.kv_ref.prefix_ref), custom_call_target="tpu_custom_call" | custom-call | flops 1000000000 | bytes 1000000 | tf_op jit(solution)/shard_map/prefix_attention/pallas_call | solution.py:147
  22.4 0.0 collective-permute-done.7.refs_3_
  22.4 0.0 collective-permute-done.6.refs_2_
  22.5 0.4 %collective-permute-done.8.refs_4_ = bf16[128,768]{1,0:T(8,128)(2,1)S(1)} collective-permute-done((bf16[128,768]{1,0:T(8,128)(2,1)S(1)}, bf16[128,768]{1,0:T(8,128)(2,1)S(1)}, u32[]{:S(2)}, u32[]{:S(2)}) %collective-permute-start.8) | collective-permute-done | bytes 196640 | tf_op jit(solution)/shard_map/ppermute | solution.py:270
  22.8 0.0 collective-permute-done.4.refs_0_
  22.9 7.5 %response_attention.1 = bf16[2,512,512]{2,1,0:T(8,128)(2,1)} custom-call(s32[2]{0:T(128)S(1)} %bitcast.25, s32[1024,1]{1,0:T(8,128)S(1)} %copy.6.order_ref, bf16[8,128,768]{2,1,0:T(8,128)(2,1)S(1)} %bitcast.22, bf16[512,256]{1,0:T(8,128)(2,1)S(1)} %pad_maximum_fusion.kv_ref.prefix_ref, bf16[128,768]{1,0:T(8,128)(2,1)S(1)} %collective-permute-done.4.refs_0_, ...), custom_call_target="tpu_custom_call" | custom-call | flops 5000000000 | bytes 4000000 | tf_op jit(solution)/shard_map/response_attention/pallas_call | solution.py:204
  (13 shorter events, 0.1 us)
Async XLA Ops:
  0.6 12.5 %copy-start.3 = (s32[1,1,1024]{2,1,0:T(1,128)S(1)}, s32[1,1,1024]{2,1,0:T(1,128)}, u32[]{:S(2)}) copy-start(s32[1,1,1024]{2,1,0:T(1,128)} %param.6) | copy-start | bytes 12292
  1.7 14.3 %collective-permute-start.3 = (bf16[2,128,768]{2,1,0:T(8,128)(2,1)S(1)}, bf16[2,128,768]{2,1,0:T(8,128)(2,1)S(1)}, u32[]{:S(2)}, u32[]{:S(2)}) collective-permute-start(bf16[2,128,768]{2,1,0:T(8,128)(2,1)S(1)} %dynamic-slice_bitcast_fusion), channel_id=1, source_target_pairs={{0,24},{4,28},{8,16},{12,20},{16,8},{20,12},{24,0},{28,4},{1,25},{... | collective-permute-start | bytes 1179656 | tf_op jit(solution)/shard_map/ppermute | solution.py:270
  6.5 6.9 %collective-permute-start = (bf16[128,256]{1,0:T(8,128)(2,1)S(1)}, bf16[128,256]{1,0:T(8,128)(2,1)S(1)}, u32[]{:S(2)}, u32[]{:S(2)}) collective-permute-start(bf16[128,256]{1,0:T(8,128)(2,1)S(1)} %slice.3), channel_id=1, source_target_pairs={{0,1},{1,2},{2,3},{3,0},{4,5},{5,6},{6,7},{7,4},{8,9},{9,10},{10,1... | collective-permute-start | bytes 196616 | tf_op jit(solution)/shard_map/ppermute | solution.py:270
  8.1 6.6 %collective-permute-start.1 = (bf16[128,256]{1,0:T(8,128)(2,1)S(1)}, bf16[128,256]{1,0:T(8,128)(2,1)S(1)}, u32[]{:S(2)}, u32[]{:S(2)}) collective-permute-start(bf16[128,256]{1,0:T(8,128)(2,1)S(1)} %slice.3), channel_id=1, source_target_pairs={{0,2},{1,3},{2,0},{3,1},{4,6},{5,7},{6,4},{7,5},{8,10},{9,11},{10,... | collective-permute-start | bytes 196616 | tf_op jit(solution)/shard_map/ppermute | solution.py:270
  10.7 9.7 %copy-start.1 = (bf16[1,128,768]{2,1,0:T(8,128)(2,1)S(1)}, bf16[1,128,768]{2,1,0:T(8,128)(2,1)}, u32[]{:S(2)}) copy-start(bf16[1,128,768]{2,1,0:T(8,128)(2,1)} %param.4) | copy-start | bytes 589828
  12.0 8.3 %collective-permute-start.5 = (bf16[128,768]{1,0:T(8,128)(2,1)S(1)}, bf16[128,768]{1,0:T(8,128)(2,1)S(1)}, u32[]{:S(2)}, u32[]{:S(2)}) collective-permute-start(bf16[128,768]{1,0:T(8,128)(2,1)S(1)} %get-tuple-element.18), channel_id=1, source_target_pairs={{0,8},{4,12},{8,0},{12,4},{16,24},{20,28},{24,16},{28,20},{1,9},{5... | collective-permute-start | bytes 589832 | tf_op jit(solution)/shard_map/ppermute | solution.py:270
  12.6 9.8 %collective-permute-start.7 = (bf16[128,768]{1,0:T(8,128)(2,1)S(1)}, bf16[128,768]{1,0:T(8,128)(2,1)S(1)}, u32[]{:S(2)}, u32[]{:S(2)}) collective-permute-start(bf16[128,768]{1,0:T(8,128)(2,1)S(1)} %get-tuple-element.20), channel_id=1, source_target_pairs={{0,16},{4,20},{8,24},{12,28},{16,0},{20,4},{24,8},{28,12},{1,17},{... | collective-permute-start | bytes 589832 | tf_op jit(solution)/shard_map/ppermute | solution.py:270
  13.4 9.1 %collective-permute-start.6 = (bf16[128,768]{1,0:T(8,128)(2,1)S(1)}, bf16[128,768]{1,0:T(8,128)(2,1)S(1)}, u32[]{:S(2)}, u32[]{:S(2)}) collective-permute-start(bf16[128,768]{1,0:T(8,128)(2,1)S(1)} %get-tuple-element.14), channel_id=1, source_target_pairs={{0,12},{4,8},{8,4},{12,0},{16,28},{20,24},{24,20},{28,16},{1,13},{... | collective-permute-start | bytes 589832 | tf_op jit(solution)/shard_map/ppermute | solution.py:270
  14.7 4.4 %collective-permute-start.2 = (bf16[128,256]{1,0:T(8,128)(2,1)S(1)}, bf16[128,256]{1,0:T(8,128)(2,1)S(1)}, u32[]{:S(2)}, u32[]{:S(2)}) collective-permute-start(bf16[128,256]{1,0:T(8,128)(2,1)S(1)} %slice.3), channel_id=1, source_target_pairs={{0,3},{1,0},{2,1},{3,2},{4,7},{5,4},{6,5},{7,6},{8,11},{9,8},{10,9... | collective-permute-start | bytes 196616 | tf_op jit(solution)/shard_map/ppermute | solution.py:270
  15.9 6.9 %collective-permute-start.8 = (bf16[128,768]{1,0:T(8,128)(2,1)S(1)}, bf16[128,768]{1,0:T(8,128)(2,1)S(1)}, u32[]{:S(2)}, u32[]{:S(2)}) collective-permute-start(bf16[128,768]{1,0:T(8,128)(2,1)S(1)} %get-tuple-element.15), channel_id=1, source_target_pairs={{0,20},{4,16},{8,28},{12,24},{16,4},{20,0},{24,12},{28,8},{1,21},{... | collective-permute-start | bytes 589832 | tf_op jit(solution)/shard_map/ppermute | solution.py:270
  19.1 3.8 %collective-permute-start.4 = (bf16[128,768]{1,0:T(8,128)(2,1)S(1)}, bf16[128,768]{1,0:T(8,128)(2,1)S(1)}, u32[]{:S(2)}, u32[]{:S(2)}) collective-permute-start(bf16[128,768]{1,0:T(8,128)(2,1)S(1)} %get-tuple-element.13), channel_id=1, source_target_pairs={{0,4},{4,0},{8,12},{12,8},{16,20},{20,16},{24,28},{28,24},{1,5},{5... | collective-permute-start | bytes 589832 | tf_op jit(solution)/shard_map/ppermute | solution.py:270
  20.4 2.5 %collective-permute-start.9 = (bf16[128,768]{1,0:T(8,128)(2,1)S(1)}, bf16[128,768]{1,0:T(8,128)(2,1)S(1)}, u32[]{:S(2)}, u32[]{:S(2)}) collective-permute-start(bf16[128,768]{1,0:T(8,128)(2,1)S(1)} %get-tuple-element.21), channel_id=1, source_target_pairs={{0,4},{4,0},{8,12},{12,8},{16,20},{20,16},{24,28},{28,24},{1,5},{5... | collective-permute-start | bytes 589832 | tf_op jit(solution)/shard_map/ppermute | solution.py:277
  20.4 2.5 %copy-start = (bf16[1,1,8,128,768]{4,3,2,1,0:T(8,128)(2,1)S(1)}, bf16[1,1,8,128,768]{4,3,2,1,0:T(8,128)(2,1)}, u32[]{:S(2)}) copy-start(bf16[1,1,8,128,768]{4,3,2,1,0:T(8,128)(2,1)} %param.5) | copy-start | bytes 4718596
  20.4 2.4 %copy-start.2 = (s32[1,2]{1,0:T(1,128)S(1)}, s32[1,2]{1,0:T(1,128)}, u32[]{:S(2)}) copy-start(s32[1,2]{1,0:T(1,128)} %param.7) | copy-start | bytes 28
